TPU v7x, 32 devices: a whole 2x2x4 slice. The times are simulated.
32 devices in a mesh: section: 2 (over core), tp: 16 (over z, y, x).
Axes of the slice: x: 2, y: 2, z: 4, core: 2. Of those that a mesh axis runs over, the one named last changes fastest.
Arguments:
- text_states: bfloat16 [128, 8192], P(None, 'tp'), may hold values from -7 to 7
- vision_states: bfloat16 [256, 1280], P('section'), may hold values from -6 to 6
- visible_tiles: int32 [128], replicated, may hold values from 0 to 4
- vision_norm_gain: float32 [1280], replicated, may hold values from 0.1 to 1.9
- vision_fc1: bfloat16 [1280, 5120], P(None, 'tp'), may hold values from -0.15625 to 0.15625
- vision_fc2: bfloat16 [5120, 1280], P('tp'), may hold values from -0.078125 to 0.078125
- vision_gate: float32 [1], replicated, may hold values from -2.5 to 2.5
- projector: bfloat16 [1280, 8192], P(None, 'tp'), may hold values from -0.15625 to 0.15625
- cross_norm: bfloat16 [2, 8192], P('section', 'tp'), may hold values from 0.099609375 to 1.8984375
- cross_q: bfloat16 [2, 8192, 4096], P('section', None, 'tp'), may hold values from -0.0625 to 0.0625
- cross_kv: bfloat16 [2, 8192, 1024], P('section', 'tp'), may hold values from -0.0625 to 0.0625
- cross_qk_gain: float32 [2, 2, 128], P('section'), may hold values from 0.1 to 1.9
- cross_o: bfloat16 [2, 4096, 8192], P('section', None, 'tp'), may hold values from -0.5 to 0.5
- cross_gate: float32 [2], P('section'), may hold values from 0.5 to 1.5
- self_norm: bfloat16 [2, 8192], P('section', 'tp'), may hold values from 0.5 to 1.5
- self_q: bfloat16 [2, 8192, 4096], P('section', None, 'tp'), may hold values from -1 to 1
- self_kv: bfloat16 [2, 8192, 1024], P('section', 'tp'), may hold values from -1 to 1
- self_o: bfloat16 [2, 4096, 8192], P('section', None, 'tp'), may hold values from -0.09375 to 0.09375
Outputs:
- section_outputs: bfloat16 [2, 128, 8192], P('section', None, 'tp')
All inputs are finite; a program needn't handle non-finite values.
Results may differ from a plain program's by a relative error of at most 0.018.
Values may be sent and summed in bfloat16 or wider, within the bound.
No kernel may reach another device: no remote copies, remote signals or barrier semaphores. Data moves between devices by JAX's collectives and lax.ppermute only.
A program may use at most 128 MiB of HBM per device.

v0:
```python
import jax
import jax.numpy as jnp
from jax import lax
from jax.sharding import PartitionSpec as P

HD = 128
HEADS = 32
KV = 4
TILES = 4
ROWS = 64
BLOCKS = 2


epsilon = 1e-05


def from_behind(block, axis, distance):
    devices = range(lax.axis_size(axis))
    route = [(i - distance, i) for i in devices if i - distance in devices]
    return lax.ppermute(block, axis, route)


def rms_norm(values, gain_row):
    mean_square = jnp.mean(values * values, axis=-1, keepdims=True)
    return values * lax.rsqrt(mean_square + epsilon) * gain_row.astype(jnp.float32)


def rotate(values, positions):
    half_dim = values.shape[-1] // 2
    exponents = jnp.arange(half_dim, dtype=jnp.float32) * (2.0 / values.shape[-1])
    inverse = jnp.float32(500000.0) ** (-exponents)
    angles = positions.astype(jnp.float32)[:, None] * inverse[None, :]
    cosine = jnp.cos(angles)[:, None, :]
    sine = jnp.sin(angles)[:, None, :]
    lower = values[..., :half_dim]
    upper = values[..., half_dim:]
    return jnp.concatenate([lower * cosine - upper * sine, upper * cosine + lower * sine], axis=-1)


def softmax_rows(scores):
    top_score = jnp.max(scores, axis=-1, keepdims=True)
    raised = jnp.exp(scores - top_score)
    return raised / jnp.sum(raised, axis=-1, keepdims=True)


def head_columns(kv_rows, kv_head):
    key_part = lax.dynamic_slice_in_dim(kv_rows, kv_head * HD, HD, 1)
    value_part = lax.dynamic_slice_in_dim(kv_rows, (KV + kv_head) * HD, HD, 1)
    return (key_part, value_part)


def attend_one(queries, key_rows, value_rows, allowed):
    scores = jnp.einsum(
        "rhd,jd->hrj", queries, key_rows, preferred_element_type=jnp.float32
    ) * HD ** (-0.5)
    scores = jnp.where(allowed[None], scores, -1e30)
    weights = softmax_rows(scores).astype(jnp.bfloat16)
    mixed_heads = jnp.einsum("hrj,jd->rhd", weights, value_rows, preferred_element_type=jnp.float32)
    return mixed_heads.astype(jnp.bfloat16).reshape(queries.shape[0], -1)


def out_fold(weight, segment):
    return jnp.dot(segment, weight, preferred_element_type=jnp.float32)


def body(
    text_states,
    vision_states,
    visible_tiles,
    vision_norm_gain,
    vision_fc1,
    vision_fc2,
    vision_gate,
    projector,
    cross_norm,
    cross_q,
    cross_kv,
    cross_qk_gain,
    cross_o,
    cross_gate,
    self_norm,
    self_q,
    self_kv,
    self_o,
):
    section_idx = lax.axis_index("section")
    section_total = lax.axis_size("section")
    tp_index = lax.axis_index("tp")
    local_width = text_states.shape[1]
    heads_local = cross_q.shape[2] // HD
    kv_group = HEADS // KV
    kv_head = tp_index * heads_local // kv_group
    vis_f32 = vision_states.astype(jnp.float32)
    centre = jnp.mean(vis_f32, axis=-1, keepdims=True)
    spread = jnp.mean((vis_f32 - centre) ** 2, axis=-1, keepdims=True)
    normed_vis = ((vis_f32 - centre) * lax.rsqrt(spread + epsilon) * vision_norm_gain).astype(
        jnp.bfloat16
    )
    vis_hidden = jax.nn.gelu(
        jnp.dot(normed_vis, vision_fc1, preferred_element_type=jnp.float32), approximate=False
    ).astype(jnp.bfloat16)
    vis_branch = lax.psum(jnp.dot(vis_hidden, vision_fc2, preferred_element_type=jnp.float32), "tp")
    vis_out = (vis_f32 + jnp.tanh(vision_gate[0]) * vis_branch).astype(jnp.bfloat16)
    every_row = lax.all_gather(vis_out, "section", axis=0, tiled=True)
    image_feats = jnp.dot(every_row, projector, preferred_element_type=jnp.float32).astype(
        jnp.bfloat16
    )
    image_count = image_feats.shape[0]
    kv_term = jnp.dot(image_feats, cross_kv[0], preferred_element_type=jnp.float32)
    key_gain = cross_qk_gain[0, 1]
    kv_image = lax.psum(kv_term, "tp")
    key_part, value_part = head_columns(kv_image, kv_head)
    key_img = rms_norm(key_part, key_gain).astype(jnp.bfloat16)
    val_img = value_part.astype(jnp.bfloat16)
    tile_of = jnp.arange(image_count, dtype=jnp.int32) // (image_count // TILES)
    seq_len = text_states.shape[0]
    positions_all = jnp.arange(seq_len, dtype=jnp.int32)
    gate_cross = jnp.tanh(cross_gate[0])
    key_cache = jnp.zeros((seq_len, HD), jnp.bfloat16)
    val_cache = jnp.zeros((seq_len, HD), jnp.bfloat16)
    outputs = jnp.zeros((seq_len, local_width), jnp.bfloat16)
    incoming = jnp.zeros((ROWS, local_width), jnp.bfloat16)
    step_count = BLOCKS + section_total - 1
    for step_no in range(step_count):
        block_idx = step_no - section_idx
        is_live = (block_idx >= 0) & (block_idx < BLOCKS)
        row_start = jnp.clip(block_idx, 0, BLOCKS - 1) * ROWS
        entry_block = min(step_no, BLOCKS - 1)
        first_rows = text_states[entry_block * ROWS : (entry_block + 1) * ROWS]
        current = jnp.where(section_idx == 0, first_rows, incoming)
        positions = row_start + jnp.arange(ROWS, dtype=jnp.int32)
        whole_rows, gain_row = (
            lax.all_gather(current, "tp", axis=1, tiled=True),
            lax.all_gather(cross_norm, "tp", axis=1, tiled=True),
        )
        normed = rms_norm(whole_rows.astype(jnp.float32), gain_row[0]).astype(jnp.bfloat16)
        queries = jnp.dot(normed, cross_q[0], preferred_element_type=jnp.float32).reshape(
            ROWS, heads_local, HD
        )
        queries = rms_norm(queries, cross_qk_gain[0, 0]).astype(jnp.bfloat16)
        row_tiles = lax.dynamic_slice_in_dim(visible_tiles, row_start, ROWS)
        allowed = tile_of[None, :] < row_tiles[:, None]
        mixed_heads = attend_one(queries, key_img, val_img, allowed)
        cross_branch = out_fold(cross_o[0], lax.all_gather(mixed_heads, "tp", axis=1, tiled=True))
        cross_branch = cross_branch * (row_tiles > 0).astype(jnp.float32)[:, None]
        current = (current.astype(jnp.float32) + gate_cross * cross_branch).astype(jnp.bfloat16)
        whole_rows, gain_row = (
            lax.all_gather(current, "tp", axis=1, tiled=True),
            lax.all_gather(self_norm, "tp", axis=1, tiled=True),
        )
        normed = rms_norm(whole_rows.astype(jnp.float32), gain_row[0]).astype(jnp.bfloat16)
        queries = rotate(
            jnp.dot(normed, self_q[0], preferred_element_type=jnp.float32).reshape(
                ROWS, heads_local, HD
            ),
            positions,
        ).astype(jnp.bfloat16)
        own_cols = lax.dynamic_slice_in_dim(normed, tp_index * local_width, local_width, 1)
        kv_text = lax.psum(
            jnp.dot(own_cols, self_kv[0], preferred_element_type=jnp.float32).astype(jnp.bfloat16),
            "tp",
        ).astype(jnp.float32)
        key_part, value_part = head_columns(kv_text, kv_head)
        new_keys = rotate(key_part[:, None, :], positions)[:, 0].astype(jnp.bfloat16)
        new_vals = value_part.astype(jnp.bfloat16)
        key_cache = jnp.where(
            is_live, lax.dynamic_update_slice_in_dim(key_cache, new_keys, row_start, 0), key_cache
        )
        val_cache = jnp.where(
            is_live, lax.dynamic_update_slice_in_dim(val_cache, new_vals, row_start, 0), val_cache
        )
        causal = positions_all[None, :] <= positions[:, None]
        mixed_heads = attend_one(queries, key_cache, val_cache, causal)
        self_branch = out_fold(self_o[0], lax.all_gather(mixed_heads, "tp", axis=1, tiled=True))
        current = (current.astype(jnp.float32) + self_branch).astype(jnp.bfloat16)
        outputs = jnp.where(
            is_live, lax.dynamic_update_slice_in_dim(outputs, current, row_start, 0), outputs
        )
        if step_no + 1 < step_count:
            incoming = from_behind(current, "section", 1)
    return outputs[None]


def solution(mesh):
    in_specs = (
        P(None, "tp"),
        P("section", None),
        P(),
        P(),
        P(None, "tp"),
        P("tp", None),
        P(),
        P(None, "tp"),
        P("section", "tp"),
        P("section", None, "tp"),
        P("section", "tp", None),
        P("section", None, None),
        P("section", None, "tp"),
        P("section"),
        P("section", "tp"),
        P("section", None, "tp"),
        P("section", "tp", None),
        P("section", None, "tp"),
    )
    out_specs = P("section", None, "tp")
    return jax.shard_map(body, mesh=mesh, in_specs=in_specs, out_specs=out_specs, check_vma=False)
```

profile of v0, /device:TPU:0, one launch (start us, length us, event | category | flops | bytes accessed | tf_op | source)
XLA Modules:
  0.0 1194.9 jit_solution(13913556536368324045)
XLA Ops:
  9.0 3.8 fusion.146
  13.6 111.8 %all-reduce.6.cloned.1.call-done = f32[128,1280]{1,0:T(8,128)} async-done(((f32[128,1280]{1,0:T(8,128)}), f32[128,1280]{1,0:T(8,128)}) %all-reduce.6.cloned.1.call-update) | async-done | bytes 655376 | tf_op jit(solution)/shard_map/psum | solution.py:102
  131.6 6.4 copy.37
  138.0 38.8 %all_gather.51 = bf16[1,8192]{1,0:T(2,128)(2,1)S(1)} all-gather(bf16[1,512]{1,0:T(2,128)(2,1)S(1)} %copy-done.36), channel_id=1, replica_groups=mesh['section'=2,'tp'=16] {'tp'}, dimensions={1}, use_global_device_ids=true | all-gather | bytes 17408 | tf_op jit(solution)/shard_map/all_gather | solution.py:134
  178.9 62.7 %all-reduce.8.cloned.1.call-done = f32[256,1024]{1,0:T(8,128)} async-done(((f32[256,1024]{1,0:T(8,128)}), f32[256,1024]{1,0:T(8,128)}) %all-reduce.8.cloned.1.call-update) | async-done | bytes 1048592 | tf_op jit(solution)/shard_map/psum | solution.py:111
  243.7 53.1 %all-gather.7.cloned.1.call-done = bf16[64,8192]{1,0:T(8,128)(2,1)} async-done(((bf16[64,512]{1,0:T(8,128)(2,1)}), bf16[64,8192]{1,0:T(8,128)(2,1)}) %all-gather.7.cloned.1.call-update) | async-done | bytes 1048592 | tf_op jit(solution)/shard_map/all_gather | solution.py:133
  298.3 4.0 multiply_reduce_fusion.3
  304.0 42.2 %all_gather.52 = bf16[64,4096]{1,0:T(8,128)(2,1)S(1)} all-gather(bf16[64,256]{1,0:T(8,128)(2,1)S(1)} %bitcast.273), channel_id=1, replica_groups=mesh['section'=2,'tp'=16] {'tp'}, dimensions={1}, use_global_device_ids=true | all-gather | bytes 557056 | tf_op jit(solution)/shard_map/all_gather | solution.py:144
  346.3 3.7 fusion.76
  350.0 35.7 %all_gather.54 = bf16[1,8192]{1,0:T(2,128)(2,1)S(1)} all-gather(bf16[1,512]{1,0:T(2,128)(2,1)S(1)} %copy-done.37), channel_id=1, replica_groups=mesh['section'=2,'tp'=16] {'tp'}, dimensions={1}, use_global_device_ids=true | all-gather | bytes 17408 | tf_op jit(solution)/shard_map/all_gather | solution.py:149
  385.8 6.4 copy.38
  394.4 5.0 all-gather.9.cloned.1.call-done
  403.5 3.6 fusion.110
  407.2 100.8 %all-reduce.10.cloned.1.call-done = bf16[64,1024]{1,0:T(8,128)(2,1)} async-done(((bf16[64,1024]{1,0:T(8,128)(2,1)}), bf16[64,1024]{1,0:T(8,128)(2,1)}) %all-reduce.10.cloned.1.call-update) | async-done | bytes 131088 | tf_op jit(solution)/shard_map/psum | solution.py:159
  510.2 41.8 %all_gather.55 = bf16[64,4096]{1,0:T(8,128)(2,1)S(1)} all-gather(bf16[64,256]{1,0:T(8,128)(2,1)S(1)} %bitcast.274), channel_id=1, replica_groups=mesh['section'=2,'tp'=16] {'tp'}, dimensions={1}, use_global_device_ids=true | all-gather | bytes 557056 | tf_op jit(solution)/shard_map/all_gather | solution.py:174
  558.0 49.6 %all-gather.11.cloned.1.call-done = bf16[64,8192]{1,0:T(8,128)(2,1)} async-done(((bf16[64,512]{1,0:T(8,128)(2,1)}), bf16[64,8192]{1,0:T(8,128)(2,1)}) %all-gather.11.cloned.1.call-update) | async-done | bytes 1048592 | tf_op jit(solution)/shard_map/all_gather | solution.py:133
  609.2 4.0 multiply_reduce_fusion.2
  614.9 42.2 %all_gather.57 = bf16[64,4096]{1,0:T(8,128)(2,1)S(1)} all-gather(bf16[64,256]{1,0:T(8,128)(2,1)S(1)} %bitcast.275), channel_id=1, replica_groups=mesh['section'=2,'tp'=16] {'tp'}, dimensions={1}, use_global_device_ids=true | all-gather | bytes 557056 | tf_op jit(solution)/shard_map/all_gather | solution.py:144
  657.2 3.6 add_convert_fusion.3
  661.7 48.4 %all-gather.13.cloned.1.call-done = bf16[64,8192]{1,0:T(8,128)(2,1)} async-done(((bf16[64,512]{1,0:T(8,128)(2,1)}), bf16[64,8192]{1,0:T(8,128)(2,1)}) %all-gather.13.cloned.1.call-update) | async-done | bytes 1048592 | tf_op jit(solution)/shard_map/all_gather | solution.py:148
  714.2 4.2 fusion.108
  719.5 102.4 %all-reduce.12.cloned.1.call-done = bf16[64,1024]{1,0:T(8,128)(2,1)} async-done(((bf16[64,1024]{1,0:T(8,128)(2,1)}), bf16[64,1024]{1,0:T(8,128)(2,1)}) %all-reduce.12.cloned.1.call-update) | async-done | bytes 131088 | tf_op jit(solution)/shard_map/psum | solution.py:159
  829.5 41.8 %all_gather.59 = bf16[64,4096]{1,0:T(8,128)(2,1)S(1)} all-gather(bf16[64,256]{1,0:T(8,128)(2,1)S(1)} %bitcast.276), channel_id=1, replica_groups=mesh['section'=2,'tp'=16] {'tp'}, dimensions={1}, use_global_device_ids=true | all-gather | bytes 557056 | tf_op jit(solution)/shard_map/all_gather | solution.py:174
  877.3 49.6 %all-gather.15.cloned.1.call-done = bf16[64,8192]{1,0:T(8,128)(2,1)} async-done(((bf16[64,512]{1,0:T(8,128)(2,1)}), bf16[64,8192]{1,0:T(8,128)(2,1)}) %all-gather.15.cloned.1.call-update) | async-done | bytes 1048592 | tf_op jit(solution)/shard_map/all_gather | solution.py:133
  928.5 4.0 multiply_reduce_fusion.1
  934.2 42.2 %all_gather.61 = bf16[64,4096]{1,0:T(8,128)(2,1)S(1)} all-gather(bf16[64,256]{1,0:T(8,128)(2,1)S(1)} %bitcast.277), channel_id=1, replica_groups=mesh['section'=2,'tp'=16] {'tp'}, dimensions={1}, use_global_device_ids=true | all-gather | bytes 557056 | tf_op jit(solution)/shard_map/all_gather | solution.py:144
  976.5 3.6 add_convert_fusion.1
  980.9 48.6 %all-gather.17.cloned.1.call-done = bf16[64,8192]{1,0:T(8,128)(2,1)} async-done(((bf16[64,512]{1,0:T(8,128)(2,1)}), bf16[64,8192]{1,0:T(8,128)(2,1)}) %all-gather.17.cloned.1.call-update) | async-done | bytes 1048592 | tf_op jit(solution)/shard_map/all_gather | solution.py:148
  1033.6 3.6 fusion.106
  1037.3 103.3 %all-reduce.14.cloned.1.call-done = bf16[64,1024]{1,0:T(8,128)(2,1)} async-done(((bf16[64,1024]{1,0:T(8,128)(2,1)}), bf16[64,1024]{1,0:T(8,128)(2,1)}) %all-reduce.14.cloned.1.call-update) | async-done | bytes 131088 | tf_op jit(solution)/shard_map/psum | solution.py:159
  1142.9 41.8 %all_gather.63 = bf16[64,4096]{1,0:T(8,128)(2,1)S(1)} all-gather(bf16[64,256]{1,0:T(8,128)(2,1)S(1)} %bitcast.278), channel_id=1, replica_groups=mesh['section'=2,'tp'=16] {'tp'}, dimensions={1}, use_global_device_ids=true | all-gather | bytes 557056 | tf_op jit(solution)/shard_map/all_gather | solution.py:174
  1184.7 3.7 fusion.182
  (209 shorter events, 62.7 us)
Async XLA Ops:
  6.5 122.3 %copy-start = (bf16[1280,512]{1,0:T(8,128)(2,1)S(1)}, bf16[1280,512]{1,0:T(8,128)(2,1)}, u32[]{:S(2)}) copy-start(bf16[1280,512]{1,0:T(8,128)(2,1)} %param.25) | copy-start | bytes 3932164
  6.5 118.9 %all-reduce.6.cloned.1.call-start = ((), (), s32[]{:S(2)}) async-start(), calls=%async_computation | async-start | bytes 1310720 | tf_op jit(solution)/shard_map/psum | solution.py:102
  9.0 116.4 %copy-start.2 = (bf16[128,1280]{1,0:T(8,128)(2,1)S(1)}, bf16[128,1280]{1,0:T(8,128)(2,1)}, u32[]{:S(2)}) copy-start(bf16[128,1280]{1,0:T(8,128)(2,1)} %param.19) | copy-start | bytes 983044
  12.7 116.1 %copy-start.6 = (bf16[1,512,1024]{2,1,0:T(8,128)(2,1)S(1)}, bf16[1,512,1024]{2,1,0:T(8,128)(2,1)}, u32[]{:S(2)}) copy-start(bf16[1,512,1024]{2,1,0:T(8,128)(2,1)} %param.28) | copy-start | bytes 3145732
  12.8 228.8 %all-reduce.8.cloned.1.call-start = ((), (), s32[]{:S(2)}) async-start(), calls=%async_computation.1 | async-start | bytes 2097152 | tf_op jit(solution)/shard_map/psum | solution.py:111
  130.8 166.0 %all-gather.7.cloned.1.call-start = ((), (), s32[]{:S(2)}) async-start(), calls=%async_computation.2 | async-start | bytes 1114112 | tf_op jit(solution)/shard_map/all_gather | solution.py:133
  131.5 267.8 %all-gather.9.cloned.1.call-start = ((), (), s32[]{:S(2)}) async-start(), calls=%async_computation.3 | async-start | bytes 1114112 | tf_op jit(solution)/shard_map/all_gather | solution.py:148
  176.9 125.5 %copy-start.15 = (f32[1,8192]{1,0:T(1,128)}, f32[1,8192]{1,0:T(1,128)S(1)}, u32[]{:S(2)}) copy-start(f32[1,8192]{1,0:T(1,128)S(1)} %mul.726) | copy-start | bytes 98308
  178.2 124.2 %copy-start.29 = (f32[128]{0:T(128)}, f32[128]{0:T(128)S(1)}, u32[]{:S(2)}) copy-start(f32[128]{0:T(128)S(1)} %get-tuple-element.34) | copy-start | bytes 1540
  243.6 58.7 %copy-start.3 = (bf16[256,128,1]{1,0,2:T(8,128)(2,1)}, bf16[256,128,1]{1,0,2:T(8,128)(2,1)S(1)}, u32[]{:S(2)}) copy-start(bf16[256,128,1]{1,0,2:T(8,128)(2,1)S(1)} %fusion.179) | copy-start | bytes 196612
  350.0 158.0 %all-reduce.10.cloned.1.call-start = ((), (), s32[]{:S(2)}) async-start(), calls=%async_computation.4 | async-start | bytes 262144 | tf_op jit(solution)/shard_map/psum | solution.py:159
  392.2 116.7 %copy-start.27 = (f32[64]{0:T(128)}, f32[64]{0:T(128)S(1)}, u32[]{:S(2)}) copy-start(f32[64]{0:T(128)S(1)} %negate_power_fusion) | copy-start | bytes 772
  403.4 204.1 %all-gather.11.cloned.1.call-start = ((), (), s32[]{:S(2)}) async-start(), calls=%async_computation.5 | async-start | bytes 1114112 | tf_op jit(solution)/shard_map/all_gather | solution.py:133
  407.1 144.9 %copy-start.9 = (bf16[64,512]{1,0:T(8,128)(2,1)S(1)}, bf16[64,512]{1,0:T(8,128)(2,1)}, u32[]{:S(2)}) copy-start(bf16[64,512]{1,0:T(8,128)(2,1)} %fusion.76) | copy-start | bytes 196612
  552.0 57.1 %copy-start.16 = (f32[1,8192]{1,0:T(1,128)S(1)}, f32[1,8192]{1,0:T(1,128)}, u32[]{:S(2)}) copy-start(f32[1,8192]{1,0:T(1,128)} %copy-done.15) | copy-start | bytes 98308
  555.1 2.2 collective-permute-start
  558.0 152.2 %all-gather.13.cloned.1.call-start = ((), (), s32[]{:S(2)}) async-start(), calls=%async_computation.6 | async-start | bytes 1114112 | tf_op jit(solution)/shard_map/all_gather | solution.py:148
  609.2 48.0 %copy-start.13 = (bf16[64,512]{1,0:T(8,128)(2,1)S(1)}, bf16[64,512]{1,0:T(8,128)(2,1)}, u32[]{:S(2)}) copy-start(bf16[64,512]{1,0:T(8,128)(2,1)} %broadcast_select_fusion.1) | copy-start | bytes 196612
  609.2 48.0 %copy-start.39 = (f32[64]{0:T(128)S(1)}, f32[64]{0:T(128)}, u32[]{:S(2)}) copy-start(f32[64]{0:T(128)} %get-tuple-element.42) | copy-start | bytes 772
  660.8 161.1 %all-reduce.12.cloned.1.call-start = ((), (), s32[]{:S(2)}) async-start(), calls=%async_computation.7 | async-start | bytes 262144 | tf_op jit(solution)/shard_map/psum | solution.py:159
  718.4 152.9 %copy-start.11 = (bf16[64,512]{1,0:T(8,128)(2,1)S(1)}, bf16[64,512]{1,0:T(8,128)(2,1)}, u32[]{:S(2)}) copy-start(bf16[64,512]{1,0:T(8,128)(2,1)} %add_convert_fusion.3) | copy-start | bytes 196612
  718.5 208.4 %all-gather.15.cloned.1.call-start = ((), (), s32[]{:S(2)}) async-start(), calls=%async_computation.8 | async-start | bytes 1114112 | tf_op jit(solution)/shard_map/all_gather | solution.py:133
  871.4 57.1 %copy-start.17 = (f32[1,8192]{1,0:T(1,128)S(1)}, f32[1,8192]{1,0:T(1,128)}, u32[]{:S(2)}) copy-start(f32[1,8192]{1,0:T(1,128)} %copy-done.15) | copy-start | bytes 98308
  874.4 2.2 collective-permute-start.1
  877.3 152.2 %all-gather.17.cloned.1.call-start = ((), (), s32[]{:S(2)}) async-start(), calls=%async_computation.9 | async-start | bytes 1114112 | tf_op jit(solution)/shard_map/all_gather | solution.py:148
  928.5 48.0 %copy-start.12 = (bf16[64,512]{1,0:T(8,128)(2,1)S(1)}, bf16[64,512]{1,0:T(8,128)(2,1)}, u32[]{:S(2)}) copy-start(bf16[64,512]{1,0:T(8,128)(2,1)} %broadcast_select_fusion) | copy-start | bytes 196612
  980.1 160.5 %all-reduce.14.cloned.1.call-start = ((), (), s32[]{:S(2)}) async-start(), calls=%async_computation.10 | async-start | bytes 262144 | tf_op jit(solution)/shard_map/psum | solution.py:159
  1033.5 108.1 %copy-start.23 = (bf16[128,128]{1,0:T(8,128)(2,1)S(1)}, bf16[128,128]{1,0:T(8,128)(2,1)}, u32[]{:S(2)}) copy-start(bf16[128,128]{1,0:T(8,128)(2,1)} %fusion.244) | copy-start | bytes 98308
  1033.5 108.1 %copy-start.28 = (f32[64]{0:T(128)S(1)}, f32[64]{0:T(128)}, u32[]{:S(2)}) copy-start(f32[64]{0:T(128)} %copy-done.27) | copy-start | bytes 772
  1033.5 108.1 %copy-start.34 = (f32[64]{0:T(128)S(1)}, f32[64]{0:T(128)}, u32[]{:S(2)}) copy-start(f32[64]{0:T(128)} %copy-done.33) | copy-start | bytes 772
  1033.5 108.3 %copy-start.8 = (bf16[128,128]{1,0:T(8,128)(2,1)S(1)}, bf16[128,128]{1,0:T(8,128)(2,1)}, u32[]{:S(2)}) copy-start(bf16[128,128]{1,0:T(8,128)(2,1)} %fusion.250) | copy-start | bytes 98308
  1037.2 147.5 %copy-start.10 = (bf16[64,512]{1,0:T(8,128)(2,1)S(1)}, bf16[64,512]{1,0:T(8,128)(2,1)}, u32[]{:S(2)}) copy-start(bf16[64,512]{1,0:T(8,128)(2,1)} %add_convert_fusion.1) | copy-start | bytes 196612
  (24 other events, 384.0 us)
Sparse Core Ops, SparseCore 0:
  12.9 112.4 all-reduce.5
  130.9 110.6 all-reduce.7
  244.3 52.3 all-gather.6
  350.1 49.2 all-gather.8
  404.6 103.2 all-reduce.9
  558.1 49.4 all-gather.10
  661.0 49.1 all-gather.12
  718.6 103.2 all-reduce.11
  877.4 49.4 all-gather.14
  980.2 49.1 all-gather.16
  1037.3 103.2 all-reduce.13
where the time goes:
time: 1200 us; the launch traced here: 1190 us
  waiting for transfers between devices  737 us (61%)
  blocking collectives  329 us (27%)
  matrix products  61.9 us (5%)
  other arithmetic  34.3 us (3%)
  between operations  15.6 us (1%)
  local copies, waits for them, and re-layouts  13.8 us (1%)
    psum x3, waiting for transfers between devices, body(): lax.psum(jnp.dot(own_cols, self_kv[0], preferred_element_type=jnp.float32...  306 us
    all_gather x6, waiting for transfers between devices, body(): lax.all_gather(current, 'tp', axis=1, tiled=True)  254 us
    all_gather x6, blocking collectives, body(): lax.all_gather(mixed_heads, 'tp', axis=1, tiled=True)  252 us
    psum x1, waiting for transfers between devices, body(): lax.psum(jnp.dot(vis_hidden, vision_fc2, preferred_element_type=jnp.float...  112 us
    psum x1, waiting for transfers between devices, body(): kv_image = lax.psum(kv_term, 'tp')  62.7 us
    all_gather x1, blocking collectives, body(): lax.all_gather(cross_norm, 'tp', axis=1, tiled=True)  38.8 us
    all_gather x1, blocking collectives, body(): lax.all_gather(self_norm, 'tp', axis=1, tiled=True)  35.7 us
  transfers between devices with their start and end apart: 13, of which 13 were waited for; matrix products, arithmetic and copies ran while one was open for 2% of the time, Pallas kernels for 0%

commit v1 on v0

--- a/solution.py
+++ b/solution.py
@@ -1,6 +1,10 @@
+import functools
+
 import jax
 import jax.numpy as jnp
 from jax import lax
+from jax.experimental import pallas as pl
+from jax.experimental.pallas import tpu as pltpu
 from jax.sharding import PartitionSpec as P
 
 HD = 128
@@ -63,7 +67,7 @@
     return jnp.dot(segment, weight, preferred_element_type=jnp.float32)
 
 
-def body(
+def blocked_body(
     text_states,
     vision_states,
     visible_tiles,
@@ -181,7 +185,491 @@
     return outputs[None]
 
 
+VMEM_LIMIT = 48 * 1024 * 1024
+GROUP = 4
+
+
+def params():
+    return pltpu.CompilerParams(vmem_limit_bytes=VMEM_LIMIT)
+
+
+def in_vmem():
+    return pl.BlockSpec(memory_space=pltpu.VMEM)
+
+
+def in_place():
+    return pl.BlockSpec(memory_space=pl.ANY)
+
+
+def swap_cores(block):
+    return lax.ppermute(block, "section", [(0, 1), (1, 0)])
+
+
+def send_xor(block, masks):
+    chips = lax.axis_size("tp")
+    route = [
+        (core * chips + chip, core * chips + (chip ^ masks[core]))
+        for core in range(2)
+        for chip in range(chips)
+    ]
+    return lax.ppermute(block, ("section", "tp"), route)
+
+
+def gather_chips(block):
+    first = jnp.stack(
+        [block] + [send_xor(block, (GROUP * k, k)) for k in range(1, GROUP)]
+    )
+    return [first] + [send_xor(first, (k, GROUP * k)) for k in range(1, GROUP)]
+
+
+def piece_chip(core, chip, outer, inner):
+    return jnp.where(core == 0, chip ^ (GROUP * inner) ^ outer, chip ^ inner ^ (GROUP * outer))
+
+
+def fetch_rows(section, own_ref, other_ref, wbuf, sems, rows, columns):
+    core = lax.axis_index("section")
+    chip = lax.axis_index("tp")
+    for outer in range(GROUP):
+        for inner in range(GROUP):
+            at = outer * GROUP + inner
+            source = piece_chip(core, chip, outer, inner)
+            start = pl.multiple_of(source * (2 * rows) + core * rows, rows)
+            target = wbuf.at[at, :, pl.ds(0, columns)]
+
+            @pl.when(core == section)
+            def _():
+                pltpu.make_async_copy(own_ref.at[pl.ds(start, rows), :], target, sems.at[at]).start()
+
+            @pl.when(core != section)
+            def _():
+                pltpu.make_async_copy(other_ref.at[pl.ds(start, rows), :], target, sems.at[at]).start()
+
+
+def wait_rows(own_ref, wbuf, sems, at, rows, columns):
+    pltpu.make_async_copy(
+        own_ref.at[pl.ds(0, rows), :], wbuf.at[at, :, pl.ds(0, columns)], sems.at[at]
+    ).wait()
+
+
+def query_kernel(section, gain_at, with_kv, *refs):
+    x_refs = refs[:GROUP]
+    gain_ref, own_ref, other_ref = refs[GROUP : GROUP + 3]
+    rest = refs[GROUP + 3 :]
+    if with_kv:
+        kv_refs, rest = rest[:GROUP], rest[GROUP:]
+    keep_ref, send_ref, wbuf, sems = rest[:4]
+    core = lax.axis_index("section")
+    rows = x_refs[0].shape[2]
+    queries = own_ref.shape[1]
+    fetch_rows(section, own_ref, other_ref, wbuf, sems, rows, queries)
+    if with_kv:
+        kv_sems = rest[4]
+        width = kv_refs[0].shape[3]
+        for outer in range(GROUP):
+            for inner in range(GROUP):
+                at = outer * GROUP + inner
+                target = wbuf.at[at, :, pl.ds(queries, width)]
+
+                @pl.when(core == 0)
+                def _():
+                    pltpu.make_async_copy(
+                        kv_refs[outer].at[inner, section], target, kv_sems.at[at]
+                    ).start()
+
+                @pl.when(core != 0)
+                def _():
+                    pltpu.make_async_copy(
+                        kv_refs[inner].at[outer, section], target, kv_sems.at[at]
+                    ).start()
+
+    total = jnp.zeros((x_refs[0].shape[1], wbuf.shape[2]), jnp.float32)
+    squares = jnp.zeros(x_refs[0].shape[1:], jnp.float32)
+    for outer in range(GROUP):
+        for inner in range(GROUP):
+            at = outer * GROUP + inner
+            piece = x_refs[outer][inner].astype(jnp.float32)
+            squares = squares + piece * piece
+            gain_row = gain_ref[at, gain_at : gain_at + 1, :].astype(jnp.float32)
+            scaled = (piece * gain_row).astype(jnp.bfloat16)
+            wait_rows(own_ref, wbuf, sems, at, rows, queries)
+            if with_kv:
+                pltpu.make_async_copy(
+                    kv_refs[0].at[0, section], wbuf.at[at, :, pl.ds(queries, width)], kv_sems.at[at]
+                ).wait()
+            total = total + jnp.dot(scaled, wbuf[at], preferred_element_type=jnp.float32)
+    half = queries // 2
+    lower, upper = total[:, :half], total[:, half:queries]
+    keep_ref[:, :half] = jnp.where(core == 0, lower, upper)
+    send_ref[:, :half] = jnp.where(core == 0, upper, lower)
+    square_sum = jnp.broadcast_to(
+        jnp.sum(squares, axis=1, keepdims=True), (squares.shape[0], 128)
+    )
+    for ref in (keep_ref, send_ref):
+        ref[:, half : half + 128] = square_sum
+        if with_kv:
+            ref[:, half + 128 :] = total[:, queries:]
+
+
+def query_part(section, gain_at, pieces, gains, own, other, kv_pieces=None):
+    rows = pieces[0].shape[1]
+    depth = pieces[0].shape[2]
+    queries = own.shape[1]
+    kv_width = kv_pieces[0].shape[3] if kv_pieces is not None else 0
+    out = jax.ShapeDtypeStruct((rows, queries // 2 + 128 + kv_width), jnp.float32)
+    scratch = [
+        pltpu.VMEM((GROUP * GROUP, depth, queries + kv_width), jnp.bfloat16),
+        pltpu.SemaphoreType.DMA((GROUP * GROUP,)),
+    ]
+    operands = list(pieces) + [gains, own, other]
+    specs = [in_vmem()] * (GROUP + 1) + [in_place()] * 2
+    if kv_pieces is not None:
+        scratch.append(pltpu.SemaphoreType.DMA((GROUP * GROUP,)))
+        operands += list(kv_pieces)
+        specs += [in_place()] * GROUP
+    return pl.pallas_call(
+        functools.partial(query_kernel, section, gain_at, kv_pieces is not None),
+        out_shape=(out, out),
+        in_specs=specs,
+        out_specs=(in_vmem(), in_vmem()),
+        scratch_shapes=scratch,
+        compiler_params=params(),
+    )(*operands)
+
+
+def out_kernel(section, *refs):
+    x_refs = refs[:GROUP]
+    own_ref, other_ref, keep_ref, send_ref, wbuf, sems = refs[GROUP:]
+    core = lax.axis_index("section")
+    rows = x_refs[0].shape[2]
+    columns = own_ref.shape[1]
+    fetch_rows(section, own_ref, other_ref, wbuf, sems, rows, columns)
+    total = jnp.zeros((x_refs[0].shape[1], columns), jnp.float32)
+    for outer in range(GROUP):
+        for inner in range(GROUP):
+            at = outer * GROUP + inner
+            wait_rows(own_ref, wbuf, sems, at, rows, columns)
+            total = total + jnp.dot(
+                x_refs[outer][inner], wbuf[at], preferred_element_type=jnp.float32
+            )
+    half = columns // 2
+    lower, upper = total[:, :half], total[:, half:]
+    keep_ref[...] = jnp.where(core == 0, lower, upper)
+    send_ref[...] = jnp.where(core == 0, upper, lower)
+
+
+def out_part(section, pieces, own, other):
+    rows, depth = pieces[0].shape[1:]
+    columns = own.shape[1]
+    out = jax.ShapeDtypeStruct((rows, columns // 2), jnp.float32)
+    return pl.pallas_call(
+        functools.partial(out_kernel, section),
+        out_shape=(out, out),
+        in_specs=[in_vmem()] * GROUP + [in_place()] * 2,
+        out_specs=(in_vmem(), in_vmem()),
+        scratch_shapes=[
+            pltpu.VMEM((GROUP * GROUP, depth, columns), jnp.bfloat16),
+            pltpu.SemaphoreType.DMA((GROUP * GROUP,)),
+        ],
+        compiler_params=params(),
+    )(*pieces, own, other)
+
+
+def dot_rows(left, right):
+    return lax.dot_general(
+        left, right, (((1,), (1,)), ((), ())), preferred_element_type=jnp.float32
+    )
+
+
+def row_scale(keep_ref, come_ref, width):
+    square_sum = keep_ref[:, HD : HD + 128] + come_ref[:, HD : HD + 128]
+    return lax.rsqrt(square_sum / width + epsilon)
+
+
+def cross_kernel(width, tile_rows, keep_ref, come_ref, near_ref, far_ref, tiles_ref, gain_ref, out_ref):
+    core = lax.axis_index("section")
+    queries = (keep_ref[:, :HD] + come_ref[:, :HD]) * row_scale(keep_ref, come_ref, width)
+    queries = rms_norm(queries, gain_ref[0:1, :]).astype(jnp.bfloat16)
+    row_tiles = tiles_ref[...]
+    count = near_ref.shape[0]
+    key_at = lax.broadcasted_iota(jnp.int32, (queries.shape[0], count), 1)
+    scores = []
+    for ref, base in ((near_ref, core * count), (far_ref, (1 - core) * count)):
+        part = dot_rows(queries, ref[:, :HD]) * HD ** (-0.5)
+        scores.append(jnp.where(key_at + base < row_tiles * tile_rows, part, -1e30))
+    top = jnp.maximum(
+        jnp.max(scores[0], axis=1, keepdims=True), jnp.max(scores[1], axis=1, keepdims=True)
+    )
+    raised = [jnp.exp(part - top) for part in scores]
+    bottom = jnp.sum(raised[0], axis=1, keepdims=True) + jnp.sum(raised[1], axis=1, keepdims=True)
+    mixed = jnp.zeros(queries.shape, jnp.float32)
+    for part, ref in zip(raised, (near_ref, far_ref)):
+        weights = (part / bottom).astype(jnp.bfloat16)
+        mixed = mixed + jnp.dot(weights, ref[:, HD:], preferred_element_type=jnp.float32)
+    out_ref[...] = mixed.astype(jnp.bfloat16)
+
+
+def cross_mix(width, tile_rows, keep, come, near, far, tiles, gain):
+    return pl.pallas_call(
+        functools.partial(cross_kernel, width, tile_rows),
+        out_shape=jax.ShapeDtypeStruct((keep.shape[0], HD), jnp.bfloat16),
+        in_specs=[in_vmem()] * 6,
+        out_specs=in_vmem(),
+        compiler_params=params(),
+    )(keep, come, near, far, tiles, gain)
+
+
+def turn(values, cosine, sine):
+    half = HD // 2
+    swapped = jnp.concatenate([values[:, half:], values[:, :half]], axis=1)
+    return values * cosine + swapped * sine
+
+
+def self_kernel(width, keep_ref, come_ref, cosine_ref, sine_ref, out_ref):
+    scale = row_scale(keep_ref, come_ref, width)
+    cosine, sine = cosine_ref[...], sine_ref[...]
+    queries = (keep_ref[:, :HD] + come_ref[:, :HD]) * scale
+    queries = turn(queries, cosine, sine).astype(jnp.bfloat16)
+    at = HD + 128
+    keys = (keep_ref[:, at : at + HD] + come_ref[:, at : at + HD]) * scale
+    keys = turn(keys, cosine, sine).astype(jnp.bfloat16)
+    values = (keep_ref[:, at + HD :] + come_ref[:, at + HD :]) * scale
+    values = values.astype(jnp.bfloat16)
+    scores = dot_rows(queries, keys) * HD ** (-0.5)
+    row_at = lax.broadcasted_iota(jnp.int32, scores.shape, 0)
+    key_at = lax.broadcasted_iota(jnp.int32, scores.shape, 1)
+    scores = jnp.where(key_at <= row_at, scores, -1e30)
+    weights = softmax_rows(scores).astype(jnp.bfloat16)
+    mixed = jnp.dot(weights, values, preferred_element_type=jnp.float32)
+    out_ref[...] = mixed.astype(jnp.bfloat16)
+
+
+def self_mix(width, keep, come, cosine, sine):
+    return pl.pallas_call(
+        functools.partial(self_kernel, width),
+        out_shape=jax.ShapeDtypeStruct((keep.shape[0], HD), jnp.bfloat16),
+        in_specs=[in_vmem()] * 4,
+        out_specs=in_vmem(),
+        compiler_params=params(),
+    )(keep, come, cosine, sine)
+
+
+def image_kernel(p0, p1, p2, p3, projector_ref, own_ref, other_ref, out_ref, rows_ref, kv_ref):
+    core = lax.axis_index("section")
+    chip = lax.axis_index("tp")
+    low, high = chip % GROUP, chip // GROUP
+    member = jnp.where(core == 0, low, high)
+    count = p0.shape[0]
+    for k, ref in enumerate((p0, p1, p2, p3)):
+        rows_ref[pl.ds(pl.multiple_of((member ^ k) * count, count), count), :] = ref[...]
+    feats = jnp.dot(
+        rows_ref[...], projector_ref[...], preferred_element_type=jnp.float32
+    ).astype(jnp.bfloat16)
+    for section in range(2):
+        weight = jnp.where(core == section, own_ref[...], other_ref[...])
+        kv_ref[...] = jnp.dot(feats, weight, preferred_element_type=jnp.float32)
+        for k in range(GROUP):
+            head = high ^ k
+            for part in range(2):
+                start = pl.multiple_of((part * KV + head) * HD, HD)
+                out_ref[section, k, :, part * HD : (part + 1) * HD] = kv_ref[
+                    :, pl.ds(start, HD)
+                ].astype(jnp.bfloat16)
+
+
+def image_part(pieces, projector, own, other):
+    rows = GROUP * pieces[0].shape[0]
+    return pl.pallas_call(
+        image_kernel,
+        out_shape=jax.ShapeDtypeStruct((2, GROUP, rows, 2 * HD), jnp.bfloat16),
+        in_specs=[in_vmem()] * 7,
+        out_specs=in_vmem(),
+        scratch_shapes=[
+            pltpu.VMEM((rows, projector.shape[0]), jnp.bfloat16),
+            pltpu.VMEM((rows, own.shape[1]), jnp.float32),
+        ],
+        compiler_params=params(),
+    )(*pieces, projector, own, other)
+
+
+def heads_kernel(own_ref, other_ref, out_ref):
+    core = lax.axis_index("section")
+    high = lax.axis_index("tp") // GROUP
+    rows = own_ref.shape[0] // 2
+    mine = pl.ds(pl.multiple_of(core * rows, rows), rows)
+    for k in range(GROUP):
+        head = high ^ k
+        for part in range(2):
+            start = pl.multiple_of((part * KV + head) * HD, HD)
+            near = own_ref[mine, pl.ds(start, HD)]
+            far = other_ref[mine, pl.ds(start, HD)]
+            columns = slice(part * HD, (part + 1) * HD)
+            out_ref[k, 0, :, columns] = jnp.where(core == 0, near, far)
+            out_ref[k, 1, :, columns] = jnp.where(core == 0, far, near)
+
+
+def self_kv_pieces(own, other):
+    rows = own.shape[0] // 2
+    blocks = pl.pallas_call(
+        heads_kernel,
+        out_shape=jax.ShapeDtypeStruct((GROUP, 2, rows, 2 * HD), jnp.bfloat16),
+        in_specs=[in_vmem()] * 2,
+        out_specs=in_vmem(),
+        compiler_params=params(),
+    )(own, other)
+    first = jnp.stack(
+        [blocks[0]] + [send_xor(blocks[k], (GROUP * k, GROUP * k)) for k in range(1, GROUP)]
+    )
+    return [first] + [send_xor(first, (k, k)) for k in range(1, GROUP)]
+
+
+def paired_body(
+    text_states,
+    vision_states,
+    visible_tiles,
+    vision_norm_gain,
+    vision_fc1,
+    vision_fc2,
+    vision_gate,
+    projector,
+    cross_norm,
+    cross_q,
+    cross_kv,
+    cross_qk_gain,
+    cross_o,
+    cross_gate,
+    self_norm,
+    self_q,
+    self_kv,
+    self_o,
+):
+    core = lax.axis_index("section")
+    chip = lax.axis_index("tp")
+    seq_len, local_width = text_states.shape
+    half = local_width // 2
+    full_width = local_width * lax.axis_size("tp")
+    low, high = chip % GROUP, chip // GROUP
+    member = jnp.where(core == 0, low, high)
+
+    vis_f32 = vision_states.astype(jnp.float32)
+    centre = jnp.mean(vis_f32, axis=-1, keepdims=True)
+    spread = jnp.mean((vis_f32 - centre) ** 2, axis=-1, keepdims=True)
+    normed_vis = ((vis_f32 - centre) * lax.rsqrt(spread + epsilon) * vision_norm_gain).astype(
+        jnp.bfloat16
+    )
+    vis_hidden = jax.nn.gelu(
+        jnp.dot(normed_vis, vision_fc1, preferred_element_type=jnp.float32), approximate=False
+    ).astype(jnp.bfloat16)
+    branch = jnp.dot(vis_hidden, vision_fc2, preferred_element_type=jnp.float32)
+    rows = branch.shape[0] // GROUP
+    branch = branch.astype(jnp.bfloat16).reshape(GROUP, rows, -1)
+
+    def chunk(array, k):
+        return lax.dynamic_index_in_dim(array, member ^ k, 0, keepdims=False)
+
+    def total(parts):
+        return sum((part.astype(jnp.float32) for part in parts[1:]), parts[0].astype(jnp.float32))
+
+    near = total(
+        [chunk(branch, 0)] + [send_xor(chunk(branch, k), (k, GROUP * k)) for k in range(1, GROUP)]
+    ).astype(jnp.bfloat16)
+    branch_rows = total([near] + [send_xor(near, (GROUP * k, k)) for k in range(1, GROUP)])
+    vis_rows = chunk(vis_f32.reshape(GROUP, rows, -1), 0)
+    vis_out = (vis_rows + jnp.tanh(vision_gate[0]) * branch_rows).astype(jnp.bfloat16)
+    vis_pieces = [vis_out] + [send_xor(vis_out, (k, GROUP * k)) for k in range(1, GROUP)]
+
+    small = jnp.concatenate(
+        [
+            cross_norm.astype(jnp.float32),
+            self_norm.astype(jnp.float32),
+            jnp.pad(cross_qk_gain.reshape(1, -1), ((0, 0), (0, local_width - 2 * HD))),
+            jnp.broadcast_to(cross_gate[None], (1, local_width)),
+        ]
+    )
+    small = lax.all_gather(small, "section", axis=0)
+    own_cross_kv, own_cross_q, own_cross_o = cross_kv[0], cross_q[0], cross_o[0]
+    own_self_kv, own_self_q, own_self_o = self_kv[0], self_q[0], self_o[0]
+    far_cross_kv = swap_cores(own_cross_kv)
+    far_cross_q = swap_cores(own_cross_q)
+    far_self_kv = swap_cores(own_self_kv)
+    far_cross_o = swap_cores(own_cross_o)
+    far_self_q = swap_cores(own_self_q)
+    far_self_o = swap_cores(own_self_o)
+
+    gain_rows = small[:, :2].astype(jnp.bfloat16).reshape(4, local_width)
+    entry = jnp.concatenate(
+        [text_states, gain_rows, jnp.zeros((12, local_width), jnp.bfloat16)], axis=0
+    )
+    entry = lax.dynamic_slice_in_dim(entry, core * half, half, 1)
+    hidden = entry[:seq_len]
+    pieces = gather_chips(entry)
+    gains = jnp.concatenate([piece[:, seq_len:] for piece in pieces], axis=0)
+    pieces = [piece[:, :seq_len] for piece in pieces]
+
+    image_parts = image_part(vis_pieces, projector, own_cross_kv, far_cross_kv)
+    image_kv = []
+    for section in range(2):
+        near = total(
+            [image_parts[section, 0]]
+            + [
+                send_xor(image_parts[section, k], (GROUP * k, GROUP * k))
+                for k in range(1, GROUP)
+            ]
+        ).astype(jnp.bfloat16)
+        kv_rows = total([near] + [send_xor(near, (k, k)) for k in range(1, GROUP)])
+        key_gain = small[section, 2, HD : 2 * HD]
+        near = jnp.concatenate(
+            [rms_norm(kv_rows[:, :HD], key_gain), kv_rows[:, HD:]], axis=1
+        ).astype(jnp.bfloat16)
+        image_kv.append((near, swap_cores(near)))
+
+    kv_pieces = self_kv_pieces(own_self_kv, far_self_kv)
+
+    tile_rows = 2 * vision_states.shape[0] // TILES
+    tiles = jnp.broadcast_to(visible_tiles[:, None], (seq_len, 128))
+    row_live = (visible_tiles > 0).astype(jnp.float32)[:, None]
+    exponents = jnp.arange(HD // 2, dtype=jnp.float32) * (2.0 / HD)
+    inverse = jnp.float32(500000.0) ** (-exponents)
+    angles = jnp.arange(seq_len, dtype=jnp.float32)[:, None] * inverse[None, :]
+    cosine = jnp.tile(jnp.cos(angles), (1, 2))
+    sine = jnp.concatenate([-jnp.sin(angles), jnp.sin(angles)], axis=1)
+
+    results = []
+    for section in range(2):
+        if section > 0:
+            pieces = gather_chips(hidden)
+        keep, send = query_part(
+            section, 2 * section, pieces, gains, own_cross_q, far_cross_q
+        )
+        near, far = image_kv[section]
+        mixed = cross_mix(
+            full_width, tile_rows, keep, swap_cores(send), near, far, tiles, small[section, 2:3, :HD]
+        )
+        keep, send = out_part(section, gather_chips(mixed), own_cross_o, far_cross_o)
+        branch = (keep + swap_cores(send)) * row_live
+        gate = jnp.tanh(small[section, 3, 0])
+        hidden = (hidden.astype(jnp.float32) + gate * branch).astype(jnp.bfloat16)
+
+        pieces = gather_chips(hidden)
+        keep, send = query_part(
+            section, 2 * section + 1, pieces, gains, own_self_q, far_self_q, kv_pieces
+        )
+        mixed = self_mix(full_width, keep, swap_cores(send), cosine, sine)
+        keep, send = out_part(section, gather_chips(mixed), own_self_o, far_self_o)
+        branch = keep + swap_cores(send)
+        hidden = (hidden.astype(jnp.float32) + branch).astype(jnp.bfloat16)
+        results.append(hidden)
+    come = swap_cores(jnp.where(core == 0, results[1], results[0]))
+    return jnp.where(
+        core == 0,
+        jnp.concatenate([results[0], come], axis=1),
+        jnp.concatenate([come, results[1]], axis=1),
+    )[None]
+
+
 def solution(mesh):
+    chips = mesh.shape["tp"]
+    paired = mesh.shape["section"] == 2 and chips == GROUP * GROUP and HEADS == 2 * chips
+    body = paired_body if paired else blocked_body
     in_specs = (
         P(None, "tp"),
         P("section", None),

time: 1200 us -> 329 us (0.27)
  waiting for transfers between devices: 737 us -> 176 us
  blocking collectives: 329 us -> 1.8 us
  starting transfers between devices: 3.19 us -> 96.8 us
  matrix products: 61.9 us -> 3.46 us
  Pallas kernels: 0 us -> 28.3 us
  other arithmetic: 34.3 us -> 10.5 us
  between operations: 15.6 us -> 3.25 us
    psum x5 -> x0, waiting for transfers between devices: 481 us -> none  [the longest x3 306 us: body(): lax.psum(jnp.dot(own_cols, self_kv[0], preferred_element_type=jnp.float32...]
    all_gather x9 -> x1, blocking collectives: 329 us -> 1.8 us  [paired_body(): small = lax.all_gather(small, 'section', axis=0)]
    all_gather x6 -> x0, waiting for transfers between devices: 254 us -> none  [body(): lax.all_gather(current, 'tp', axis=1, tiled=True)]
    ppermute x2 -> x92, waiting for transfers between devices: 1.76 us -> 176 us  [the longest x75 166 us: send_xor(): return lax.ppermute(block, ('section', 'tp'), route)]
    ppermute x2 -> x92, starting transfers between devices: 2.59 us -> 96.8 us  [the longest x75 92 us: send_xor(): return lax.ppermute(block, ('section', 'tp'), route)]
    dot_general x29 -> x1, matrix products: 60 us -> 3.46 us  [paired_body(): branch = jnp.dot(vis_hidden, vision_fc2, preferred_element_type=jnp.float32)]
    pallas_call x0 -> x14, Pallas kernels: none -> 28.3 us  [the longest x4 12.7 us: query_part(): pl.pallas_call(functools.partial(query_kernel, section, gain_at, kv_piece...]
    dot_general x2 -> x0, local copies, waits for them, and re-layouts: 12.8 us -> none  [the longest x1 6.43 us: body(): jnp.dot(normed, self_q[0], preferred_element_type=jnp.float32)]
  transfers between devices with their start and end apart: 13 -> 92, of which waited for: 13 -> 64; matrix products, arithmetic and copies ran while one was open for 2% -> 5% of each run, Pallas kernels for 0% -> 5%
where the time goes in v1:
time: 329 us; the launch traced here: 328 us
  waiting for transfers between devices  176 us (53%)
  starting transfers between devices  96.8 us (29%)
  Pallas kernels  28.3 us (9%)
  other arithmetic  10.5 us (3%)
  local copies, waits for them, and re-layouts  8.78 us (3%)
  matrix products  3.46 us (1%)
    ppermute x75, waiting for transfers between devices, send_xor(): return lax.ppermute(block, ('section', 'tp'), route)  166 us
    ppermute x75, starting transfers between devices, send_xor(): return lax.ppermute(block, ('section', 'tp'), route)  92 us
    pallas_call x4, Pallas kernels, query_part(): pl.pallas_call(functools.partial(query_kernel, section, gain_at, kv_piece...  12.7 us
    pallas_call x4, Pallas kernels, out_part(): pl.pallas_call(functools.partial(out_kernel, section), out_shape=(out, ou...  10.2 us
    ppermute x17, waiting for transfers between devices, swap_cores(): return lax.ppermute(block, 'section', [(0, 1), (1, 0)])  10 us
  transfers between devices with their start and end apart: 92, of which 64 were waited for; matrix products, arithmetic and copies ran while one was open for 5% of the time, Pallas kernels for 5%

profile of v1, /device:TPU:0, one launch (start us, length us, event | category | flops | bytes accessed | tf_op | source)
XLA Modules:
  0.0 328.3 jit_solution(2525609463595716027)
XLA Ops:
  3.1 3.5 %convolution_convert_fusion = bf16[128,1280]{1,0:T(8,128)(2,1)} fusion(bf16[320,1280]{1,0:T(8,128)(2,1)S(1)} %copy-done, bf16[1280,320]{0,1:T(8,128)(2,1)} %param.22, bf16[128,1280]{1,0:T(8,128)(2,1)} %param.19, f32[1280]{0:T(1024)} %param.21, f32[128]{0:T(128)S(1)} %add_rsqrt_fusion.2, f32[128]{0:T(128)S(1)} %broadcast_multiply_fusion), kind=kOutput, calls=%fused_computation | convolution fusion | flops 213360640 | bytes 2299904 | tf_op jit(solution)/shard_map/dot_general | solution.py:562
  8.2 3.9 %collective-permute-start.10 = (bf16[32,1280]{1,0:T(8,128)(2,1)}, bf16[32,1280]{1,0:T(8,128)(2,1)}, u32[]{:S(2)}, u32[]{:S(2)}) collective-permute-start(bf16[32,1280]{1,0:T(8,128)(2,1)} %get-tuple-element.52), channel_id=1, source_target_pairs={{0,3},{1,2},{2,1},{3,0},{4,7},{5,6},{6,5},{7,4},{8,11},{9,10},{10,... | collective-permute-start | bytes 245768 | tf_op jit(solution)/shard_map/ppermute | solution.py:215
  19.0 3.6 %collective-permute-start.13 = (bf16[32,1280]{1,0:T(8,128)(2,1)}, bf16[32,1280]{1,0:T(8,128)(2,1)}, u32[]{:S(2)}, u32[]{:S(2)}) collective-permute-start(bf16[32,1280]{1,0:T(8,128)(2,1)} %fusion.9), channel_id=1, source_target_pairs={{0,12},{1,13},{2,14},{3,15},{4,8},{5,9},{6,10},{7,11},{8,4},{9,5},... | collective-permute-start | bytes 245768 | tf_op jit(solution)/shard_map/ppermute | solution.py:215
  27.6 2.7 collective-permute-done.12
  33.4 3.2 collective-permute-done.2
  38.0 5.6 %collective-permute-done = bf16[144,256]{1,0:T(8,128)(2,1)S(1)} collective-permute-done((bf16[144,256]{1,0:T(8,128)(2,1)S(1)}, bf16[144,256]{1,0:T(8,128)(2,1)S(1)}, u32[]{:S(2)}, u32[]{:S(2)}) %collective-permute-start) | collective-permute-done | bytes 73760 | tf_op jit(solution)/shard_map/ppermute | solution.py:215
  56.9 2.4 collective-permute-done.65
  59.7 3.5 %collective-permute-done.64 = bf16[128,256]{1,0:T(8,128)(2,1)S(1)} collective-permute-done((bf16[128,256]{1,0:T(8,128)(2,1)S(1)}, bf16[128,256]{1,0:T(8,128)(2,1)S(1)}, u32[]{:S(2)}, u32[]{:S(2)}) %collective-permute-start.64) | collective-permute-done | bytes 65568 | tf_op jit(solution)/shard_map/ppermute | solution.py:215
  63.2 3.3 %collective-permute-start.18 = (bf16[128,256]{1,0:T(8,128)(2,1)S(1)}, bf16[128,256]{1,0:T(8,128)(2,1)S(1)}, u32[]{:S(2)}, u32[]{:S(2)}) collective-permute-start(bf16[128,256]{1,0:T(8,128)(2,1)S(1)} %get-tuple-element.50), channel_id=1, source_target_pairs={{0,4},{1,5},{2,6},{3,7},{4,0},{5,1},{6,2},{7,3},{8,12},{9,13},{10,... | collective-permute-start | bytes 196616 | tf_op jit(solution)/shard_map/ppermute | solution.py:215
  74.4 3.3 %collective-permute-done.5 = bf16[4,144,256]{2,1,0:T(8,128)(2,1)S(1)} collective-permute-done((bf16[4,144,256]{2,1,0:T(8,128)(2,1)S(1)}, bf16[4,144,256]{2,1,0:T(8,128)(2,1)S(1)}, u32[]{:S(2)}, u32[]{:S(2)}) %collective-permute-start.5) | collective-permute-done | bytes 294944 | tf_op jit(solution)/shard_map/ppermute | solution.py:215
  83.9 4.3 %shard_map.172 = (f32[128,256]{1,0:T(8,128)S(1)}, f32[128,256]{1,0:T(8,128)S(1)}) custom-call(bf16[4,128,256]{2,1,0:T(8,128)(2,1)S(1)} %slice.134.refs_0_, bf16[4,128,256]{2,1,0:T(8,128)(2,1)S(1)} %slice.135.refs_1_, bf16[4,128,256]{2,1,0:T(8,128)(2,1)S(1)} %slice.136.refs_2_, bf16[4,128,256]{2,1,0:T(8,128)(2,1)S(1)} %slice.137.refs_3_, ...), custom_call_target="tpu_custom_call" | custom-call | tf_op jit(solution)/shard_map/pallas_call | solution.py:329
  94.3 3.8 %collective-permute-done.27 = bf16[128,128]{1,0:T(8,128)(2,1)S(1)} collective-permute-done((bf16[128,128]{1,0:T(8,128)(2,1)S(1)}, bf16[128,128]{1,0:T(8,128)(2,1)S(1)}, u32[]{:S(2)}, u32[]{:S(2)}) %collective-permute-start.27) | collective-permute-done | bytes 32800 | tf_op jit(solution)/shard_map/ppermute | solution.py:215
  98.2 4.8 %collective-permute-done.26 = bf16[128,128]{1,0:T(8,128)(2,1)S(1)} collective-permute-done((bf16[128,128]{1,0:T(8,128)(2,1)S(1)}, bf16[128,128]{1,0:T(8,128)(2,1)S(1)}, u32[]{:S(2)}, u32[]{:S(2)}) %collective-permute-start.26) | collective-permute-done | bytes 32800 | tf_op jit(solution)/shard_map/ppermute | solution.py:215
  103.0 4.6 %collective-permute-done.25 = bf16[128,128]{1,0:T(8,128)(2,1)S(1)} collective-permute-done((bf16[128,128]{1,0:T(8,128)(2,1)S(1)}, bf16[128,128]{1,0:T(8,128)(2,1)S(1)}, u32[]{:S(2)}, u32[]{:S(2)}) %collective-permute-start.25) | collective-permute-done | bytes 32800 | tf_op jit(solution)/shard_map/ppermute | solution.py:215
  117.4 3.8 %shard_map.175 = (f32[128,256]{1,0:T(8,128)S(1)}, f32[128,256]{1,0:T(8,128)S(1)}) custom-call(bf16[4,128,128]{2,1,0:T(8,128)(2,1)S(1)} %pad_maximum_fusion.6.refs_0_, bf16[4,128,128]{2,1,0:T(8,128)(2,1)S(1)} %collective-permute-done.28.refs_1_, bf16[4,128,128]{2,1,0:T(8,128)(2,1)S(1)} %collective-permute-done.29.refs_2_, ...), custom_call_target="tpu_custom_call" | custom-call | tf_op jit(solution)/shard_map/pallas_call | solution.py:364
  123.5 2.4 collective-permute-start.41
  127.2 5.4 %collective-permute-done.43 = bf16[2,256,256]{2,1,0:T(8,128)(2,1)S(1)} collective-permute-done((bf16[2,256,256]{2,1,0:T(8,128)(2,1)S(1)}, bf16[2,256,256]{2,1,0:T(8,128)(2,1)S(1)}, u32[]{:S(2)}, u32[]{:S(2)}) %collective-permute-start.43) | collective-permute-done | bytes 262176 | tf_op jit(solution)/shard_map/ppermute | solution.py:215
  134.5 12.4 %collective-permute-done.42 = bf16[2,256,256]{2,1,0:T(8,128)(2,1)S(1)} collective-permute-done((bf16[2,256,256]{2,1,0:T(8,128)(2,1)S(1)}, bf16[2,256,256]{2,1,0:T(8,128)(2,1)S(1)}, u32[]{:S(2)}, u32[]{:S(2)}) %collective-permute-start.42) | collective-permute-done | bytes 262176 | tf_op jit(solution)/shard_map/ppermute | solution.py:215
  147.0 2.5 collective-permute-start.33
  154.9 20.8 %collective-permute-done.44.refs_8_ = bf16[4,2,256,256]{3,2,1,0:T(8,128)(2,1)S(1)} collective-permute-done((bf16[4,2,256,256]{3,2,1,0:T(8,128)(2,1)S(1)}, bf16[4,2,256,256]{3,2,1,0:T(8,128)(2,1)S(1)}, u32[]{:S(2)}, u32[]{:S(2)}) %collective-permute-start.44) | collective-permute-done | bytes 1048608 | tf_op jit(solution)/shard_map/ppermute | solution.py:215
  176.9 20.5 %collective-permute-done.45.refs_9_ = bf16[4,2,256,256]{3,2,1,0:T(8,128)(2,1)S(1)} collective-permute-done((bf16[4,2,256,256]{3,2,1,0:T(8,128)(2,1)S(1)}, bf16[4,2,256,256]{3,2,1,0:T(8,128)(2,1)S(1)}, u32[]{:S(2)}, u32[]{:S(2)}) %collective-permute-start.45) | collective-permute-done | bytes 1048608 | tf_op jit(solution)/shard_map/ppermute | solution.py:215
  200.0 6.5 %collective-permute-done.37.refs_2_ = bf16[4,128,256]{2,1,0:T(8,128)(2,1)S(1)} collective-permute-done((bf16[4,128,256]{2,1,0:T(8,128)(2,1)S(1)}, bf16[4,128,256]{2,1,0:T(8,128)(2,1)S(1)}, u32[]{:S(2)}, u32[]{:S(2)}) %collective-permute-start.37) | collective-permute-done | bytes 262176 | tf_op jit(solution)/shard_map/ppermute | solution.py:215
  206.5 3.4 %shard_map.177 = (f32[128,512]{1,0:T(8,128)S(1)}, f32[128,512]{1,0:T(8,128)}) custom-call(bf16[4,128,256]{2,1,0:T(8,128)(2,1)S(1)} %pad_maximum_fusion.2.refs_0_, bf16[4,128,256]{2,1,0:T(8,128)(2,1)S(1)} %collective-permute-done.36.refs_1_, bf16[4,128,256]{2,1,0:T(8,128)(2,1)S(1)} %collective-permute-done.37.refs_2_, ...), custom_call_target="tpu_custom_call" | custom-call | tf_op jit(solution)/shard_map/pallas_call | solution.py:329
  217.0 2.5 collective-permute-start.48
  245.7 2.8 collective-permute-done.59.refs_1_
  252.6 2.4 shard_map.180
  260.4 2.8 collective-permute-start.71
  273.7 2.5 collective-permute-done.75.refs_3_
  293.7 2.9 collective-permute-done.80.refs_1_
  296.5 2.4 collective-permute-done.81.refs_2_
  300.7 2.7 shard_map.183
  306.9 2.8 collective-permute-start.85
  (271 shorter events, 171.3 us)
Async XLA Ops:
  0.0 83.2 %collective-permute-start.6 = (bf16[8192,256]{1,0:T(8,128)(2,1)}, bf16[8192,256]{1,0:T(8,128)(2,1)}, u32[]{:S(2)}, u32[]{:S(2)}) collective-permute-start(bf16[8192,256]{1,0:T(8,128)(2,1)} %bitcast.105), channel_id=1, source_target_pairs={{0,16},{16,0},{1,17},{17,1},{2,18},{18,2},{3,19},{19,3},{4,20},{20... | collective-permute-start | bytes 12582920 | tf_op jit(solution)/shard_map/ppermute | solution.py:205
  0.6 108.8 %collective-permute-start.31 = (bf16[4096,512]{1,0:T(8,128)(2,1)}, bf16[4096,512]{1,0:T(8,128)(2,1)}, u32[]{:S(2)}, u32[]{:S(2)}) collective-permute-start(bf16[4096,512]{1,0:T(8,128)(2,1)} %bitcast.108), channel_id=1, source_target_pairs={{0,16},{16,0},{1,17},{17,1},{2,18},{18,2},{3,19},{19,3},{4,20},{20... | collective-permute-start | bytes 12582920 | tf_op jit(solution)/shard_map/ppermute | solution.py:205
  14.8 35.5 %collective-permute-start.17 = (bf16[512,1024]{1,0:T(8,128)(2,1)S(1)}, bf16[512,1024]{1,0:T(8,128)(2,1)}, u32[]{:S(2)}, u32[]{:S(2)}) collective-permute-start(bf16[512,1024]{1,0:T(8,128)(2,1)S(1)} %bitcast.113), channel_id=1, source_target_pairs={{0,16},{16,0},{1,17},{17,1},{2,18},{18,2},{3,19},{19,3},{4,20},{20... | collective-permute-start | bytes 3145736 | tf_op jit(solution)/shard_map/ppermute | solution.py:205
  19.0 6.6 %collective-permute-start.13 = (bf16[32,1280]{1,0:T(8,128)(2,1)}, bf16[32,1280]{1,0:T(8,128)(2,1)}, u32[]{:S(2)}, u32[]{:S(2)}) collective-permute-start(bf16[32,1280]{1,0:T(8,128)(2,1)} %fusion.9), channel_id=1, source_target_pairs={{0,12},{1,13},{2,14},{3,15},{4,8},{5,9},{6,10},{7,11},{8,4},{9,5},... | collective-permute-start | bytes 245768 | tf_op jit(solution)/shard_map/ppermute | solution.py:215
  36.5 8.4 %collective-permute-start.14 = (bf16[32,1280]{1,0:T(8,128)(2,1)S(1)}, bf16[32,1280]{1,0:T(8,128)(2,1)S(1)}, u32[]{:S(2)}, u32[]{:S(2)}) collective-permute-start(bf16[32,1280]{1,0:T(8,128)(2,1)S(1)} %fusion.10.p0), channel_id=1, source_target_pairs={{0,1},{1,0},{2,3},{3,2},{4,5},{5,4},{6,7},{7,6},{8,9},{9,8},{10,11... | collective-permute-start | bytes 245768 | tf_op jit(solution)/shard_map/ppermute | solution.py:215
  48.0 6.7 %collective-permute-start.3 = (bf16[4,144,256]{2,1,0:T(8,128)(2,1)S(1)}, bf16[4,144,256]{2,1,0:T(8,128)(2,1)S(1)}, u32[]{:S(2)}, u32[]{:S(2)}) collective-permute-start(bf16[4,144,256]{2,1,0:T(8,128)(2,1)S(1)} %pad_maximum_fusion.1), channel_id=1, source_target_pairs={{0,1},{1,0},{2,3},{3,2},{4,5},{5,4},{6,7},{7,6},{8,9},{9,8},{10,11... | collective-permute-start | bytes 884744 | tf_op jit(solution)/shard_map/ppermute | solution.py:215
  52.4 6.8 %collective-permute-start.65 = (bf16[128,256]{1,0:T(8,128)(2,1)S(1)}, bf16[128,256]{1,0:T(8,128)(2,1)S(1)}, u32[]{:S(2)}, u32[]{:S(2)}) collective-permute-start(bf16[128,256]{1,0:T(8,128)(2,1)S(1)} %get-tuple-element.46), channel_id=1, source_target_pairs={{0,12},{1,13},{2,14},{3,15},{4,8},{5,9},{6,10},{7,11},{8,4},{9,5},... | collective-permute-start | bytes 196616 | tf_op jit(solution)/shard_map/ppermute | solution.py:215
  53.1 10.1 %collective-permute-start.64 = (bf16[128,256]{1,0:T(8,128)(2,1)S(1)}, bf16[128,256]{1,0:T(8,128)(2,1)S(1)}, u32[]{:S(2)}, u32[]{:S(2)}) collective-permute-start(bf16[128,256]{1,0:T(8,128)(2,1)S(1)} %get-tuple-element.47), channel_id=1, source_target_pairs={{0,8},{1,9},{2,10},{3,11},{4,12},{5,13},{6,14},{7,15},{8,0},{9,1},... | collective-permute-start | bytes 196616 | tf_op jit(solution)/shard_map/ppermute | solution.py:215
  54.7 8.4 %collective-permute-start.63 = (bf16[128,256]{1,0:T(8,128)(2,1)S(1)}, bf16[128,256]{1,0:T(8,128)(2,1)S(1)}, u32[]{:S(2)}, u32[]{:S(2)}) collective-permute-start(bf16[128,256]{1,0:T(8,128)(2,1)S(1)} %get-tuple-element.45), channel_id=1, source_target_pairs={{0,4},{1,5},{2,6},{3,7},{4,0},{5,1},{6,2},{7,3},{8,12},{9,13},{10,... | collective-permute-start | bytes 196616 | tf_op jit(solution)/shard_map/ppermute | solution.py:215
  59.2 7.3 %collective-permute-start.20 = (bf16[128,256]{1,0:T(8,128)(2,1)S(1)}, bf16[128,256]{1,0:T(8,128)(2,1)S(1)}, u32[]{:S(2)}, u32[]{:S(2)}) collective-permute-start(bf16[128,256]{1,0:T(8,128)(2,1)S(1)} %get-tuple-element.48), channel_id=1, source_target_pairs={{0,12},{1,13},{2,14},{3,15},{4,8},{5,9},{6,10},{7,11},{8,4},{9,5},... | collective-permute-start | bytes 196616 | tf_op jit(solution)/shard_map/ppermute | solution.py:215
  66.5 6.7 %collective-permute-start.4 = (bf16[4,144,256]{2,1,0:T(8,128)(2,1)S(1)}, bf16[4,144,256]{2,1,0:T(8,128)(2,1)S(1)}, u32[]{:S(2)}, u32[]{:S(2)}) collective-permute-start(bf16[4,144,256]{2,1,0:T(8,128)(2,1)S(1)} %pad_maximum_fusion.1), channel_id=1, source_target_pairs={{0,2},{1,3},{2,0},{3,1},{4,6},{5,7},{6,4},{7,5},{8,10},{9,11},{10,... | collective-permute-start | bytes 884744 | tf_op jit(solution)/shard_map/ppermute | solution.py:215
  69.0 131.0 %collective-permute-start.39 = (bf16[8192,256]{1,0:T(8,128)(2,1)S(1)}, bf16[8192,256]{1,0:T(8,128)(2,1)}, u32[]{:S(2)}, u32[]{:S(2)}) collective-permute-start(bf16[8192,256]{1,0:T(8,128)(2,1)S(1)} %bitcast.121), channel_id=1, source_target_pairs={{0,16},{16,0},{1,17},{17,1},{2,18},{18,2},{3,19},{19,3},{4,20},{20... | collective-permute-start | bytes 12582920 | tf_op jit(solution)/shard_map/ppermute | solution.py:205
  69.4 8.3 %collective-permute-start.5 = (bf16[4,144,256]{2,1,0:T(8,128)(2,1)S(1)}, bf16[4,144,256]{2,1,0:T(8,128)(2,1)S(1)}, u32[]{:S(2)}, u32[]{:S(2)}) collective-permute-start(bf16[4,144,256]{2,1,0:T(8,128)(2,1)S(1)} %pad_maximum_fusion.1), channel_id=1, source_target_pairs={{0,3},{1,2},{2,1},{3,0},{4,7},{5,6},{6,5},{7,4},{8,11},{9,10},{10,... | collective-permute-start | bytes 884744 | tf_op jit(solution)/shard_map/ppermute | solution.py:215
  82.0 26.4 %collective-permute-start.40 = (bf16[512,1024]{1,0:T(8,128)(2,1)S(1)}, bf16[512,1024]{1,0:T(8,128)(2,1)S(1)}, u32[]{:S(2)}, u32[]{:S(2)}) collective-permute-start(bf16[512,1024]{1,0:T(8,128)(2,1)S(1)} %bitcast.111), channel_id=1, source_target_pairs={{0,16},{16,0},{1,17},{17,1},{2,18},{18,2},{3,19},{19,3},{4,20},{20... | collective-permute-start | bytes 3145736 | tf_op jit(solution)/shard_map/ppermute | solution.py:205
  83.0 144.1 %collective-permute-start.54 = (bf16[4096,512]{1,0:T(8,128)(2,1)}, bf16[4096,512]{1,0:T(8,128)(2,1)}, u32[]{:S(2)}, u32[]{:S(2)}) collective-permute-start(bf16[4096,512]{1,0:T(8,128)(2,1)} %bitcast.46.refs_4_), channel_id=1, source_target_pairs={{0,16},{16,0},{1,17},{17,1},{2,18},{18,2},{3,19},{19,3},{4,20},{20... | collective-permute-start | bytes 12582920 | tf_op jit(solution)/shard_map/ppermute | solution.py:205
  83.2 7.2 %collective-permute-start.24 = (bf16[128,256]{1,0:T(8,128)(2,1)S(1)}, bf16[128,256]{1,0:T(8,128)(2,1)S(1)}, u32[]{:S(2)}, u32[]{:S(2)}) collective-permute-start(bf16[128,256]{1,0:T(8,128)(2,1)S(1)} %pad_maximum_fusion.10.near_ref), channel_id=1, source_target_pairs={{0,16},{16,0},{1,17},{17,1},{2,18},{18,2},{3,19},{19,3},{4,20},{20... | collective-permute-start | bytes 196616 | tf_op jit(solution)/shard_map/ppermute | solution.py:205
  121.4 11.1 %collective-permute-start.43 = (bf16[2,256,256]{2,1,0:T(8,128)(2,1)S(1)}, bf16[2,256,256]{2,1,0:T(8,128)(2,1)S(1)}, u32[]{:S(2)}, u32[]{:S(2)}) collective-permute-start(bf16[2,256,256]{2,1,0:T(8,128)(2,1)S(1)} %get-tuple-element.40), channel_id=1, source_target_pairs={{0,12},{1,13},{2,14},{3,15},{4,8},{5,9},{6,10},{7,11},{8,4},{9,5},... | collective-permute-start | bytes 786440 | tf_op jit(solution)/shard_map/ppermute | solution.py:215
  123.5 23.5 %collective-permute-start.42 = (bf16[2,256,256]{2,1,0:T(8,128)(2,1)S(1)}, bf16[2,256,256]{2,1,0:T(8,128)(2,1)S(1)}, u32[]{:S(2)}, u32[]{:S(2)}) collective-permute-start(bf16[2,256,256]{2,1,0:T(8,128)(2,1)S(1)} %get-tuple-element.41), channel_id=1, source_target_pairs={{0,8},{1,9},{2,10},{3,11},{4,12},{5,13},{6,14},{7,15},{8,0},{9,1},... | collective-permute-start | bytes 786440 | tf_op jit(solution)/shard_map/ppermute | solution.py:215
  123.5 23.5 %collective-permute-start.41 = (bf16[2,256,256]{2,1,0:T(8,128)(2,1)S(1)}, bf16[2,256,256]{2,1,0:T(8,128)(2,1)S(1)}, u32[]{:S(2)}, u32[]{:S(2)}) collective-permute-start(bf16[2,256,256]{2,1,0:T(8,128)(2,1)S(1)} %get-tuple-element.42), channel_id=1, source_target_pairs={{0,4},{1,5},{2,6},{3,7},{4,0},{5,1},{6,2},{7,3},{8,12},{9,13},{10,... | collective-permute-start | bytes 786440 | tf_op jit(solution)/shard_map/ppermute | solution.py:215
  132.5 17.0 %collective-permute-start.35 = (bf16[128,256]{1,0:T(8,128)(2,1)S(1)}, bf16[128,256]{1,0:T(8,128)(2,1)S(1)}, u32[]{:S(2)}, u32[]{:S(2)}) collective-permute-start(bf16[128,256]{1,0:T(8,128)(2,1)S(1)} %add_convert_fusion.3), channel_id=1, source_target_pairs={{0,12},{1,13},{2,14},{3,15},{4,8},{5,9},{6,10},{7,11},{8,4},{9,5},... | collective-permute-start | bytes 196616 | tf_op jit(solution)/shard_map/ppermute | solution.py:215
  149.6 26.2 %collective-permute-start.44 = (bf16[4,2,256,256]{3,2,1,0:T(8,128)(2,1)S(1)}, bf16[4,2,256,256]{3,2,1,0:T(8,128)(2,1)S(1)}, u32[]{:S(2)}, u32[]{:S(2)}) collective-permute-start(bf16[4,2,256,256]{3,2,1,0:T(8,128)(2,1)S(1)} %pad_maximum_fusion.refs_7_), channel_id=1, source_target_pairs={{0,1},{1,0},{2,3},{3,2},{4,5},{5,4},{6,7},{7,6},{8,9},{9,8},{10,11... | collective-permute-start | bytes 3145736 | tf_op jit(solution)/shard_map/ppermute | solution.py:215
  152.2 45.1 %collective-permute-start.45 = (bf16[4,2,256,256]{3,2,1,0:T(8,128)(2,1)S(1)}, bf16[4,2,256,256]{3,2,1,0:T(8,128)(2,1)S(1)}, u32[]{:S(2)}, u32[]{:S(2)}) collective-permute-start(bf16[4,2,256,256]{3,2,1,0:T(8,128)(2,1)S(1)} %pad_maximum_fusion.refs_7_), channel_id=1, source_target_pairs={{0,2},{1,3},{2,0},{3,1},{4,6},{5,7},{6,4},{7,5},{8,10},{9,11},{10,... | collective-permute-start | bytes 3145736 | tf_op jit(solution)/shard_map/ppermute | solution.py:215
  153.1 45.1 %collective-permute-start.46 = (bf16[4,2,256,256]{3,2,1,0:T(8,128)(2,1)S(1)}, bf16[4,2,256,256]{3,2,1,0:T(8,128)(2,1)S(1)}, u32[]{:S(2)}, u32[]{:S(2)}) collective-permute-start(bf16[4,2,256,256]{3,2,1,0:T(8,128)(2,1)S(1)} %pad_maximum_fusion.refs_7_), channel_id=1, source_target_pairs={{0,3},{1,2},{2,1},{3,0},{4,7},{5,6},{6,5},{7,4},{8,11},{9,10},{10,... | collective-permute-start | bytes 3145736 | tf_op jit(solution)/shard_map/ppermute | solution.py:215
  175.8 24.2 %collective-permute-start.36 = (bf16[4,128,256]{2,1,0:T(8,128)(2,1)S(1)}, bf16[4,128,256]{2,1,0:T(8,128)(2,1)S(1)}, u32[]{:S(2)}, u32[]{:S(2)}) collective-permute-start(bf16[4,128,256]{2,1,0:T(8,128)(2,1)S(1)} %pad_maximum_fusion.2.refs_0_), channel_id=1, source_target_pairs={{0,1},{1,0},{2,3},{3,2},{4,5},{5,4},{6,7},{7,6},{8,9},{9,8},{10,11... | collective-permute-start | bytes 786440 | tf_op jit(solution)/shard_map/ppermute | solution.py:215
  197.3 9.2 %collective-permute-start.37 = (bf16[4,128,256]{2,1,0:T(8,128)(2,1)S(1)}, bf16[4,128,256]{2,1,0:T(8,128)(2,1)S(1)}, u32[]{:S(2)}, u32[]{:S(2)}) collective-permute-start(bf16[4,128,256]{2,1,0:T(8,128)(2,1)S(1)} %pad_maximum_fusion.2.refs_0_), channel_id=1, source_target_pairs={{0,2},{1,3},{2,0},{3,1},{4,6},{5,7},{6,4},{7,5},{8,10},{9,11},{10,... | collective-permute-start | bytes 786440 | tf_op jit(solution)/shard_map/ppermute | solution.py:215
  198.2 8.3 %collective-permute-start.38 = (bf16[4,128,256]{2,1,0:T(8,128)(2,1)S(1)}, bf16[4,128,256]{2,1,0:T(8,128)(2,1)S(1)}, u32[]{:S(2)}, u32[]{:S(2)}) collective-permute-start(bf16[4,128,256]{2,1,0:T(8,128)(2,1)S(1)} %pad_maximum_fusion.2.refs_0_), channel_id=1, source_target_pairs={{0,3},{1,2},{2,1},{3,0},{4,7},{5,6},{6,5},{7,4},{8,11},{9,10},{10,... | collective-permute-start | bytes 786440 | tf_op jit(solution)/shard_map/ppermute | solution.py:215
  224.1 6.8 %collective-permute-start.53 = (bf16[4,128,128]{2,1,0:T(8,128)(2,1)S(1)}, bf16[4,128,128]{2,1,0:T(8,128)(2,1)S(1)}, u32[]{:S(2)}, u32[]{:S(2)}) collective-permute-start(bf16[4,128,128]{2,1,0:T(8,128)(2,1)S(1)} %pad_maximum_fusion.7.refs_0_), channel_id=1, source_target_pairs={{0,3},{1,2},{2,1},{3,0},{4,7},{5,6},{6,5},{7,4},{8,11},{9,10},{10,... | collective-permute-start | bytes 393224 | tf_op jit(solution)/shard_map/ppermute | solution.py:215
  225.4 7.7 %collective-permute-start.68 = (bf16[128,256]{1,0:T(8,128)(2,1)}, bf16[128,256]{1,0:T(8,128)(2,1)S(1)}, u32[]{:S(2)}, u32[]{:S(2)}) collective-permute-start(bf16[128,256]{1,0:T(8,128)(2,1)} %get-tuple-element.43), channel_id=1, source_target_pairs={{0,3},{1,2},{2,1},{3,0},{4,7},{5,6},{6,5},{7,4},{8,11},{9,10},{10,... | collective-permute-start | bytes 196616 | tf_op jit(solution)/shard_map/ppermute | solution.py:215
  242.7 8.1 %collective-permute-start.60 = (bf16[4,128,256]{2,1,0:T(8,128)(2,1)S(1)}, bf16[4,128,256]{2,1,0:T(8,128)(2,1)S(1)}, u32[]{:S(2)}, u32[]{:S(2)}) collective-permute-start(bf16[4,128,256]{2,1,0:T(8,128)(2,1)S(1)} %pad_maximum_fusion.3.refs_0_), channel_id=1, source_target_pairs={{0,2},{1,3},{2,0},{3,1},{4,6},{5,7},{6,4},{7,5},{8,10},{9,11},{10,... | collective-permute-start | bytes 786440 | tf_op jit(solution)/shard_map/ppermute | solution.py:215
  244.1 8.5 %collective-permute-start.61 = (bf16[4,128,256]{2,1,0:T(8,128)(2,1)S(1)}, bf16[4,128,256]{2,1,0:T(8,128)(2,1)S(1)}, u32[]{:S(2)}, u32[]{:S(2)}) collective-permute-start(bf16[4,128,256]{2,1,0:T(8,128)(2,1)S(1)} %pad_maximum_fusion.3.refs_0_), channel_id=1, source_target_pairs={{0,3},{1,2},{2,1},{3,0},{4,7},{5,6},{6,5},{7,4},{8,11},{9,10},{10,... | collective-permute-start | bytes 786440 | tf_op jit(solution)/shard_map/ppermute | solution.py:215
  290.5 8.4 %collective-permute-start.81 = (bf16[4,128,256]{2,1,0:T(8,128)(2,1)S(1)}, bf16[4,128,256]{2,1,0:T(8,128)(2,1)S(1)}, u32[]{:S(2)}, u32[]{:S(2)}) collective-permute-start(bf16[4,128,256]{2,1,0:T(8,128)(2,1)S(1)} %pad_maximum_fusion.4.refs_0_), channel_id=1, source_target_pairs={{0,2},{1,3},{2,0},{3,1},{4,6},{5,7},{6,4},{7,5},{8,10},{9,11},{10,... | collective-permute-start | bytes 786440 | tf_op jit(solution)/shard_map/ppermute | solution.py:215
  292.2 8.5 %collective-permute-start.82 = (bf16[4,128,256]{2,1,0:T(8,128)(2,1)S(1)}, bf16[4,128,256]{2,1,0:T(8,128)(2,1)S(1)}, u32[]{:S(2)}, u32[]{:S(2)}) collective-permute-start(bf16[4,128,256]{2,1,0:T(8,128)(2,1)S(1)} %pad_maximum_fusion.4.refs_0_), channel_id=1, source_target_pairs={{0,3},{1,2},{2,1},{3,0},{4,7},{5,6},{6,5},{7,4},{8,11},{9,10},{10,... | collective-permute-start | bytes 786440 | tf_op jit(solution)/shard_map/ppermute | solution.py:215
  (79 other events, 663.2 us)

commit v2 on v0

--- a/solution.py
+++ b/solution.py
@@ -1,6 +1,11 @@
+import functools
+
 import jax
 import jax.numpy as jnp
+import numpy as np
 from jax import lax
+from jax.experimental import pallas as pl
+from jax.experimental.pallas import tpu as pltpu
 from jax.sharding import PartitionSpec as P
 
 HD = 128
@@ -63,7 +68,7 @@
     return jnp.dot(segment, weight, preferred_element_type=jnp.float32)
 
 
-def body(
+def blocked_body(
     text_states,
     vision_states,
     visible_tiles,
@@ -181,7 +186,540 @@
     return outputs[None]
 
 
+VMEM_LIMIT = 8 * 1024 * 1024
+GROUP = 4
+
+
+def params():
+    return pltpu.CompilerParams(vmem_limit_bytes=VMEM_LIMIT)
+
+
+def in_vmem():
+    return pl.BlockSpec(memory_space=pltpu.VMEM)
+
+
+def swap_cores(block):
+    return lax.ppermute(block, "section", [(0, 1), (1, 0)])
+
+
+def send_xor(block, masks):
+    chips = lax.axis_size("tp")
+    route = [
+        (core * chips + chip, core * chips + (chip ^ masks[core]))
+        for core in range(2)
+        for chip in range(chips)
+    ]
+    return lax.ppermute(block, ("section", "tp"), route)
+
+
+def gather_chips(block):
+    first = jnp.stack(
+        [block] + [send_xor(block, (GROUP * k, k)) for k in range(1, GROUP)]
+    )
+    return [first] + [send_xor(first, (k, GROUP * k)) for k in range(1, GROUP)]
+
+
+def total(parts):
+    return sum((part.astype(jnp.float32) for part in parts[1:]), parts[0].astype(jnp.float32))
+
+
+def reduce_heads(blocks):
+    near = total(
+        [blocks[0]] + [send_xor(blocks[k], (GROUP * k, GROUP * k)) for k in range(1, GROUP)]
+    ).astype(jnp.bfloat16)
+    return total([near] + [send_xor(near, (k, k)) for k in range(1, GROUP)])
+
+
+def piece_chip(core, chip, outer, inner):
+    return jnp.where(core == 0, chip ^ (GROUP * inner) ^ outer, chip ^ inner ^ (GROUP * outer))
+
+
+def with_weight(section, own_ref, other_ref, run):
+    core = lax.axis_index("section")
+
+    @pl.when(core == section)
+    def _():
+        run(own_ref)
+
+    @pl.when(core != section)
+    def _():
+        run(other_ref)
+
+
+def weight_rows(weight_ref, at, rows):
+    source = piece_chip(lax.axis_index("section"), lax.axis_index("tp"), at // GROUP, at % GROUP)
+    return weight_ref[pl.ds(pl.multiple_of(source * rows, rows), rows), :]
+
+
+def project(section, gain_at, rows, x_refs, gain_ref, own_ref, other_ref, product_ref):
+    depth = x_refs[0].shape[2]
+
+    def run(weight_ref):
+        product = jnp.zeros(product_ref.shape, jnp.float32)
+        squares = jnp.zeros((rows, depth), jnp.float32)
+        for at in range(GROUP * GROUP):
+            piece = x_refs[at // GROUP][at % GROUP, :rows, :].astype(jnp.float32)
+            squares = squares + piece * piece
+            gain_row = gain_ref[at, gain_at : gain_at + 1, :].astype(jnp.float32)
+            scaled = (piece * gain_row).astype(jnp.bfloat16)
+            product = product + jnp.dot(
+                scaled, weight_rows(weight_ref, at, depth), preferred_element_type=jnp.float32
+            )
+        mean_square = jnp.sum(squares, axis=1, keepdims=True) / (GROUP * GROUP * depth)
+        product_ref[...] = product * lax.rsqrt(mean_square + epsilon)
+
+    with_weight(section, own_ref, other_ref, run)
+    return product_ref[...]
+
+
+def dot_rows(left, right):
+    return lax.dot_general(
+        left, right, (((1,), (1,)), ((), ())), preferred_element_type=jnp.float32
+    )
+
+
+def mix(queries, key_sets, value_sets, allowed_sets, value_scales):
+    scores = []
+    for keys, allowed, scale in zip(key_sets, allowed_sets, value_scales):
+        part = dot_rows(queries, keys) * HD ** (-0.5)
+        if scale is not None:
+            part = part * scale
+        scores.append(jnp.where(allowed, part, -1e30))
+    top = functools.reduce(
+        jnp.maximum, [jnp.max(part, axis=1, keepdims=True) for part in scores]
+    )
+    raised = [jnp.exp(part - top) for part in scores]
+    bottom = sum(jnp.sum(part, axis=1, keepdims=True) for part in raised)
+    mixed = jnp.zeros(queries.shape, jnp.float32)
+    for part, values, scale in zip(raised, value_sets, value_scales):
+        weights = part / bottom
+        if scale is not None:
+            weights = weights * scale
+        mixed = mixed + jnp.dot(
+            weights.astype(jnp.bfloat16), values, preferred_element_type=jnp.float32
+        )
+    return mixed.astype(jnp.bfloat16)
+
+
+def by_head(queries):
+    heads = queries.shape[1] // HD
+    return jnp.concatenate([queries[:, h * HD : (h + 1) * HD] for h in range(heads)], axis=0)
+
+
+def side_by_side(mixed, rows):
+    return jnp.concatenate(
+        [mixed[start : start + rows] for start in range(0, mixed.shape[0], rows)], axis=1
+    )
+
+
+def cross_attend(tile_rows, queries, near_ref, far_ref, tiles_ref, qk_ref, out_ref):
+    core = lax.axis_index("section")
+    rows = out_ref.shape[0]
+    queries = rms_norm(by_head(queries), qk_ref[2:3, :HD]).astype(jnp.bfloat16)
+    row_tiles = tiles_ref[pl.ds(pl.multiple_of(core * rows, rows), rows), :]
+    row_tiles = jnp.concatenate([row_tiles] * (queries.shape[0] // rows), axis=0)
+    count = near_ref.shape[0]
+    key_at = lax.broadcasted_iota(jnp.int32, (queries.shape[0], count), 1)
+    allowed = [
+        key_at + core * count < row_tiles * tile_rows,
+        key_at + (1 - core) * count < row_tiles * tile_rows,
+    ]
+    sets = (near_ref[...], far_ref[...])
+    mixed = mix(
+        queries, [kv[:, :HD] for kv in sets], [kv[:, HD:] for kv in sets], allowed, (None, None)
+    )
+    out_ref[...] = side_by_side(mixed, rows)
+
+
+def cross_kernel(section, gain_at, tile_rows, *refs):
+    x_refs = refs[:GROUP]
+    (gain_ref, near_ref, far_ref, tiles_ref, qk_ref, own_ref, other_ref) = refs[GROUP : GROUP + 7]
+    out_ref, product_ref = refs[GROUP + 7 :]
+    rows = out_ref.shape[0]
+    queries = project(section, gain_at, rows, x_refs, gain_ref, own_ref, other_ref, product_ref)
+    cross_attend(tile_rows, queries, near_ref, far_ref, tiles_ref, qk_ref, out_ref)
+
+
+def cross_mix(section, gain_at, tile_rows, rows, pieces, gains, near, far, tiles, qk, own, other):
+    columns = own.shape[1]
+    return pl.pallas_call(
+        functools.partial(cross_kernel, section, gain_at, tile_rows),
+        out_shape=jax.ShapeDtypeStruct((rows, columns), jnp.bfloat16),
+        in_specs=[in_vmem()] * (GROUP + 7),
+        out_specs=in_vmem(),
+        scratch_shapes=[pltpu.VMEM((rows, columns), jnp.float32)],
+        compiler_params=params(),
+    )(*pieces, gains, near, far, tiles, qk, own, other)
+
+
+def attend_kernel(tile_rows, q_ref, near_ref, far_ref, tiles_ref, qk_ref, out_ref):
+    cross_attend(tile_rows, q_ref[...], near_ref, far_ref, tiles_ref, qk_ref, out_ref)
+
+
+def cross_mix_from(tile_rows, queries, near, far, tiles, qk):
+    return pl.pallas_call(
+        functools.partial(attend_kernel, tile_rows),
+        out_shape=jax.ShapeDtypeStruct(queries.shape, jnp.bfloat16),
+        in_specs=[in_vmem()] * 5,
+        out_specs=in_vmem(),
+        compiler_params=params(),
+    )(queries, near, far, tiles, qk)
+
+
+def plain_query_kernel(section, gain_at, *refs):
+    x_refs = refs[:GROUP]
+    gain_ref, own_ref, other_ref, out_ref = refs[GROUP:]
+    rows = out_ref.shape[0]
+    project(section, gain_at, rows, x_refs, gain_ref, own_ref, other_ref, out_ref)
+
+
+def plain_query_part(section, gain_at, rows, pieces, gains, own, other):
+    return pl.pallas_call(
+        functools.partial(plain_query_kernel, section, gain_at),
+        out_shape=jax.ShapeDtypeStruct((rows, own.shape[1]), jnp.float32),
+        in_specs=[in_vmem()] * (GROUP + 3),
+        out_specs=in_vmem(),
+        compiler_params=params(),
+    )(*pieces, gains, own, other)
+
+
+def turn(values, cosine, sine):
+    half = HD // 2
+    swapped = jnp.concatenate([values[:, half:], values[:, :half]], axis=1)
+    return values * cosine + swapped * sine
+
+
+def query_kernel(section, gain_at, *refs):
+    x_refs = refs[:GROUP]
+    gain_ref, cosine_ref, sine_ref, own_ref, other_ref, out_ref, product_ref = refs[GROUP:]
+    rows = product_ref.shape[0]
+    core = lax.axis_index("section")
+    mine = pl.ds(pl.multiple_of(core * rows, rows), rows)
+    queries = project(section, gain_at, rows, x_refs, gain_ref, own_ref, other_ref, product_ref)
+    for head in range(queries.shape[1] // HD):
+        turned = turn(queries[:, head * HD : (head + 1) * HD], cosine_ref[mine, :], sine_ref[mine, :])
+        out_ref[head * rows : (head + 1) * rows, :] = turned.astype(jnp.bfloat16)
+
+
+def query_part(section, gain_at, rows, pieces, gains, cosine, sine, own, other):
+    columns = own.shape[1]
+    return pl.pallas_call(
+        functools.partial(query_kernel, section, gain_at),
+        out_shape=jax.ShapeDtypeStruct((rows * columns // HD, HD), jnp.bfloat16),
+        in_specs=[in_vmem()] * (GROUP + 5),
+        out_specs=in_vmem(),
+        scratch_shapes=[pltpu.VMEM((rows, columns), jnp.float32)],
+        compiler_params=params(),
+    )(*pieces, gains, cosine, sine, own, other)
+
+
+def self_kernel(width, q_ref, near_ref, far_ref, cosine_ref, sine_ref, out_ref):
+    core = lax.axis_index("section")
+    rows = out_ref.shape[0]
+    queries = q_ref[...]
+    shape = (queries.shape[0], rows)
+    row_at = lax.rem(lax.broadcasted_iota(jnp.int32, shape, 0), rows) + core * rows
+    key_at = lax.broadcasted_iota(jnp.int32, shape, 1)
+    keys, values, allowed, scales = [], [], [], []
+    for ref, side in ((near_ref, core), (far_ref, 1 - core)):
+        at = pl.ds(pl.multiple_of(side * rows, rows), rows)
+        raw = ref[:rows, :HD].astype(jnp.float32)
+        keys.append(turn(raw, cosine_ref[at, :], sine_ref[at, :]).astype(jnp.bfloat16))
+        values.append(ref[:rows, HD:])
+        allowed.append(key_at + side * rows <= row_at)
+        square_sum = ref[rows : rows + 1, :rows].astype(jnp.float32)
+        scales.append(lax.rsqrt(square_sum / width + epsilon))
+    out_ref[...] = side_by_side(mix(queries, keys, values, allowed, scales), rows)
+
+
+def self_mix(width, queries, near, far, cosine, sine):
+    rows = cosine.shape[0] // 2
+    return pl.pallas_call(
+        functools.partial(self_kernel, width),
+        out_shape=jax.ShapeDtypeStruct((rows, queries.shape[0] // rows * HD), jnp.bfloat16),
+        in_specs=[in_vmem()] * 5,
+        out_specs=in_vmem(),
+        compiler_params=params(),
+    )(queries, near, far, cosine, sine)
+
+
+def key_value_kernel(section, hidden_ref, small_ref, own_ref, other_ref, out_ref, product):
+    high = lax.axis_index("tp") // GROUP
+    rows = hidden_ref.shape[0]
+    hidden = hidden_ref[...].astype(jnp.float32)
+    scaled = (hidden * small_ref[1:2, :]).astype(jnp.bfloat16)
+    squares = hidden * hidden
+    top = squares.astype(jnp.bfloat16)
+    rest = (squares - top.astype(jnp.float32)).astype(jnp.bfloat16)
+    ones = jnp.ones((16, hidden.shape[1]), jnp.bfloat16)
+    square_sum = dot_rows(ones, top) + dot_rows(ones, rest)
+    square_sum = jnp.concatenate(
+        [square_sum, jnp.zeros((16, 2 * HD - rows), jnp.float32)], axis=1
+    ).astype(jnp.bfloat16)
+
+    def run(weight_ref):
+        product[...] = jnp.dot(scaled, weight_ref[...], preferred_element_type=jnp.float32)
+
+    with_weight(section, own_ref, other_ref, run)
+    for k in range(GROUP):
+        for part in range(2):
+            start = pl.multiple_of((part * KV + (high ^ k)) * HD, HD)
+            out_ref[k, :rows, part * HD : (part + 1) * HD] = product[:, pl.ds(start, HD)].astype(
+                jnp.bfloat16
+            )
+        out_ref[k, rows:, :] = square_sum
+
+
+def key_value_part(section, hidden, small, own, other):
+    rows = hidden.shape[0]
+    return pl.pallas_call(
+        functools.partial(key_value_kernel, section),
+        out_shape=jax.ShapeDtypeStruct((GROUP, rows + 16, 2 * HD), jnp.bfloat16),
+        in_specs=[in_vmem()] * 4,
+        out_specs=in_vmem(),
+        scratch_shapes=[pltpu.VMEM((rows, own.shape[1]), jnp.float32)],
+        compiler_params=params(),
+    )(hidden, small, own, other)
+
+
+def out_kernel(section, gated, *refs):
+    x_refs = refs[:GROUP]
+    hidden_ref, small_ref, tiles_ref, own_ref, other_ref, out_ref = refs[GROUP:]
+    core = lax.axis_index("section")
+    rows = out_ref.shape[0]
+    depth = x_refs[0].shape[2]
+
+    def run(weight_ref):
+        branch = jnp.zeros(out_ref.shape, jnp.float32)
+        for at in range(GROUP * GROUP):
+            branch = branch + jnp.dot(
+                x_refs[at // GROUP][at % GROUP],
+                weight_rows(weight_ref, at, depth),
+                preferred_element_type=jnp.float32,
+            )
+        if gated:
+            row_tiles = tiles_ref[pl.ds(pl.multiple_of(core * rows, rows), rows), :1]
+            branch = branch * (row_tiles > 0).astype(jnp.float32) * jnp.tanh(small_ref[3:4, :])
+        out_ref[...] = (hidden_ref[...].astype(jnp.float32) + branch).astype(jnp.bfloat16)
+
+    with_weight(section, own_ref, other_ref, run)
+
+
+def out_part(section, gated, pieces, hidden, small, tiles, own, other):
+    return pl.pallas_call(
+        functools.partial(out_kernel, section, gated),
+        out_shape=jax.ShapeDtypeStruct(hidden.shape, jnp.bfloat16),
+        in_specs=[in_vmem()] * (GROUP + 5),
+        out_specs=in_vmem(),
+        compiler_params=params(),
+    )(*pieces, hidden, small, tiles, own, other)
+
+
+def encoder_kernel(states_ref, gain_ref, fc1_ref, fc2_ref, out_ref, product):
+    core = lax.axis_index("section")
+    chip = lax.axis_index("tp")
+    member = jnp.where(core == 0, chip % GROUP, chip // GROUP)
+    states = states_ref[...].astype(jnp.float32)
+    centred = states - jnp.mean(states, axis=-1, keepdims=True)
+    spread = jnp.mean(centred * centred, axis=-1, keepdims=True)
+    normed = (centred * lax.rsqrt(spread + epsilon) * gain_ref[...]).astype(jnp.bfloat16)
+    inner = jnp.dot(normed, fc1_ref[...], preferred_element_type=jnp.float32)
+    inner = (0.5 * inner * (1.0 + lax.erf(inner * 2.0 ** (-0.5)))).astype(jnp.bfloat16)
+    product[...] = jnp.dot(inner, fc2_ref[...], preferred_element_type=jnp.float32).astype(
+        jnp.bfloat16
+    )
+    rows = out_ref.shape[1]
+    for k in range(GROUP):
+        out_ref[k] = product[pl.ds(pl.multiple_of((member ^ k) * rows, rows), rows), :]
+
+
+def encoder_part(states, gain, fc1, fc2):
+    rows, width = states.shape
+    return pl.pallas_call(
+        encoder_kernel,
+        out_shape=jax.ShapeDtypeStruct((GROUP, rows // GROUP, width), jnp.bfloat16),
+        in_specs=[in_vmem()] * 4,
+        out_specs=in_vmem(),
+        scratch_shapes=[pltpu.VMEM((rows, width), jnp.bfloat16)],
+        compiler_params=params(),
+    )(states, gain, fc1, fc2)
+
+
+def image_kernel(p0, p1, p2, p3, projector_ref, own_ref, other_ref, out_ref, rows_ref, kv_ref):
+    core = lax.axis_index("section")
+    chip = lax.axis_index("tp")
+    low, high = chip % GROUP, chip // GROUP
+    member = jnp.where(core == 0, low, high)
+    count = p0.shape[0]
+    for k, ref in enumerate((p0, p1, p2, p3)):
+        rows_ref[pl.ds(pl.multiple_of((member ^ k) * count, count), count), :] = ref[...]
+    feats = jnp.dot(
+        rows_ref[...], projector_ref[...], preferred_element_type=jnp.float32
+    ).astype(jnp.bfloat16)
+    for section in range(2):
+        weight = jnp.where(core == section, own_ref[...], other_ref[...])
+        kv_ref[...] = jnp.dot(feats, weight, preferred_element_type=jnp.float32)
+        for k in range(GROUP):
+            head = high ^ k
+            for part in range(2):
+                start = pl.multiple_of((part * KV + head) * HD, HD)
+                out_ref[section, k, :, part * HD : (part + 1) * HD] = kv_ref[
+                    :, pl.ds(start, HD)
+                ].astype(jnp.bfloat16)
+
+
+def image_part(pieces, projector, own, other):
+    rows = GROUP * pieces[0].shape[0]
+    return pl.pallas_call(
+        image_kernel,
+        out_shape=jax.ShapeDtypeStruct((2, GROUP, rows, 2 * HD), jnp.bfloat16),
+        in_specs=[in_vmem()] * 7,
+        out_specs=in_vmem(),
+        scratch_shapes=[
+            pltpu.VMEM((rows, projector.shape[0]), jnp.bfloat16),
+            pltpu.VMEM((rows, own.shape[1]), jnp.float32),
+        ],
+        compiler_params=params(),
+    )(*pieces, projector, own, other)
+
+
+def rope_tables(positions):
+    inverse = 500000.0 ** (-np.arange(HD // 2) * (2.0 / HD))
+    angles = np.arange(positions)[:, None] * inverse[None, :]
+    cosine, sine = np.cos(angles), np.sin(angles)
+    return (
+        np.concatenate([cosine, cosine], axis=1).astype(np.float32),
+        np.concatenate([-sine, sine], axis=1).astype(np.float32),
+    )
+
+
+def paired_body(
+    text_states,
+    vision_states,
+    visible_tiles,
+    vision_norm_gain,
+    vision_fc1,
+    vision_fc2,
+    vision_gate,
+    projector,
+    cross_norm,
+    cross_q,
+    cross_kv,
+    cross_qk_gain,
+    cross_o,
+    cross_gate,
+    self_norm,
+    self_q,
+    self_kv,
+    self_o,
+):
+    core = lax.axis_index("section")
+    chip = lax.axis_index("tp")
+    seq_len, local_width = text_states.shape
+    rows = seq_len // 2
+    full_width = local_width * lax.axis_size("tp")
+    member = jnp.where(core == 0, chip % GROUP, chip // GROUP)
+
+    small = jnp.concatenate(
+        [
+            cross_norm.astype(jnp.float32),
+            self_norm.astype(jnp.float32),
+            jnp.pad(cross_qk_gain.reshape(1, -1), ((0, 0), (0, local_width - 2 * HD))),
+            jnp.broadcast_to(cross_gate[None], (1, local_width)),
+        ]
+    )
+    small = lax.all_gather(small, "section", axis=0)
+    own_cross_kv, own_cross_q, own_cross_o = cross_kv[0], cross_q[0], cross_o[0]
+    own_self_kv, own_self_q, own_self_o = self_kv[0], self_q[0], self_o[0]
+    far_cross_kv = swap_cores(own_cross_kv)
+    far_cross_q = swap_cores(own_cross_q)
+    far_cross_o = swap_cores(own_cross_o)
+    far_self_kv = swap_cores(own_self_kv)
+    far_self_q = swap_cores(own_self_q)
+    far_self_o = swap_cores(own_self_o)
+
+    hidden = lax.dynamic_slice_in_dim(text_states, core * rows, rows, 0)
+    gain_rows = small[:, :2].astype(jnp.bfloat16).reshape(4, local_width)
+    entry = jnp.concatenate(
+        [hidden, gain_rows, jnp.zeros((12, local_width), jnp.bfloat16)], axis=0
+    )
+    come = [send_xor(entry, (GROUP * k, k)) for k in range(1, GROUP)]
+
+    branch = encoder_part(vision_states, vision_norm_gain[None], vision_fc1, vision_fc2)
+    branch, come = lax.optimization_barrier((branch, come))
+    first = jnp.stack([entry] + come)
+    pieces = [first] + [send_xor(first, (k, GROUP * k)) for k in range(1, GROUP)]
+    near = total(
+        [branch[0]] + [send_xor(branch[k], (k, GROUP * k)) for k in range(1, GROUP)]
+    ).astype(jnp.bfloat16)
+    come = [send_xor(near, (GROUP * k, k)) for k in range(1, GROUP)]
+    come, pieces = lax.optimization_barrier((come, pieces))
+    gains = jnp.concatenate([piece[:, rows:] for piece in pieces], axis=0)
+    branch_rows = total([near] + come)
+    vis_rows = lax.dynamic_index_in_dim(
+        vision_states.reshape(branch.shape), member, 0, keepdims=False
+    )
+    vis_out = (vis_rows.astype(jnp.float32) + jnp.tanh(vision_gate[0]) * branch_rows).astype(
+        jnp.bfloat16
+    )
+    come = [send_xor(vis_out, (k, GROUP * k)) for k in range(1, GROUP)]
+    queries = plain_query_part(0, 0, rows, pieces, gains, own_cross_q, far_cross_q)
+    come, queries = lax.optimization_barrier((come, queries))
+    vis_pieces = [vis_out] + come
+
+    image_parts = image_part(vis_pieces, projector, own_cross_kv, far_cross_kv)
+    image_kv = []
+    for section in range(2):
+        kv_rows = reduce_heads(image_parts[section])
+        key_gain = small[section, 2, HD : 2 * HD]
+        near = jnp.concatenate(
+            [rms_norm(kv_rows[:, :HD], key_gain), kv_rows[:, HD:]], axis=1
+        ).astype(jnp.bfloat16)
+        image_kv.append((near, swap_cores(near)))
+
+    tile_rows = 2 * vision_states.shape[0] // TILES
+    tiles = jnp.broadcast_to(visible_tiles[:, None], (seq_len, HD))
+    cosine, sine = (jnp.asarray(table) for table in rope_tables(seq_len))
+
+    results = []
+    for section in range(2):
+        scalars = small[section]
+        near, far = image_kv[section]
+        if section == 0:
+            mixed = cross_mix_from(tile_rows, queries, near, far, tiles, scalars)
+        else:
+            mixed = cross_mix(
+                section, 2 * section, tile_rows, rows, gather_chips(hidden), gains, near, far,
+                tiles, scalars, own_cross_q, far_cross_q,
+            )
+        hidden = out_part(
+            section, True, gather_chips(mixed), hidden, scalars, tiles, own_cross_o, far_cross_o
+        )
+        pieces = gather_chips(hidden)
+        near = reduce_heads(
+            key_value_part(section, hidden, scalars, own_self_kv, far_self_kv)
+        ).astype(jnp.bfloat16)
+        far = swap_cores(near)
+        queries = query_part(
+            section, 2 * section + 1, rows, pieces, gains, cosine, sine, own_self_q, far_self_q
+        )
+        mixed = self_mix(full_width, queries, near, far, cosine, sine)
+        hidden = out_part(
+            section, False, gather_chips(mixed), hidden, scalars, tiles, own_self_o, far_self_o
+        )
+        results.append(hidden)
+    come = swap_cores(jnp.where(core == 0, results[1], results[0]))
+    return jnp.where(
+        core == 0,
+        jnp.concatenate([results[0], come], axis=0),
+        jnp.concatenate([come, results[1]], axis=0),
+    )[None]
+
+
 def solution(mesh):
+    chips = mesh.shape["tp"]
+    paired = mesh.shape["section"] == 2 and chips == GROUP * GROUP and HEADS == 2 * chips
+    body = paired_body if paired else blocked_body
     in_specs = (
         P(None, "tp"),
         P("section", None),

time: 1200 us -> 276 us (0.23)
  waiting for transfers between devices: 737 us -> 120 us
  blocking collectives: 329 us -> 3.97 us
  starting transfers between devices: 3.19 us -> 116 us
  matrix products: 61.9 us -> 0 us
  other arithmetic: 34.3 us -> 4.83 us
  Pallas kernels: 0 us -> 21 us
  between operations: 15.6 us -> 2 us
    psum x5 -> x0, waiting for transfers between devices: 481 us -> none  [the longest x3 306 us: body(): lax.psum(jnp.dot(own_cols, self_kv[0], preferred_element_type=jnp.float32...]
    all_gather x9 -> x1, blocking collectives: 329 us -> 3.97 us  [paired_body(): small = lax.all_gather(small, 'section', axis=0)]
    all_gather x6 -> x0, waiting for transfers between devices: 254 us -> none  [body(): lax.all_gather(current, 'tp', axis=1, tiled=True)]
    ppermute x2 -> x92, waiting for transfers between devices: 1.76 us -> 120 us  [the longest x81 116 us: send_xor(): return lax.ppermute(block, ('section', 'tp'), route)]
    ppermute x2 -> x92, starting transfers between devices: 2.59 us -> 116 us  [the longest x81 108 us: send_xor(): return lax.ppermute(block, ('section', 'tp'), route)]
    dot_general x29 -> x0, matrix products: 60 us -> none  [the longest x6 20.8 us: out_fold(): return jnp.dot(segment, weight, preferred_element_type=jnp.float32)]
    pallas_call x0 -> x15, Pallas kernels: none -> 21 us  [the longest x4 7.73 us: out_part(): pl.pallas_call(functools.partial(out_kernel, section, gated), out_shape=j...]
    dot_general x2 -> x0, local copies, waits for them, and re-layouts: 12.8 us -> none  [the longest x1 6.43 us: body(): jnp.dot(normed, self_q[0], preferred_element_type=jnp.float32)]
  transfers between devices with their start and end apart: 13 -> 92, of which waited for: 13 -> 53; matrix products, arithmetic and copies ran while one was open for 2% -> 3% of each run, Pallas kernels for 0% -> 4%
where the time goes in v2:
time: 276 us
  waiting for transfers between devices  120 us (43%)
  starting transfers between devices  116 us (42%)
  Pallas kernels  21 us (8%)
  local copies, waits for them, and re-layouts  7.81 us (3%)
  other arithmetic  4.83 us (2%)
  blocking collectives  3.97 us (1%)
    ppermute x81, waiting for transfers between devices, send_xor(): return lax.ppermute(block, ('section', 'tp'), route)  116 us
    ppermute x81, starting transfers between devices, send_xor(): return lax.ppermute(block, ('section', 'tp'), route)  108 us
    ppermute x11, starting transfers between devices, swap_cores(): return lax.ppermute(block, 'section', [(0, 1), (1, 0)])  8.77 us
    pallas_call x4, Pallas kernels, out_part(): pl.pallas_call(functools.partial(out_kernel, section, gated), out_shape=j...  7.73 us
    unnamed x31, local copies, waits for them, and re-layouts  5.91 us
  transfers between devices with their start and end apart: 92, of which 53 were waited for; matrix products, arithmetic and copies ran while one was open for 3% of the time, Pallas kernels for 4%

profile of v2, /device:TPU:0, one launch (start us, length us, event | category | flops | bytes accessed | tf_op | source)
XLA Modules:
  0.0 275.8 jit_solution(15227773757050960049)
XLA Ops:
  3.3 4.0 %all-gather.1 = f32[2,4,512]{2,1,0:T(4,128)S(1)} all-gather(f32[1,4,512]{2,1,0:T(4,128)S(1)} %fusion.17), channel_id=2, replica_groups=mesh['section'=2,'tp'=16] {'section'}, dimensions={0}, use_global_device_ids=true | all-gather | bytes 24576 | tf_op jit(solution)/shard_map/all_gather | solution.py:631
  7.5 5.0 %collective-permute-start.2 = (bf16[80,512]{1,0:T(8,128)(2,1)S(1)}, bf16[80,512]{1,0:T(8,128)(2,1)S(1)}, u32[]{:S(2)}, u32[]{:S(2)}) collective-permute-start(bf16[80,512]{1,0:T(8,128)(2,1)S(1)} %get-tuple-element.53), channel_id=1, source_target_pairs={{0,12},{1,13},{2,14},{3,15},{4,8},{5,9},{6,10},{7,11},{8,4},{9,5},... | collective-permute-start | bytes 245768 | tf_op jit(solution)/shard_map/ppermute | solution.py:212
  26.4 3.7 %collective-permute-start.8 = (bf16[32,1280]{1,0:T(8,128)(2,1)S(1)}, bf16[32,1280]{1,0:T(8,128)(2,1)S(1)}, u32[]{:S(2)}, u32[]{:S(2)}) collective-permute-start(bf16[32,1280]{1,0:T(8,128)(2,1)S(1)} %fusion.2), channel_id=1, source_target_pairs={{0,12},{1,13},{2,14},{3,15},{4,8},{5,9},{6,10},{7,11},{8,4},{9,5},... | collective-permute-start | bytes 245768 | tf_op jit(solution)/shard_map/ppermute | solution.py:212
  30.1 2.7 collective-permute-done.8
  48.8 3.5 %collective-permute-done.14.p3 = bf16[32,1280]{1,0:T(8,128)(2,1)S(1)} collective-permute-done((bf16[32,1280]{1,0:T(8,128)(2,1)S(1)}, bf16[32,1280]{1,0:T(8,128)(2,1)S(1)}, u32[]{:S(2)}, u32[]{:S(2)}) %collective-permute-start.14) | collective-permute-done | bytes 81952 | tf_op jit(solution)/shard_map/ppermute | solution.py:212
  53.8 2.9 %collective-permute-done.13.p2 = bf16[32,1280]{1,0:T(8,128)(2,1)S(1)} collective-permute-done((bf16[32,1280]{1,0:T(8,128)(2,1)S(1)}, bf16[32,1280]{1,0:T(8,128)(2,1)S(1)}, u32[]{:S(2)}, u32[]{:S(2)}) %collective-permute-start.13) | collective-permute-done | bytes 81952 | tf_op jit(solution)/shard_map/ppermute | solution.py:212
  56.7 3.0 %collective-permute-start.52 = (bf16[4096,512]{1,0:T(8,128)(2,1)}, bf16[4096,512]{1,0:T(8,128)(2,1)S(1)}, u32[]{:S(2)}, u32[]{:S(2)}) collective-permute-start(bf16[4096,512]{1,0:T(8,128)(2,1)} %bitcast.120), channel_id=1, source_target_pairs={{0,16},{16,0},{1,17},{17,1},{2,18},{18,2},{3,19},{19,3},{4,20},{20... | collective-permute-start | bytes 12582920 | tf_op jit(solution)/shard_map/ppermute | solution.py:202
  63.8 3.3 %shard_map.191.q_ref = f32[64,256]{1,0:T(8,128)S(1)} custom-call(bf16[4,80,512]{2,1,0:T(8,128)(2,1)S(1)} %pad_maximum_fusion.refs_0_, bf16[4,80,512]{2,1,0:T(8,128)(2,1)} %collective-permute-done.9.refs_1_, bf16[4,80,512]{2,1,0:T(8,128)(2,1)S(1)} %collective-permute-done.10.refs_2_, bf16[4,80,512]{2,1,0:T(8,128)(2,1)S(1)} %collective-permute-done.11.refs_3_, ...), custom_call_target="tpu_custom_call" | custom-call | tf_op jit(solution)/shard_map/pallas_call | solution.py:377
  88.0 3.2 %collective-permute-done.22 = bf16[128,256]{1,0:T(8,128)(2,1)S(1)} collective-permute-done((bf16[128,256]{1,0:T(8,128)(2,1)S(1)}, bf16[128,256]{1,0:T(8,128)(2,1)S(1)}, u32[]{:S(2)}, u32[]{:S(2)}) %collective-permute-start.22) | collective-permute-done | bytes 65568 | tf_op jit(solution)/shard_map/ppermute | solution.py:212
  91.9 3.6 %collective-permute-done.20 = bf16[128,256]{1,0:T(8,128)(2,1)S(1)} collective-permute-done((bf16[128,256]{1,0:T(8,128)(2,1)S(1)}, bf16[128,256]{1,0:T(8,128)(2,1)S(1)}, u32[]{:S(2)}, u32[]{:S(2)}) %collective-permute-start.20) | collective-permute-done | bytes 65568 | tf_op jit(solution)/shard_map/ppermute | solution.py:212
  100.0 3.4 %collective-permute-done.26 = bf16[64,256]{1,0:T(8,128)(2,1)S(1)} collective-permute-done((bf16[64,256]{1,0:T(8,128)(2,1)S(1)}, bf16[64,256]{1,0:T(8,128)(2,1)S(1)}, u32[]{:S(2)}, u32[]{:S(2)}) %collective-permute-start.26) | collective-permute-done | bytes 32800 | tf_op jit(solution)/shard_map/ppermute | solution.py:212
  103.4 4.8 %collective-permute-done.25 = bf16[64,256]{1,0:T(8,128)(2,1)S(1)} collective-permute-done((bf16[64,256]{1,0:T(8,128)(2,1)S(1)}, bf16[64,256]{1,0:T(8,128)(2,1)S(1)}, u32[]{:S(2)}, u32[]{:S(2)}) %collective-permute-start.25) | collective-permute-done | bytes 32800 | tf_op jit(solution)/shard_map/ppermute | solution.py:212
  108.2 4.7 %collective-permute-done.24 = bf16[64,256]{1,0:T(8,128)(2,1)S(1)} collective-permute-done((bf16[64,256]{1,0:T(8,128)(2,1)S(1)}, bf16[64,256]{1,0:T(8,128)(2,1)S(1)}, u32[]{:S(2)}, u32[]{:S(2)}) %collective-permute-start.24) | collective-permute-done | bytes 32800 | tf_op jit(solution)/shard_map/ppermute | solution.py:212
  113.0 2.7 collective-permute-start.29
  115.7 3.2 %collective-permute-done.29.refs_3_ = bf16[4,64,256]{2,1,0:T(8,128)(2,1)S(1)} collective-permute-done((bf16[4,64,256]{2,1,0:T(8,128)(2,1)S(1)}, bf16[4,64,256]{2,1,0:T(8,128)(2,1)S(1)}, u32[]{:S(2)}, u32[]{:S(2)}) %collective-permute-start.29) | collective-permute-done | bytes 131104 | tf_op jit(solution)/shard_map/ppermute | solution.py:212
  120.7 3.2 %collective-permute-done.27.refs_1_ = bf16[4,64,256]{2,1,0:T(8,128)(2,1)S(1)} collective-permute-done((bf16[4,64,256]{2,1,0:T(8,128)(2,1)S(1)}, bf16[4,64,256]{2,1,0:T(8,128)(2,1)S(1)}, u32[]{:S(2)}, u32[]{:S(2)}) %collective-permute-start.27) | collective-permute-done | bytes 131104 | tf_op jit(solution)/shard_map/ppermute | solution.py:212
  123.9 3.0 %shard_map.194.hidden_ref.refs_4_ = bf16[64,512]{1,0:T(8,128)(2,1)S(1)} custom-call(bf16[4,64,256]{2,1,0:T(8,128)(2,1)S(1)} %pad_maximum_fusion.5.refs_0_, bf16[4,64,256]{2,1,0:T(8,128)(2,1)S(1)} %collective-permute-done.27.refs_1_, bf16[4,64,256]{2,1,0:T(8,128)(2,1)S(1)} %collective-permute-done.28.refs_2_, ...), custom_call_target="tpu_custom_call" | custom-call | tf_op jit(solution)/shard_map/pallas_call | solution.py:509
  127.6 3.1 %collective-permute-start.41 = (bf16[80,256]{1,0:T(8,128)(2,1)S(1)}, bf16[80,256]{1,0:T(8,128)(2,1)S(1)}, u32[]{:S(2)}, u32[]{:S(2)}) collective-permute-start(bf16[80,256]{1,0:T(8,128)(2,1)S(1)} %get-tuple-element.50), channel_id=1, source_target_pairs={{0,12},{1,13},{2,14},{3,15},{4,8},{5,9},{6,10},{7,11},{8,4},{9,5},... | collective-permute-start | bytes 122888 | tf_op jit(solution)/shard_map/ppermute | solution.py:212
  131.5 3.0 %collective-permute-start.33 = (bf16[64,512]{1,0:T(8,128)(2,1)S(1)}, bf16[64,512]{1,0:T(8,128)(2,1)S(1)}, u32[]{:S(2)}, u32[]{:S(2)}) collective-permute-start(bf16[64,512]{1,0:T(8,128)(2,1)S(1)} %shard_map.194.hidden_ref.refs_4_), channel_id=1, source_target_pairs={{0,12},{1,13},{2,14},{3,15},{4,8},{5,9},{6,10},{7,11},{8,4},{9,5},... | collective-permute-start | bytes 196616 | tf_op jit(solution)/shard_map/ppermute | solution.py:212
  138.4 2.8 %collective-permute-start.44 = (bf16[80,256]{1,0:T(8,128)(2,1)S(1)}, bf16[80,256]{1,0:T(8,128)(2,1)S(1)}, u32[]{:S(2)}, u32[]{:S(2)}) collective-permute-start(bf16[80,256]{1,0:T(8,128)(2,1)S(1)} %fusion.15), channel_id=1, source_target_pairs={{0,3},{1,2},{2,1},{3,0},{4,7},{5,6},{6,5},{7,4},{8,11},{9,10},{10,... | collective-permute-start | bytes 122888 | tf_op jit(solution)/shard_map/ppermute | solution.py:212
  141.2 5.0 %collective-permute-done.32 = bf16[64,512]{1,0:T(8,128)(2,1)S(1)} collective-permute-done((bf16[64,512]{1,0:T(8,128)(2,1)S(1)}, bf16[64,512]{1,0:T(8,128)(2,1)S(1)}, u32[]{:S(2)}, u32[]{:S(2)}) %collective-permute-start.32) | collective-permute-done | bytes 65568 | tf_op jit(solution)/shard_map/ppermute | solution.py:212
  152.9 3.4 %collective-permute-done.36.refs_3_ = bf16[4,64,512]{2,1,0:T(8,128)(2,1)S(1)} collective-permute-done((bf16[4,64,512]{2,1,0:T(8,128)(2,1)S(1)}, bf16[4,64,512]{2,1,0:T(8,128)(2,1)S(1)}, u32[]{:S(2)}, u32[]{:S(2)}) %collective-permute-start.36) | collective-permute-done | bytes 262176 | tf_op jit(solution)/shard_map/ppermute | solution.py:212
  156.3 3.4 %collective-permute-done.35.refs_2_ = bf16[4,64,512]{2,1,0:T(8,128)(2,1)S(1)} collective-permute-done((bf16[4,64,512]{2,1,0:T(8,128)(2,1)S(1)}, bf16[4,64,512]{2,1,0:T(8,128)(2,1)S(1)}, u32[]{:S(2)}, u32[]{:S(2)}) %collective-permute-start.35) | collective-permute-done | bytes 262176 | tf_op jit(solution)/shard_map/ppermute | solution.py:212
  175.1 3.5 %collective-permute-done.51.refs_3_ = bf16[4,64,256]{2,1,0:T(8,128)(2,1)S(1)} collective-permute-done((bf16[4,64,256]{2,1,0:T(8,128)(2,1)S(1)}, bf16[4,64,256]{2,1,0:T(8,128)(2,1)S(1)}, u32[]{:S(2)}, u32[]{:S(2)}) %collective-permute-start.51) | collective-permute-done | bytes 131104 | tf_op jit(solution)/shard_map/ppermute | solution.py:212
  187.7 5.8 %collective-permute-done.54 = bf16[64,512]{1,0:T(8,128)(2,1)S(1)} collective-permute-done((bf16[64,512]{1,0:T(8,128)(2,1)S(1)}, bf16[64,512]{1,0:T(8,128)(2,1)S(1)}, u32[]{:S(2)}, u32[]{:S(2)}) %collective-permute-start.54) | collective-permute-done | bytes 65568 | tf_op jit(solution)/shard_map/ppermute | solution.py:212
  201.0 2.7 collective-permute-done.57.refs_2_
  203.7 3.6 %shard_map.199 = bf16[64,256]{1,0:T(8,128)(2,1)S(1)} custom-call(bf16[4,64,512]{2,1,0:T(8,128)(2,1)S(1)} %pad_maximum_fusion.3.refs_0_, bf16[4,64,512]{2,1,0:T(8,128)(2,1)S(1)} %collective-permute-done.56.refs_1_, bf16[4,64,512]{2,1,0:T(8,128)(2,1)S(1)} %collective-permute-done.57.refs_2_, bf16[4,64,512]{2,1,0:T(8,128)(2,1)S(1)} %collective-permute-done.58.refs_3_, ...), custom_call_target="tpu_custom_call" | custom-call | tf_op jit(solution)/shard_map/pallas_call | solution.py:345
  209.1 2.7 collective-permute-start.66
  223.5 3.0 %shard_map.200.hidden_ref.refs_4_ = bf16[64,512]{1,0:T(8,128)(2,1)S(1)} custom-call(bf16[4,64,256]{2,1,0:T(8,128)(2,1)S(1)} %pad_maximum_fusion.7.refs_0_, bf16[4,64,256]{2,1,0:T(8,128)(2,1)S(1)} %collective-permute-done.69.refs_1_, bf16[4,64,256]{2,1,0:T(8,128)(2,1)S(1)} %collective-permute-done.70.refs_2_, ...), custom_call_target="tpu_custom_call" | custom-call | tf_op jit(solution)/shard_map/pallas_call | solution.py:509
  235.0 6.7 %collective-permute-done.79 = bf16[80,256]{1,0:T(8,128)(2,1)S(1)} collective-permute-done((bf16[80,256]{1,0:T(8,128)(2,1)S(1)}, bf16[80,256]{1,0:T(8,128)(2,1)S(1)}, u32[]{:S(2)}, u32[]{:S(2)}) %collective-permute-start.79) | collective-permute-done | bytes 40992 | tf_op jit(solution)/shard_map/ppermute | solution.py:212
  249.0 3.8 %collective-permute-done.77.refs_3_ = bf16[4,64,512]{2,1,0:T(8,128)(2,1)S(1)} collective-permute-done((bf16[4,64,512]{2,1,0:T(8,128)(2,1)S(1)}, bf16[4,64,512]{2,1,0:T(8,128)(2,1)S(1)}, u32[]{:S(2)}, u32[]{:S(2)}) %collective-permute-start.77) | collective-permute-done | bytes 262176 | tf_op jit(solution)/shard_map/ppermute | solution.py:212
  252.8 3.4 %collective-permute-done.76.refs_2_ = bf16[4,64,512]{2,1,0:T(8,128)(2,1)S(1)} collective-permute-done((bf16[4,64,512]{2,1,0:T(8,128)(2,1)S(1)}, bf16[4,64,512]{2,1,0:T(8,128)(2,1)S(1)}, u32[]{:S(2)}, u32[]{:S(2)}) %collective-permute-start.76) | collective-permute-done | bytes 262176 | tf_op jit(solution)/shard_map/ppermute | solution.py:212
  (251 shorter events, 158.1 us)
Async XLA Ops:
  0.0 60.6 %collective-permute-start.15 = (bf16[8192,256]{1,0:T(8,128)(2,1)}, bf16[8192,256]{1,0:T(8,128)(2,1)}, u32[]{:S(2)}, u32[]{:S(2)}) collective-permute-start(bf16[8192,256]{1,0:T(8,128)(2,1)} %bitcast.114), channel_id=1, source_target_pairs={{0,16},{16,0},{1,17},{17,1},{2,18},{18,2},{3,19},{19,3},{4,20},{20... | collective-permute-start | bytes 12582920 | tf_op jit(solution)/shard_map/ppermute | solution.py:202
  7.5 10.9 %collective-permute-start.2 = (bf16[80,512]{1,0:T(8,128)(2,1)S(1)}, bf16[80,512]{1,0:T(8,128)(2,1)S(1)}, u32[]{:S(2)}, u32[]{:S(2)}) collective-permute-start(bf16[80,512]{1,0:T(8,128)(2,1)S(1)} %get-tuple-element.53), channel_id=1, source_target_pairs={{0,12},{1,13},{2,14},{3,15},{4,8},{5,9},{6,10},{7,11},{8,4},{9,5},... | collective-permute-start | bytes 245768 | tf_op jit(solution)/shard_map/ppermute | solution.py:212
  13.1 102.6 %collective-permute-start.30 = (bf16[4096,512]{1,0:T(8,128)(2,1)}, bf16[4096,512]{1,0:T(8,128)(2,1)}, u32[]{:S(2)}, u32[]{:S(2)}) collective-permute-start(bf16[4096,512]{1,0:T(8,128)(2,1)} %bitcast.117), channel_id=1, source_target_pairs={{0,16},{16,0},{1,17},{17,1},{2,18},{18,2},{3,19},{19,3},{4,20},{20... | collective-permute-start | bytes 12582920 | tf_op jit(solution)/shard_map/ppermute | solution.py:202
  23.0 16.2 %collective-permute-start.11 = (bf16[4,80,512]{2,1,0:T(8,128)(2,1)S(1)}, bf16[4,80,512]{2,1,0:T(8,128)(2,1)S(1)}, u32[]{:S(2)}, u32[]{:S(2)}) collective-permute-start(bf16[4,80,512]{2,1,0:T(8,128)(2,1)S(1)} %pad_maximum_fusion.refs_0_), channel_id=1, source_target_pairs={{0,3},{1,2},{2,1},{3,0},{4,7},{5,6},{6,5},{7,4},{8,11},{9,10},{10,... | collective-permute-start | bytes 983048 | tf_op jit(solution)/shard_map/ppermute | solution.py:212
  37.7 8.2 %collective-permute-start.9 = (bf16[4,80,512]{2,1,0:T(8,128)(2,1)S(1)}, bf16[4,80,512]{2,1,0:T(8,128)(2,1)}, u32[]{:S(2)}, u32[]{:S(2)}) collective-permute-start(bf16[4,80,512]{2,1,0:T(8,128)(2,1)S(1)} %pad_maximum_fusion.refs_0_), channel_id=1, source_target_pairs={{0,1},{1,0},{2,3},{3,2},{4,5},{5,4},{6,7},{7,6},{8,9},{9,8},{10,11... | collective-permute-start | bytes 983048 | tf_op jit(solution)/shard_map/ppermute | solution.py:212
  39.2 28.0 %collective-permute-start.16 = (bf16[512,1024]{1,0:T(8,128)(2,1)S(1)}, bf16[512,1024]{1,0:T(8,128)(2,1)S(1)}, u32[]{:S(2)}, u32[]{:S(2)}) collective-permute-start(bf16[512,1024]{1,0:T(8,128)(2,1)S(1)} %bitcast.128), channel_id=1, source_target_pairs={{0,16},{16,0},{1,17},{17,1},{2,18},{18,2},{3,19},{19,3},{4,20},{20... | collective-permute-start | bytes 3145736 | tf_op jit(solution)/shard_map/ppermute | solution.py:202
  43.4 109.4 %collective-permute-start.37 = (bf16[8192,256]{1,0:T(8,128)(2,1)}, bf16[8192,256]{1,0:T(8,128)(2,1)S(1)}, u32[]{:S(2)}, u32[]{:S(2)}) collective-permute-start(bf16[8192,256]{1,0:T(8,128)(2,1)} %bitcast.111), channel_id=1, source_target_pairs={{0,16},{16,0},{1,17},{17,1},{2,18},{18,2},{3,19},{19,3},{4,20},{20... | collective-permute-start | bytes 12582920 | tf_op jit(solution)/shard_map/ppermute | solution.py:202
  56.7 118.4 %collective-permute-start.52 = (bf16[4096,512]{1,0:T(8,128)(2,1)}, bf16[4096,512]{1,0:T(8,128)(2,1)S(1)}, u32[]{:S(2)}, u32[]{:S(2)}) collective-permute-start(bf16[4096,512]{1,0:T(8,128)(2,1)} %bitcast.120), channel_id=1, source_target_pairs={{0,16},{16,0},{1,17},{17,1},{2,18},{18,2},{3,19},{19,3},{4,20},{20... | collective-permute-start | bytes 12582920 | tf_op jit(solution)/shard_map/ppermute | solution.py:202
  91.9 35.1 %collective-permute-start.38 = (bf16[512,1024]{1,0:T(8,128)(2,1)S(1)}, bf16[512,1024]{1,0:T(8,128)(2,1)S(1)}, u32[]{:S(2)}, u32[]{:S(2)}) collective-permute-start(bf16[512,1024]{1,0:T(8,128)(2,1)S(1)} %bitcast.123), channel_id=1, source_target_pairs={{0,16},{16,0},{1,17},{17,1},{2,18},{18,2},{3,19},{19,3},{4,20},{20... | collective-permute-start | bytes 3145736 | tf_op jit(solution)/shard_map/ppermute | solution.py:202
  134.6 11.6 %collective-permute-start.32 = (bf16[64,512]{1,0:T(8,128)(2,1)S(1)}, bf16[64,512]{1,0:T(8,128)(2,1)S(1)}, u32[]{:S(2)}, u32[]{:S(2)}) collective-permute-start(bf16[64,512]{1,0:T(8,128)(2,1)S(1)} %shard_map.194.hidden_ref.refs_4_), channel_id=1, source_target_pairs={{0,8},{1,9},{2,10},{3,11},{4,12},{5,13},{6,14},{7,15},{8,0},{9,1},... | collective-permute-start | bytes 196616 | tf_op jit(solution)/shard_map/ppermute | solution.py:212
  136.3 11.8 %collective-permute-start.31 = (bf16[64,512]{1,0:T(8,128)(2,1)S(1)}, bf16[64,512]{1,0:T(8,128)(2,1)S(1)}, u32[]{:S(2)}, u32[]{:S(2)}) collective-permute-start(bf16[64,512]{1,0:T(8,128)(2,1)S(1)} %shard_map.194.hidden_ref.refs_4_), channel_id=1, source_target_pairs={{0,4},{1,5},{2,6},{3,7},{4,0},{5,1},{6,2},{7,3},{8,12},{9,13},{10,... | collective-permute-start | bytes 196616 | tf_op jit(solution)/shard_map/ppermute | solution.py:212
  138.4 10.5 %collective-permute-start.44 = (bf16[80,256]{1,0:T(8,128)(2,1)S(1)}, bf16[80,256]{1,0:T(8,128)(2,1)S(1)}, u32[]{:S(2)}, u32[]{:S(2)}) collective-permute-start(bf16[80,256]{1,0:T(8,128)(2,1)S(1)} %fusion.15), channel_id=1, source_target_pairs={{0,3},{1,2},{2,1},{3,0},{4,7},{5,6},{6,5},{7,4},{8,11},{9,10},{10,... | collective-permute-start | bytes 122888 | tf_op jit(solution)/shard_map/ppermute | solution.py:212
  148.9 7.4 %collective-permute-start.36 = (bf16[4,64,512]{2,1,0:T(8,128)(2,1)S(1)}, bf16[4,64,512]{2,1,0:T(8,128)(2,1)S(1)}, u32[]{:S(2)}, u32[]{:S(2)}) collective-permute-start(bf16[4,64,512]{2,1,0:T(8,128)(2,1)S(1)} %pad_maximum_fusion.2.refs_0_), channel_id=1, source_target_pairs={{0,3},{1,2},{2,1},{3,0},{4,7},{5,6},{6,5},{7,4},{8,11},{9,10},{10,... | collective-permute-start | bytes 786440 | tf_op jit(solution)/shard_map/ppermute | solution.py:212
  150.2 9.5 %collective-permute-start.35 = (bf16[4,64,512]{2,1,0:T(8,128)(2,1)S(1)}, bf16[4,64,512]{2,1,0:T(8,128)(2,1)S(1)}, u32[]{:S(2)}, u32[]{:S(2)}) collective-permute-start(bf16[4,64,512]{2,1,0:T(8,128)(2,1)S(1)} %pad_maximum_fusion.2.refs_0_), channel_id=1, source_target_pairs={{0,2},{1,3},{2,0},{3,1},{4,6},{5,7},{6,4},{7,5},{8,10},{9,11},{10,... | collective-permute-start | bytes 786440 | tf_op jit(solution)/shard_map/ppermute | solution.py:212
  152.1 7.6 %collective-permute-start.34 = (bf16[4,64,512]{2,1,0:T(8,128)(2,1)S(1)}, bf16[4,64,512]{2,1,0:T(8,128)(2,1)S(1)}, u32[]{:S(2)}, u32[]{:S(2)}) collective-permute-start(bf16[4,64,512]{2,1,0:T(8,128)(2,1)S(1)} %pad_maximum_fusion.2.refs_0_), channel_id=1, source_target_pairs={{0,1},{1,0},{2,3},{3,2},{4,5},{5,4},{6,7},{7,6},{8,9},{9,8},{10,11... | collective-permute-start | bytes 786440 | tf_op jit(solution)/shard_map/ppermute | solution.py:212
  152.9 7.9 %collective-permute-start.45 = (bf16[80,256]{1,0:T(8,128)(2,1)S(1)}, bf16[80,256]{1,0:T(8,128)(2,1)S(1)}, u32[]{:S(2)}, u32[]{:S(2)}) collective-permute-start(bf16[80,256]{1,0:T(8,128)(2,1)S(1)} %add_convert_fusion.1.near_ref), channel_id=1, source_target_pairs={{0,16},{16,0},{1,17},{17,1},{2,18},{18,2},{3,19},{19,3},{4,20},{20... | collective-permute-start | bytes 122888 | tf_op jit(solution)/shard_map/ppermute | solution.py:202
  165.8 7.3 %collective-permute-start.64 = (bf16[128,256]{1,0:T(8,128)(2,1)S(1)}, bf16[128,256]{1,0:T(8,128)(2,1)S(1)}, u32[]{:S(2)}, u32[]{:S(2)}) collective-permute-start(bf16[128,256]{1,0:T(8,128)(2,1)S(1)} %get-tuple-element.35), channel_id=1, source_target_pairs={{0,3},{1,2},{2,1},{3,0},{4,7},{5,6},{6,5},{7,4},{8,11},{9,10},{10,... | collective-permute-start | bytes 196616 | tf_op jit(solution)/shard_map/ppermute | solution.py:212
  171.3 7.2 %collective-permute-start.51 = (bf16[4,64,256]{2,1,0:T(8,128)(2,1)S(1)}, bf16[4,64,256]{2,1,0:T(8,128)(2,1)S(1)}, u32[]{:S(2)}, u32[]{:S(2)}) collective-permute-start(bf16[4,64,256]{2,1,0:T(8,128)(2,1)S(1)} %pad_maximum_fusion.6.refs_0_), channel_id=1, source_target_pairs={{0,3},{1,2},{2,1},{3,0},{4,7},{5,6},{6,5},{7,4},{8,11},{9,10},{10,... | collective-permute-start | bytes 393224 | tf_op jit(solution)/shard_map/ppermute | solution.py:212
  182.6 10.9 %collective-permute-start.54 = (bf16[64,512]{1,0:T(8,128)(2,1)S(1)}, bf16[64,512]{1,0:T(8,128)(2,1)S(1)}, u32[]{:S(2)}, u32[]{:S(2)}) collective-permute-start(bf16[64,512]{1,0:T(8,128)(2,1)S(1)} %shard_map.198.refs_4_), channel_id=1, source_target_pairs={{0,8},{1,9},{2,10},{3,11},{4,12},{5,13},{6,14},{7,15},{8,0},{9,1},... | collective-permute-start | bytes 196616 | tf_op jit(solution)/shard_map/ppermute | solution.py:212
  182.6 10.9 %collective-permute-start.53 = (bf16[64,512]{1,0:T(8,128)(2,1)S(1)}, bf16[64,512]{1,0:T(8,128)(2,1)S(1)}, u32[]{:S(2)}, u32[]{:S(2)}) collective-permute-start(bf16[64,512]{1,0:T(8,128)(2,1)S(1)} %shard_map.198.refs_4_), channel_id=1, source_target_pairs={{0,4},{1,5},{2,6},{3,7},{4,0},{5,1},{6,2},{7,3},{8,12},{9,13},{10,... | collective-permute-start | bytes 196616 | tf_op jit(solution)/shard_map/ppermute | solution.py:212
  193.6 7.4 %collective-permute-start.58 = (bf16[4,64,512]{2,1,0:T(8,128)(2,1)S(1)}, bf16[4,64,512]{2,1,0:T(8,128)(2,1)S(1)}, u32[]{:S(2)}, u32[]{:S(2)}) collective-permute-start(bf16[4,64,512]{2,1,0:T(8,128)(2,1)S(1)} %pad_maximum_fusion.3.refs_0_), channel_id=1, source_target_pairs={{0,3},{1,2},{2,1},{3,0},{4,7},{5,6},{6,5},{7,4},{8,11},{9,10},{10,... | collective-permute-start | bytes 786440 | tf_op jit(solution)/shard_map/ppermute | solution.py:212
  194.9 8.8 %collective-permute-start.57 = (bf16[4,64,512]{2,1,0:T(8,128)(2,1)S(1)}, bf16[4,64,512]{2,1,0:T(8,128)(2,1)S(1)}, u32[]{:S(2)}, u32[]{:S(2)}) collective-permute-start(bf16[4,64,512]{2,1,0:T(8,128)(2,1)S(1)} %pad_maximum_fusion.3.refs_0_), channel_id=1, source_target_pairs={{0,2},{1,3},{2,0},{3,1},{4,6},{5,7},{6,4},{7,5},{8,10},{9,11},{10,... | collective-permute-start | bytes 786440 | tf_op jit(solution)/shard_map/ppermute | solution.py:212
  196.1 7.7 %collective-permute-start.56 = (bf16[4,64,512]{2,1,0:T(8,128)(2,1)S(1)}, bf16[4,64,512]{2,1,0:T(8,128)(2,1)S(1)}, u32[]{:S(2)}, u32[]{:S(2)}) collective-permute-start(bf16[4,64,512]{2,1,0:T(8,128)(2,1)S(1)} %pad_maximum_fusion.3.refs_0_), channel_id=1, source_target_pairs={{0,1},{1,0},{2,3},{3,2},{4,5},{5,4},{6,7},{7,6},{8,9},{9,8},{10,11... | collective-permute-start | bytes 786440 | tf_op jit(solution)/shard_map/ppermute | solution.py:212
  227.2 7.8 %collective-permute-start.80 = (bf16[80,256]{1,0:T(8,128)(2,1)S(1)}, bf16[80,256]{1,0:T(8,128)(2,1)S(1)}, u32[]{:S(2)}, u32[]{:S(2)}) collective-permute-start(bf16[80,256]{1,0:T(8,128)(2,1)S(1)} %get-tuple-element.47), channel_id=1, source_target_pairs={{0,12},{1,13},{2,14},{3,15},{4,8},{5,9},{6,10},{7,11},{8,4},{9,5},... | collective-permute-start | bytes 122888 | tf_op jit(solution)/shard_map/ppermute | solution.py:212
  228.9 12.8 %collective-permute-start.79 = (bf16[80,256]{1,0:T(8,128)(2,1)S(1)}, bf16[80,256]{1,0:T(8,128)(2,1)S(1)}, u32[]{:S(2)}, u32[]{:S(2)}) collective-permute-start(bf16[80,256]{1,0:T(8,128)(2,1)S(1)} %get-tuple-element.48), channel_id=1, source_target_pairs={{0,8},{1,9},{2,10},{3,11},{4,12},{5,13},{6,14},{7,15},{8,0},{9,1},... | collective-permute-start | bytes 122888 | tf_op jit(solution)/shard_map/ppermute | solution.py:212
  230.6 13.7 %collective-permute-start.74 = (bf16[64,512]{1,0:T(8,128)(2,1)S(1)}, bf16[64,512]{1,0:T(8,128)(2,1)S(1)}, u32[]{:S(2)}, u32[]{:S(2)}) collective-permute-start(bf16[64,512]{1,0:T(8,128)(2,1)S(1)} %shard_map.200.hidden_ref.refs_4_), channel_id=1, source_target_pairs={{0,12},{1,13},{2,14},{3,15},{4,8},{5,9},{6,10},{7,11},{8,4},{9,5},... | collective-permute-start | bytes 196616 | tf_op jit(solution)/shard_map/ppermute | solution.py:212
  232.3 13.0 %collective-permute-start.73 = (bf16[64,512]{1,0:T(8,128)(2,1)S(1)}, bf16[64,512]{1,0:T(8,128)(2,1)S(1)}, u32[]{:S(2)}, u32[]{:S(2)}) collective-permute-start(bf16[64,512]{1,0:T(8,128)(2,1)S(1)} %shard_map.200.hidden_ref.refs_4_), channel_id=1, source_target_pairs={{0,8},{1,9},{2,10},{3,11},{4,12},{5,13},{6,14},{7,15},{8,0},{9,1},... | collective-permute-start | bytes 196616 | tf_op jit(solution)/shard_map/ppermute | solution.py:212
  233.1 12.2 %collective-permute-start.72 = (bf16[64,512]{1,0:T(8,128)(2,1)S(1)}, bf16[64,512]{1,0:T(8,128)(2,1)S(1)}, u32[]{:S(2)}, u32[]{:S(2)}) collective-permute-start(bf16[64,512]{1,0:T(8,128)(2,1)S(1)} %shard_map.200.hidden_ref.refs_4_), channel_id=1, source_target_pairs={{0,4},{1,5},{2,6},{3,7},{4,0},{5,1},{6,2},{7,3},{8,12},{9,13},{10,... | collective-permute-start | bytes 196616 | tf_op jit(solution)/shard_map/ppermute | solution.py:212
  245.4 7.4 %collective-permute-start.77 = (bf16[4,64,512]{2,1,0:T(8,128)(2,1)S(1)}, bf16[4,64,512]{2,1,0:T(8,128)(2,1)S(1)}, u32[]{:S(2)}, u32[]{:S(2)}) collective-permute-start(bf16[4,64,512]{2,1,0:T(8,128)(2,1)S(1)} %pad_maximum_fusion.4.refs_0_), channel_id=1, source_target_pairs={{0,3},{1,2},{2,1},{3,0},{4,7},{5,6},{6,5},{7,4},{8,11},{9,10},{10,... | collective-permute-start | bytes 786440 | tf_op jit(solution)/shard_map/ppermute | solution.py:212
  246.8 9.4 %collective-permute-start.76 = (bf16[4,64,512]{2,1,0:T(8,128)(2,1)S(1)}, bf16[4,64,512]{2,1,0:T(8,128)(2,1)S(1)}, u32[]{:S(2)}, u32[]{:S(2)}) collective-permute-start(bf16[4,64,512]{2,1,0:T(8,128)(2,1)S(1)} %pad_maximum_fusion.4.refs_0_), channel_id=1, source_target_pairs={{0,2},{1,3},{2,0},{3,1},{4,6},{5,7},{6,4},{7,5},{8,10},{9,11},{10,... | collective-permute-start | bytes 786440 | tf_op jit(solution)/shard_map/ppermute | solution.py:212
  247.9 8.3 %collective-permute-start.75 = (bf16[4,64,512]{2,1,0:T(8,128)(2,1)S(1)}, bf16[4,64,512]{2,1,0:T(8,128)(2,1)S(1)}, u32[]{:S(2)}, u32[]{:S(2)}) collective-permute-start(bf16[4,64,512]{2,1,0:T(8,128)(2,1)S(1)} %pad_maximum_fusion.4.refs_0_), channel_id=1, source_target_pairs={{0,1},{1,0},{2,3},{3,2},{4,5},{5,4},{6,7},{7,6},{8,9},{9,8},{10,11... | collective-permute-start | bytes 786440 | tf_op jit(solution)/shard_map/ppermute | solution.py:212
  248.9 8.3 %collective-permute-start.84 = (bf16[80,256]{1,0:T(8,128)(2,1)S(1)}, bf16[80,256]{1,0:T(8,128)(2,1)S(1)}, u32[]{:S(2)}, u32[]{:S(2)}) collective-permute-start(bf16[80,256]{1,0:T(8,128)(2,1)S(1)} %add_convert_fusion.near_ref), channel_id=1, source_target_pairs={{0,16},{16,0},{1,17},{17,1},{2,18},{18,2},{3,19},{19,3},{4,20},{20... | collective-permute-start | bytes 122888 | tf_op jit(solution)/shard_map/ppermute | solution.py:202
  (75 other events, 688.3 us)

commit v3 on v2

--- a/solution.py
+++ b/solution.py
@@ -186,12 +186,12 @@
     return outputs[None]
 
 
-VMEM_LIMIT = 8 * 1024 * 1024
+VMEM_LIMIT = 11 * 1024 * 1024
 GROUP = 4
 
 
-def params():
-    return pltpu.CompilerParams(vmem_limit_bytes=VMEM_LIMIT)
+def params(limit=VMEM_LIMIT):
+    return pltpu.CompilerParams(vmem_limit_bytes=limit)
 
 
 def in_vmem():
@@ -212,63 +212,97 @@
     return lax.ppermute(block, ("section", "tp"), route)
 
 
-def gather_chips(block):
-    first = jnp.stack(
-        [block] + [send_xor(block, (GROUP * k, k)) for k in range(1, GROUP)]
-    )
-    return [first] + [send_xor(first, (k, GROUP * k)) for k in range(1, GROUP)]
+def send_group(blocks, scale):
+    order = range(GROUP - 1, 0, -1)
+    sent = {k: send_xor(blocks[k], (scale[0] * k, scale[1] * k)) for k in order}
+    return [sent[k] for k in range(1, GROUP)]
+
+
+def gather_chips(block, beside_first=None, beside_second=None):
+    after = lax.optimization_barrier
+    come = send_group([block] * GROUP, (GROUP, 1))
+    extras = []
+    if beside_first is not None:
+        come, extra = after((come, beside_first()))
+        extras.append(extra)
+    first = jnp.stack([block] + come)
+    come = send_group([first] * GROUP, (1, GROUP))
+    if beside_second is not None:
+        come, extra = after((come, beside_second(extras[0])))
+        extras.append(extra)
+    return [first] + come, extras
 
 
 def total(parts):
     return sum((part.astype(jnp.float32) for part in parts[1:]), parts[0].astype(jnp.float32))
 
 
-def reduce_heads(blocks):
-    near = total(
-        [blocks[0]] + [send_xor(blocks[k], (GROUP * k, GROUP * k)) for k in range(1, GROUP)]
-    ).astype(jnp.bfloat16)
-    return total([near] + [send_xor(near, (k, k)) for k in range(1, GROUP)])
-
-
-def piece_chip(core, chip, outer, inner):
-    return jnp.where(core == 0, chip ^ (GROUP * inner) ^ outer, chip ^ inner ^ (GROUP * outer))
-
-
-def with_weight(section, own_ref, other_ref, run):
+def head_steps(blocks):
+    def fold(kept, come):
+        return (kept.astype(jnp.float32) + come.astype(jnp.float32)).astype(jnp.bfloat16)
+
+    return [
+        lambda: send_xor(blocks[2:], (2 * GROUP, 2 * GROUP)),
+        lambda come: fold(blocks[:2], come),
+        lambda rows: send_xor(rows[1], (GROUP, GROUP)),
+        lambda rows, come: fold(rows[0], come),
+        lambda rows: send_xor(rows, (1, 1)),
+        lambda rows, come: fold(rows, come),
+        lambda rows: send_xor(rows, (2, 2)),
+        lambda rows, come: rows.astype(jnp.float32) + come.astype(jnp.float32),
+    ]
+
+
+def gather_mask(core, at):
+    outer, inner = divmod(at, GROUP)
+    return outer ^ GROUP * inner if core == 0 else inner ^ GROUP * outer
+
+
+def text_mask(core, at):
+    outer, inner = divmod(at, GROUP)
+    return (outer if core == 0 else outer % 2 * 2 + outer // 2) ^ GROUP * inner
+
+
+def with_weight(section, own, other, run):
     core = lax.axis_index("section")
 
     @pl.when(core == section)
     def _():
-        run(own_ref)
+        run(section, *own)
 
     @pl.when(core != section)
     def _():
-        run(other_ref)
-
-
-def weight_rows(weight_ref, at, rows):
-    source = piece_chip(lax.axis_index("section"), lax.axis_index("tp"), at // GROUP, at % GROUP)
+        run(1 - section, *other)
+
+
+def weight_rows(weight_ref, mask, rows):
+    source = lax.axis_index("tp") ^ mask
     return weight_ref[pl.ds(pl.multiple_of(source * rows, rows), rows), :]
 
 
-def project(section, gain_at, rows, x_refs, gain_ref, own_ref, other_ref, product_ref):
+def project(section, gain_at, rows, x_refs, gain_refs, weight_refs, product_ref, mask_of=gather_mask):
     depth = x_refs[0].shape[2]
-
-    def run(weight_ref):
+    pieces = range(GROUP * GROUP)
+    gain_place = {text_mask(section, at): at for at in pieces}
+
+    def run(core, gain_ref, weight_ref):
         product = jnp.zeros(product_ref.shape, jnp.float32)
         squares = jnp.zeros((rows, depth), jnp.float32)
-        for at in range(GROUP * GROUP):
+        for at in pieces:
+            mask = mask_of(core, at)
             piece = x_refs[at // GROUP][at % GROUP, :rows, :].astype(jnp.float32)
             squares = squares + piece * piece
-            gain_row = gain_ref[at, gain_at : gain_at + 1, :].astype(jnp.float32)
+            gain_row = gain_ref[gain_place[mask], gain_at : gain_at + 1, :].astype(jnp.float32)
             scaled = (piece * gain_row).astype(jnp.bfloat16)
             product = product + jnp.dot(
-                scaled, weight_rows(weight_ref, at, depth), preferred_element_type=jnp.float32
+                scaled, weight_rows(weight_ref, mask, depth), preferred_element_type=jnp.float32
             )
         mean_square = jnp.sum(squares, axis=1, keepdims=True) / (GROUP * GROUP * depth)
         product_ref[...] = product * lax.rsqrt(mean_square + epsilon)
 
-    with_weight(section, own_ref, other_ref, run)
+    with_weight(
+        section, (gain_refs[0], weight_refs[0]), (gain_refs[1], weight_refs[1]), run
+    )
     return product_ref[...]
 
 
@@ -315,7 +349,7 @@
 def cross_attend(tile_rows, queries, near_ref, far_ref, tiles_ref, qk_ref, out_ref):
     core = lax.axis_index("section")
     rows = out_ref.shape[0]
-    queries = rms_norm(by_head(queries), qk_ref[2:3, :HD]).astype(jnp.bfloat16)
+    queries = rms_norm(by_head(queries), qk_ref[1:2, :HD]).astype(jnp.bfloat16)
     row_tiles = tiles_ref[pl.ds(pl.multiple_of(core * rows, rows), rows), :]
     row_tiles = jnp.concatenate([row_tiles] * (queries.shape[0] // rows), axis=0)
     count = near_ref.shape[0]
@@ -333,23 +367,23 @@
 
 def cross_kernel(section, gain_at, tile_rows, *refs):
     x_refs = refs[:GROUP]
-    (gain_ref, near_ref, far_ref, tiles_ref, qk_ref, own_ref, other_ref) = refs[GROUP : GROUP + 7]
-    out_ref, product_ref = refs[GROUP + 7 :]
+    gain_refs, weight_refs = refs[GROUP : GROUP + 2], refs[GROUP + 2 : GROUP + 4]
+    near_ref, far_ref, tiles_ref, qk_ref, out_ref, product_ref = refs[GROUP + 4 :]
     rows = out_ref.shape[0]
-    queries = project(section, gain_at, rows, x_refs, gain_ref, own_ref, other_ref, product_ref)
+    queries = project(section, gain_at, rows, x_refs, gain_refs, weight_refs, product_ref)
     cross_attend(tile_rows, queries, near_ref, far_ref, tiles_ref, qk_ref, out_ref)
 
 
-def cross_mix(section, gain_at, tile_rows, rows, pieces, gains, near, far, tiles, qk, own, other):
-    columns = own.shape[1]
+def cross_mix(section, gain_at, tile_rows, rows, pieces, gains, weights, near, far, tiles, qk):
+    columns = weights[0].shape[1]
     return pl.pallas_call(
         functools.partial(cross_kernel, section, gain_at, tile_rows),
         out_shape=jax.ShapeDtypeStruct((rows, columns), jnp.bfloat16),
-        in_specs=[in_vmem()] * (GROUP + 7),
+        in_specs=[in_vmem()] * (GROUP + 8),
         out_specs=in_vmem(),
         scratch_shapes=[pltpu.VMEM((rows, columns), jnp.float32)],
         compiler_params=params(),
-    )(*pieces, gains, near, far, tiles, qk, own, other)
+    )(*pieces, *gains, *weights, near, far, tiles, qk)
 
 
 def attend_kernel(tile_rows, q_ref, near_ref, far_ref, tiles_ref, qk_ref, out_ref):
@@ -367,20 +401,19 @@
 
 
 def plain_query_kernel(section, gain_at, *refs):
-    x_refs = refs[:GROUP]
-    gain_ref, own_ref, other_ref, out_ref = refs[GROUP:]
+    x_refs, gain_refs, weight_refs, out_ref = refs[:-5], refs[-5:-3], refs[-3:-1], refs[-1]
     rows = out_ref.shape[0]
-    project(section, gain_at, rows, x_refs, gain_ref, own_ref, other_ref, out_ref)
-
-
-def plain_query_part(section, gain_at, rows, pieces, gains, own, other):
+    project(section, gain_at, rows, x_refs, gain_refs, weight_refs, out_ref, text_mask)
+
+
+def plain_query_part(section, gain_at, rows, pieces, gains, weights):
     return pl.pallas_call(
         functools.partial(plain_query_kernel, section, gain_at),
-        out_shape=jax.ShapeDtypeStruct((rows, own.shape[1]), jnp.float32),
-        in_specs=[in_vmem()] * (GROUP + 3),
+        out_shape=jax.ShapeDtypeStruct((rows, weights[0].shape[1]), jnp.float32),
+        in_specs=[in_vmem()] * (len(pieces) + 4),
         out_specs=in_vmem(),
         compiler_params=params(),
-    )(*pieces, gains, own, other)
+    )(*pieces, *gains, *weights)
 
 
 def turn(values, cosine, sine):
@@ -390,27 +423,27 @@
 
 
 def query_kernel(section, gain_at, *refs):
-    x_refs = refs[:GROUP]
-    gain_ref, cosine_ref, sine_ref, own_ref, other_ref, out_ref, product_ref = refs[GROUP:]
+    x_refs, gain_refs, weight_refs = refs[:GROUP], refs[GROUP : GROUP + 2], refs[GROUP + 2 : GROUP + 4]
+    cosine_ref, sine_ref, out_ref, product_ref = refs[GROUP + 4 :]
     rows = product_ref.shape[0]
     core = lax.axis_index("section")
     mine = pl.ds(pl.multiple_of(core * rows, rows), rows)
-    queries = project(section, gain_at, rows, x_refs, gain_ref, own_ref, other_ref, product_ref)
+    queries = project(section, gain_at, rows, x_refs, gain_refs, weight_refs, product_ref)
     for head in range(queries.shape[1] // HD):
         turned = turn(queries[:, head * HD : (head + 1) * HD], cosine_ref[mine, :], sine_ref[mine, :])
         out_ref[head * rows : (head + 1) * rows, :] = turned.astype(jnp.bfloat16)
 
 
-def query_part(section, gain_at, rows, pieces, gains, cosine, sine, own, other):
-    columns = own.shape[1]
+def query_part(section, gain_at, rows, pieces, gains, weights, cosine, sine):
+    columns = weights[0].shape[1]
     return pl.pallas_call(
         functools.partial(query_kernel, section, gain_at),
         out_shape=jax.ShapeDtypeStruct((rows * columns // HD, HD), jnp.bfloat16),
-        in_specs=[in_vmem()] * (GROUP + 5),
+        in_specs=[in_vmem()] * (GROUP + 6),
         out_specs=in_vmem(),
         scratch_shapes=[pltpu.VMEM((rows, columns), jnp.float32)],
         compiler_params=params(),
-    )(*pieces, gains, cosine, sine, own, other)
+    )(*pieces, *gains, *weights, cosine, sine)
 
 
 def self_kernel(width, q_ref, near_ref, far_ref, cosine_ref, sine_ref, out_ref):
@@ -447,7 +480,7 @@
     high = lax.axis_index("tp") // GROUP
     rows = hidden_ref.shape[0]
     hidden = hidden_ref[...].astype(jnp.float32)
-    scaled = (hidden * small_ref[1:2, :]).astype(jnp.bfloat16)
+    scaled = (hidden * small_ref[0:1, :]).astype(jnp.bfloat16)
     squares = hidden * hidden
     top = squares.astype(jnp.bfloat16)
     rest = (squares - top.astype(jnp.float32)).astype(jnp.bfloat16)
@@ -457,10 +490,10 @@
         [square_sum, jnp.zeros((16, 2 * HD - rows), jnp.float32)], axis=1
     ).astype(jnp.bfloat16)
 
-    def run(weight_ref):
+    def run(core, weight_ref):
         product[...] = jnp.dot(scaled, weight_ref[...], preferred_element_type=jnp.float32)
 
-    with_weight(section, own_ref, other_ref, run)
+    with_weight(section, (own_ref,), (other_ref,), run)
     for k in range(GROUP):
         for part in range(2):
             start = pl.multiple_of((part * KV + (high ^ k)) * HD, HD)
@@ -485,24 +518,23 @@
 def out_kernel(section, gated, *refs):
     x_refs = refs[:GROUP]
     hidden_ref, small_ref, tiles_ref, own_ref, other_ref, out_ref = refs[GROUP:]
-    core = lax.axis_index("section")
     rows = out_ref.shape[0]
     depth = x_refs[0].shape[2]
 
-    def run(weight_ref):
+    def run(core, weight_ref):
         branch = jnp.zeros(out_ref.shape, jnp.float32)
         for at in range(GROUP * GROUP):
             branch = branch + jnp.dot(
                 x_refs[at // GROUP][at % GROUP],
-                weight_rows(weight_ref, at, depth),
+                weight_rows(weight_ref, gather_mask(core, at), depth),
                 preferred_element_type=jnp.float32,
             )
         if gated:
-            row_tiles = tiles_ref[pl.ds(pl.multiple_of(core * rows, rows), rows), :1]
-            branch = branch * (row_tiles > 0).astype(jnp.float32) * jnp.tanh(small_ref[3:4, :])
+            row_tiles = tiles_ref[core * rows : (core + 1) * rows, :1]
+            branch = branch * (row_tiles > 0).astype(jnp.float32) * jnp.tanh(small_ref[2:3, :])
         out_ref[...] = (hidden_ref[...].astype(jnp.float32) + branch).astype(jnp.bfloat16)
 
-    with_weight(section, own_ref, other_ref, run)
+    with_weight(section, (own_ref,), (other_ref,), run)
 
 
 def out_part(section, gated, pieces, hidden, small, tiles, own, other):
@@ -515,16 +547,27 @@
     )(*pieces, hidden, small, tiles, own, other)
 
 
-def encoder_kernel(states_ref, gain_ref, fc1_ref, fc2_ref, out_ref, product):
+def encoder_kernel(states_hbm, gain_ref, fc1_hbm, fc2_hbm, out_ref, states_ref, fc1_ref, fc2_ref, product, sems):
+    copies = [
+        pltpu.make_async_copy(source, target, sems.at[at])
+        for at, (source, target) in enumerate(
+            ((states_hbm, states_ref), (fc1_hbm, fc1_ref), (fc2_hbm, fc2_ref))
+        )
+    ]
+    for copy in copies:
+        copy.start()
     core = lax.axis_index("section")
     chip = lax.axis_index("tp")
     member = jnp.where(core == 0, chip % GROUP, chip // GROUP)
+    copies[0].wait()
     states = states_ref[...].astype(jnp.float32)
     centred = states - jnp.mean(states, axis=-1, keepdims=True)
     spread = jnp.mean(centred * centred, axis=-1, keepdims=True)
     normed = (centred * lax.rsqrt(spread + epsilon) * gain_ref[...]).astype(jnp.bfloat16)
-    inner = jnp.dot(normed, fc1_ref[...], preferred_element_type=jnp.float32)
+    copies[1].wait()
+    inner = dot_rows(normed, fc1_ref[...])
     inner = (0.5 * inner * (1.0 + lax.erf(inner * 2.0 ** (-0.5)))).astype(jnp.bfloat16)
+    copies[2].wait()
     product[...] = jnp.dot(inner, fc2_ref[...], preferred_element_type=jnp.float32).astype(
         jnp.bfloat16
     )
@@ -535,13 +578,20 @@
 
 def encoder_part(states, gain, fc1, fc2):
     rows, width = states.shape
+    in_place = pl.BlockSpec(memory_space=pltpu.HBM)
     return pl.pallas_call(
         encoder_kernel,
         out_shape=jax.ShapeDtypeStruct((GROUP, rows // GROUP, width), jnp.bfloat16),
-        in_specs=[in_vmem()] * 4,
+        in_specs=[in_place, in_vmem(), in_place, in_place],
         out_specs=in_vmem(),
-        scratch_shapes=[pltpu.VMEM((rows, width), jnp.bfloat16)],
-        compiler_params=params(),
+        scratch_shapes=[
+            pltpu.VMEM(states.shape, jnp.bfloat16),
+            pltpu.VMEM(fc1.shape, jnp.bfloat16),
+            pltpu.VMEM(fc2.shape, jnp.bfloat16),
+            pltpu.VMEM((rows, width), jnp.bfloat16),
+            pltpu.SemaphoreType.DMA((3,)),
+        ],
+        compiler_params=params(5 * VMEM_LIMIT),
     )(states, gain, fc1, fc2)
 
 
@@ -620,41 +670,35 @@
     full_width = local_width * lax.axis_size("tp")
     member = jnp.where(core == 0, chip % GROUP, chip // GROUP)
 
+    after = lax.optimization_barrier
+    own_cross_kv, own_cross_q, own_cross_o = cross_kv[0], cross_q[0], cross_o[0]
+    own_self_kv, own_self_q, own_self_o = self_kv[0], self_q[0], self_o[0]
+
+    hidden = lax.dynamic_slice_in_dim(text_states, core * rows, rows, 0)
+    entry = jnp.concatenate(
+        [hidden, cross_norm, self_norm, jnp.zeros((14, local_width), jnp.bfloat16)]
+    )
+    text_come = send_group([entry] * GROUP, (GROUP, GROUP))
+    branch = encoder_part(vision_states, vision_norm_gain[None], vision_fc1.T, vision_fc2)
+    come = send_group(branch, (1, GROUP))
+    come, text_come, own, self_norm, cross_qk_gain, cross_gate = after(
+        (come, text_come, own_cross_kv, self_norm, cross_qk_gain, cross_gate)
+    )
+    near = total([branch[0]] + come).astype(jnp.bfloat16)
+    come = send_group([near] * GROUP, (GROUP, 1))
+    far_cross_kv = swap_cores(own)
     small = jnp.concatenate(
         [
-            cross_norm.astype(jnp.float32),
             self_norm.astype(jnp.float32),
             jnp.pad(cross_qk_gain.reshape(1, -1), ((0, 0), (0, local_width - 2 * HD))),
             jnp.broadcast_to(cross_gate[None], (1, local_width)),
         ]
     )
-    small = lax.all_gather(small, "section", axis=0)
-    own_cross_kv, own_cross_q, own_cross_o = cross_kv[0], cross_q[0], cross_o[0]
-    own_self_kv, own_self_q, own_self_o = self_kv[0], self_q[0], self_o[0]
-    far_cross_kv = swap_cores(own_cross_kv)
-    far_cross_q = swap_cores(own_cross_q)
-    far_cross_o = swap_cores(own_cross_o)
-    far_self_kv = swap_cores(own_self_kv)
-    far_self_q = swap_cores(own_self_q)
-    far_self_o = swap_cores(own_self_o)
-
-    hidden = lax.dynamic_slice_in_dim(text_states, core * rows, rows, 0)
-    gain_rows = small[:, :2].astype(jnp.bfloat16).reshape(4, local_width)
-    entry = jnp.concatenate(
-        [hidden, gain_rows, jnp.zeros((12, local_width), jnp.bfloat16)], axis=0
-    )
-    come = [send_xor(entry, (GROUP * k, k)) for k in range(1, GROUP)]
-
-    branch = encoder_part(vision_states, vision_norm_gain[None], vision_fc1, vision_fc2)
-    branch, come = lax.optimization_barrier((branch, come))
-    first = jnp.stack([entry] + come)
-    pieces = [first] + [send_xor(first, (k, GROUP * k)) for k in range(1, GROUP)]
-    near = total(
-        [branch[0]] + [send_xor(branch[k], (k, GROUP * k)) for k in range(1, GROUP)]
-    ).astype(jnp.bfloat16)
-    come = [send_xor(near, (GROUP * k, k)) for k in range(1, GROUP)]
-    come, pieces = lax.optimization_barrier((come, pieces))
-    gains = jnp.concatenate([piece[:, rows:] for piece in pieces], axis=0)
+    far_small = swap_cores(small)
+    text = jnp.stack([entry] + text_come)
+    come, far_cross_kv, far_small, text, own = after(
+        (come, far_cross_kv, far_small, text, own_cross_q)
+    )
     branch_rows = total([near] + come)
     vis_rows = lax.dynamic_index_in_dim(
         vision_states.reshape(branch.shape), member, 0, keepdims=False
@@ -662,52 +706,96 @@
     vis_out = (vis_rows.astype(jnp.float32) + jnp.tanh(vision_gate[0]) * branch_rows).astype(
         jnp.bfloat16
     )
-    come = [send_xor(vis_out, (k, GROUP * k)) for k in range(1, GROUP)]
-    queries = plain_query_part(0, 0, rows, pieces, gains, own_cross_q, far_cross_q)
-    come, queries = lax.optimization_barrier((come, queries))
-    vis_pieces = [vis_out] + come
-
-    image_parts = image_part(vis_pieces, projector, own_cross_kv, far_cross_kv)
-    image_kv = []
-    for section in range(2):
-        kv_rows = reduce_heads(image_parts[section])
-        key_gain = small[section, 2, HD : 2 * HD]
+    come = send_group([vis_out] * GROUP, (1, GROUP))
+    text_come = send_xor(text, (1, 2))
+    far_cross_q = swap_cores(own)
+    come, text_come, far_cross_q, own = after((come, text_come, far_cross_q, own_cross_o))
+    scalars = [jnp.where(core == 0, small, far_small), jnp.where(core == 0, far_small, small)]
+
+    image_parts = image_part([vis_out] + come, projector, own_cross_kv, far_cross_kv)
+    come = send_group(image_parts[0], (GROUP, GROUP))
+    text = jnp.concatenate([text, text_come])
+    text_come = send_xor(text, (2, 1))
+    far_cross_o = swap_cores(own)
+    come, text_come, far_cross_o, own = after((come, text_come, far_cross_o, own_self_kv))
+    near = total([image_parts[0, 0]] + come).astype(jnp.bfloat16)
+    come = send_group([near] * GROUP, (1, 1))
+    gains = jnp.concatenate([text[:, rows:], text_come[:, rows:]])
+    far_gains = swap_cores(gains)
+    far_self_kv = swap_cores(own)
+    gains = (gains, far_gains)
+    text = [half[at : at + GROUP] for half in (text, text_come) for at in (0, GROUP)]
+    queries = plain_query_part(0, 0, rows, text, gains, (own_cross_q, far_cross_q))
+    come, queries, far_self_kv = after((come, queries, far_self_kv))
+    parts = [near] + come
+
+    def image_rows(kv_rows, section):
+        key_gain = scalars[section][1, HD : 2 * HD]
         near = jnp.concatenate(
             [rms_norm(kv_rows[:, :HD], key_gain), kv_rows[:, HD:]], axis=1
         ).astype(jnp.bfloat16)
-        image_kv.append((near, swap_cores(near)))
-
+        return near, swap_cores(near)
+
+    near, far = image_rows(total(parts), 0)
     tile_rows = 2 * vision_states.shape[0] // TILES
     tiles = jnp.broadcast_to(visible_tiles[:, None], (seq_len, HD))
     cosine, sine = (jnp.asarray(table) for table in rope_tables(seq_len))
 
-    results = []
-    for section in range(2):
-        scalars = small[section]
-        near, far = image_kv[section]
+    def self_block(section, hidden, beside_mixed):
+        nonlocal far_self_o
+        steps = head_steps(key_value_part(section, hidden, scalars[section], own_self_kv, far_self_kv))
+        come = send_group([hidden] * GROUP, (GROUP, 1))
+        kv_rows = steps[1](steps[0]())
+        extra = steps[2](kv_rows)
         if section == 0:
-            mixed = cross_mix_from(tile_rows, queries, near, far, tiles, scalars)
+            far_self_o = swap_cores(after((own_self_o, hidden))[0])
+            come, kv_rows, extra, far_self_o = after((come, kv_rows, extra, far_self_o))
         else:
-            mixed = cross_mix(
-                section, 2 * section, tile_rows, rows, gather_chips(hidden), gains, near, far,
-                tiles, scalars, own_cross_q, far_cross_q,
-            )
-        hidden = out_part(
-            section, True, gather_chips(mixed), hidden, scalars, tiles, own_cross_o, far_cross_o
-        )
-        pieces = gather_chips(hidden)
-        near = reduce_heads(
-            key_value_part(section, hidden, scalars, own_self_kv, far_self_kv)
-        ).astype(jnp.bfloat16)
+            come, kv_rows, extra = after((come, kv_rows, extra))
+        first = jnp.stack([hidden] + come)
+        come = send_group([first] * GROUP, (1, GROUP))
+        kv_rows = steps[3](kv_rows, extra)
+        kv_rows = steps[5](kv_rows, steps[4](kv_rows))
+        come, kv_rows, extra = after((come, kv_rows, steps[6](kv_rows)))
+        near = steps[7](kv_rows, extra).astype(jnp.bfloat16)
         far = swap_cores(near)
         queries = query_part(
-            section, 2 * section + 1, rows, pieces, gains, cosine, sine, own_self_q, far_self_q
+            section, 1, rows, [first] + come, gains, (own_self_q, far_self_q), cosine, sine
         )
         mixed = self_mix(full_width, queries, near, far, cosine, sine)
+        pieces, extras = gather_chips(mixed, *beside_mixed)
         hidden = out_part(
-            section, False, gather_chips(mixed), hidden, scalars, tiles, own_self_o, far_self_o
-        )
-        results.append(hidden)
+            section, False, pieces, hidden, scalars[section], tiles, own_self_o, far_self_o
+        )
+        return hidden, extras
+
+    mixed = cross_mix_from(tile_rows, queries, near, far, tiles, scalars[0])
+    mixed, own, second_kept = after((mixed, own_self_q, image_parts[1]))
+    second = head_steps(second_kept)
+    pieces, ((far_self_q, come), second_come) = gather_chips(
+        mixed,
+        lambda: (swap_cores(own), second[0]()),
+        lambda extra: second[2](second[1](extra[1])),
+    )
+    second_rows = second[3](second[1](come), second_come)
+    hidden = out_part(0, True, pieces, hidden, scalars[0], tiles, own_cross_o, far_cross_o)
+    far_self_o = None
+    hidden, (come, second_come) = self_block(
+        0,
+        hidden,
+        (lambda: second[4](second_rows), lambda extra: second[6](second[5](second_rows, extra))),
+    )
+    second_rows = second[7](second[5](second_rows, come), second_come)
+    results = [hidden]
+    near, far = image_rows(second_rows, 1)
+    pieces, (far,) = gather_chips(hidden, lambda: far)
+    mixed = cross_mix(
+        1, 0, tile_rows, rows, pieces, gains, (own_cross_q, far_cross_q), near, far, tiles, scalars[1]
+    )
+    pieces, _ = gather_chips(mixed)
+    hidden = out_part(1, True, pieces, hidden, scalars[1], tiles, own_cross_o, far_cross_o)
+    hidden, _ = self_block(1, hidden, ())
+    results.append(hidden)
     come = swap_cores(jnp.where(core == 0, results[1], results[0]))
     return jnp.where(
         core == 0,

time: 276 us -> 221 us (0.80)
  waiting for transfers between devices: 120 us -> 82.7 us
  starting transfers between devices: 116 us -> 98.8 us
  blocking collectives: 3.97 us -> 0 us
    ppermute x81 -> x74, waiting for transfers between devices: 116 us -> 79.1 us  [send_xor(): return lax.ppermute(block, ('section', 'tp'), route)]
    ppermute x81 -> x74, starting transfers between devices: 108 us -> 94.5 us  [send_xor(): return lax.ppermute(block, ('section', 'tp'), route)]
    ppermute x11 -> x13, starting transfers between devices: 8.77 us -> 4.26 us  [swap_cores(): return lax.ppermute(block, 'section', [(0, 1), (1, 0)])]
    pallas_call x4, Pallas kernels: 7.73 us -> 3.58 us  [out_part(): pl.pallas_call(functools.partial(out_kernel, section, gated), out_shape=j...]
    all_gather x1 -> x0, blocking collectives: 3.97 us -> none  [paired_body(): small = lax.all_gather(small, 'section', axis=0)]
    unnamed x31 -> x29, local copies, waits for them, and re-layouts: 5.91 us -> 4.97 us
  transfers between devices with their start and end apart: 92 -> 87, of which waited for: 53 -> 40; matrix products, arithmetic and copies ran while one was open for 3% -> 3% of each run, Pallas kernels for 4% -> 6%
where the time goes in v3:
time: 221 us; the launch traced here: 220 us
  starting transfers between devices  98.8 us (45%)
  waiting for transfers between devices  82.7 us (37%)
  Pallas kernels  22.2 us (10%)
  local copies, waits for them, and re-layouts  7.75 us (4%)
  other arithmetic  6.62 us (3%)
    ppermute x74, starting transfers between devices, send_xor(): return lax.ppermute(block, ('section', 'tp'), route)  94.5 us
    ppermute x74, waiting for transfers between devices, send_xor(): return lax.ppermute(block, ('section', 'tp'), route)  79.1 us
    pallas_call x1, Pallas kernels, cross_mix(): pl.pallas_call(functools.partial(cross_kernel, section, gain_at, tile_row...  4.97 us
    unnamed x29, local copies, waits for them, and re-layouts  4.97 us
    pallas_call x1, Pallas kernels, plain_query_part(): pl.pallas_call(functools.partial(plain_query_kernel, section, gain_at), o...  4.51 us
  transfers between devices with their start and end apart: 87, of which 40 were waited for; matrix products, arithmetic and copies ran while one was open for 3% of the time, Pallas kernels for 6%

profile of v3, /device:TPU:0, one launch (start us, length us, event | category | flops | bytes accessed | tf_op | source)
XLA Modules:
  0.0 220.1 jit_solution(8987973034442929316)
XLA Ops:
  1.7 5.1 %collective-permute-start.5 = (bf16[80,512]{1,0:T(8,128)(2,1)S(1)}, bf16[80,512]{1,0:T(8,128)(2,1)S(1)}, u32[]{:S(2)}, u32[]{:S(2)}) collective-permute-start(bf16[80,512]{1,0:T(8,128)(2,1)S(1)} %maximum_maximum_fusion), channel_id=1, source_target_pairs={{0,12},{1,13},{2,14},{3,15},{4,8},{5,9},{6,10},{7,11},{8,4},{9,5},... | collective-permute-start | bytes 245768 | tf_op jit(solution)/shard_map/ppermute | solution.py:212
  8.7 3.6 %shard_map.190 = bf16[4,32,1280]{2,1,0:T(8,128)(2,1)} custom-call(bf16[128,1280]{1,0:T(8,128)(2,1)} %states_hbm.1, f32[1,1280]{1,0:T(1,128)} %broadcast_in_dim.10.gain_ref, bf16[320,1280]{1,0:T(8,128)(2,1)} %bitcast.117, bf16[320,1280]{1,0:T(8,128)(2,1)} %fc2_hbm.1), custom_call_target="tpu_custom_call" | custom-call | tf_op jit(solution)/shard_map/pallas_call | solution.py:582
  13.5 2.7 %collective-permute-start.2 = (bf16[32,1280]{1,0:T(8,128)(2,1)S(1)}, bf16[32,1280]{1,0:T(8,128)(2,1)S(1)}, u32[]{:S(2)}, u32[]{:S(2)}) collective-permute-start(bf16[32,1280]{1,0:T(8,128)(2,1)S(1)} %get-tuple-element.170), channel_id=1, source_target_pairs={{0,3},{1,2},{2,1},{3,0},{4,7},{5,6},{6,5},{7,4},{8,11},{9,10},{10,... | collective-permute-start | bytes 245768 | tf_op jit(solution)/shard_map/ppermute | solution.py:212
  23.5 3.7 %collective-permute-start.8 = (bf16[32,1280]{1,0:T(8,128)(2,1)S(1)}, bf16[32,1280]{1,0:T(8,128)(2,1)S(1)}, u32[]{:S(2)}, u32[]{:S(2)}) collective-permute-start(bf16[32,1280]{1,0:T(8,128)(2,1)S(1)} %fusion.2), channel_id=1, source_target_pairs={{0,12},{1,13},{2,14},{3,15},{4,8},{5,9},{6,10},{7,11},{8,4},{9,5},... | collective-permute-start | bytes 245768 | tf_op jit(solution)/shard_map/ppermute | solution.py:212
  36.5 2.5 %collective-permute-start.13 = (bf16[32,1280]{1,0:T(8,128)(2,1)S(1)}, bf16[32,1280]{1,0:T(8,128)(2,1)S(1)}, u32[]{:S(2)}, u32[]{:S(2)}) collective-permute-start(bf16[32,1280]{1,0:T(8,128)(2,1)S(1)} %fusion.3.p0), channel_id=1, source_target_pairs={{0,3},{1,2},{2,1},{3,0},{4,7},{5,6},{6,5},{7,4},{8,11},{9,10},{10,... | collective-permute-start | bytes 245768 | tf_op jit(solution)/shard_map/ppermute | solution.py:212
  40.0 3.9 %collective-permute-done.13.p3 = bf16[32,1280]{1,0:T(8,128)(2,1)S(1)} collective-permute-done((bf16[32,1280]{1,0:T(8,128)(2,1)S(1)}, bf16[32,1280]{1,0:T(8,128)(2,1)S(1)}, u32[]{:S(2)}, u32[]{:S(2)}) %collective-permute-start.13) | collective-permute-done | bytes 81952 | tf_op jit(solution)/shard_map/ppermute | solution.py:212
  53.3 2.1 collective-permute-done.18
  55.5 2.3 %collective-permute-done.17 = bf16[128,256]{1,0:T(8,128)(2,1)S(1)} collective-permute-done((bf16[128,256]{1,0:T(8,128)(2,1)S(1)}, bf16[128,256]{1,0:T(8,128)(2,1)S(1)}, u32[]{:S(2)}, u32[]{:S(2)}) %collective-permute-start.17) | collective-permute-done | bytes 65568 | tf_op jit(solution)/shard_map/ppermute | solution.py:212
  62.3 4.5 %shard_map.192.q_ref = f32[64,256]{1,0:T(8,128)S(1)} custom-call(bf16[4,80,512]{2,1,0:T(8,128)(2,1)S(1)} %pad_maximum_fusion.refs_0_, bf16[4,80,512]{2,1,0:T(8,128)(2,1)S(1)} %collective-permute-done.14.refs_1_, bf16[4,80,512]{2,1,0:T(8,128)(2,1)S(1)} %get-tuple-element.166.refs_2_, bf16[4,80,512]{2,1,0:T(8,128)(2,1)S(1)} %get-tuple-element.165.refs_3_, ...), custom_call_target="tpu_custom_call" | custom-call | tf_op jit(solution)/shard_map/pallas_call | solution.py:410
  76.0 3.8 %collective-permute-done.28 = bf16[64,256]{1,0:T(8,128)(2,1)S(1)} collective-permute-done((bf16[64,256]{1,0:T(8,128)(2,1)S(1)}, bf16[64,256]{1,0:T(8,128)(2,1)S(1)}, u32[]{:S(2)}, u32[]{:S(2)}) %collective-permute-start.28) | collective-permute-done | bytes 32800 | tf_op jit(solution)/shard_map/ppermute | solution.py:212
  83.8 5.5 %collective-permute-done.35 = bf16[128,256]{1,0:T(8,128)(2,1)S(1)} collective-permute-done((bf16[128,256]{1,0:T(8,128)(2,1)S(1)}, bf16[128,256]{1,0:T(8,128)(2,1)S(1)}, u32[]{:S(2)}, u32[]{:S(2)}) %collective-permute-start.35) | collective-permute-done | bytes 65568 | tf_op jit(solution)/shard_map/ppermute | solution.py:212
  95.7 2.7 %collective-permute-done.39 = bf16[2,80,256]{2,1,0:T(8,128)(2,1)S(1)} collective-permute-done((bf16[2,80,256]{2,1,0:T(8,128)(2,1)S(1)}, bf16[2,80,256]{2,1,0:T(8,128)(2,1)S(1)}, u32[]{:S(2)}, u32[]{:S(2)}) %collective-permute-start.39) | collective-permute-done | bytes 81952 | tf_op jit(solution)/shard_map/ppermute | solution.py:212
  108.3 6.3 %collective-permute-done.46 = bf16[80,256]{1,0:T(8,128)(2,1)S(1)} collective-permute-done((bf16[80,256]{1,0:T(8,128)(2,1)S(1)}, bf16[80,256]{1,0:T(8,128)(2,1)S(1)}, u32[]{:S(2)}, u32[]{:S(2)}) %collective-permute-start.46) | collective-permute-done | bytes 40992 | tf_op jit(solution)/shard_map/ppermute | solution.py:212
  118.5 2.2 %collective-permute-start.50 = (bf16[64,256]{1,0:T(8,128)(2,1)S(1)}, bf16[64,256]{1,0:T(8,128)(2,1)S(1)}, u32[]{:S(2)}, u32[]{:S(2)}) collective-permute-start(bf16[64,256]{1,0:T(8,128)(2,1)S(1)} %shard_map.197), channel_id=1, source_target_pairs={{0,12},{1,13},{2,14},{3,15},{4,8},{5,9},{6,10},{7,11},{8,4},{9,5},... | collective-permute-start | bytes 98312 | tf_op jit(solution)/shard_map/ppermute | solution.py:212
  120.7 2.2 %collective-permute-start.48 = (bf16[64,256]{1,0:T(8,128)(2,1)S(1)}, bf16[64,256]{1,0:T(8,128)(2,1)S(1)}, u32[]{:S(2)}, u32[]{:S(2)}) collective-permute-start(bf16[64,256]{1,0:T(8,128)(2,1)S(1)} %shard_map.197), channel_id=1, source_target_pairs={{0,4},{1,5},{2,6},{3,7},{4,0},{5,1},{6,2},{7,3},{8,12},{9,13},{10,... | collective-permute-start | bytes 98312 | tf_op jit(solution)/shard_map/ppermute | solution.py:212
  125.5 2.6 %collective-permute-start.54 = (bf16[4,64,256]{2,1,0:T(8,128)(2,1)S(1)}, bf16[4,64,256]{2,1,0:T(8,128)(2,1)S(1)}, u32[]{:S(2)}, u32[]{:S(2)}) collective-permute-start(bf16[4,64,256]{2,1,0:T(8,128)(2,1)S(1)} %pad_maximum_fusion.6.refs_0_), channel_id=1, source_target_pairs={{0,3},{1,2},{2,1},{3,0},{4,7},{5,6},{6,5},{7,4},{8,11},{9,10},{10,... | collective-permute-start | bytes 393224 | tf_op jit(solution)/shard_map/ppermute | solution.py:212
  130.3 3.7 %collective-permute-done.55 = bf16[128,256]{1,0:T(8,128)(2,1)S(1)} collective-permute-done((bf16[128,256]{1,0:T(8,128)(2,1)S(1)}, bf16[128,256]{1,0:T(8,128)(2,1)S(1)}, u32[]{:S(2)}, u32[]{:S(2)}) %collective-permute-start.55) | collective-permute-done | bytes 65568 | tf_op jit(solution)/shard_map/ppermute | solution.py:212
  135.5 2.1 collective-permute-start.58
  137.8 2.1 collective-permute-start.56
  147.0 3.9 %collective-permute-done.62.refs_3_ = bf16[4,64,512]{2,1,0:T(8,128)(2,1)S(1)} collective-permute-done((bf16[4,64,512]{2,1,0:T(8,128)(2,1)S(1)}, bf16[4,64,512]{2,1,0:T(8,128)(2,1)S(1)}, u32[]{:S(2)}, u32[]{:S(2)}) %collective-permute-start.62) | collective-permute-done | bytes 262176 | tf_op jit(solution)/shard_map/ppermute | solution.py:212
  150.9 2.7 %collective-permute-done.61.refs_2_ = bf16[4,64,512]{2,1,0:T(8,128)(2,1)S(1)} collective-permute-done((bf16[4,64,512]{2,1,0:T(8,128)(2,1)S(1)}, bf16[4,64,512]{2,1,0:T(8,128)(2,1)S(1)}, u32[]{:S(2)}, u32[]{:S(2)}) %collective-permute-start.61) | collective-permute-done | bytes 262176 | tf_op jit(solution)/shard_map/ppermute | solution.py:212
  153.6 5.0 %shard_map.199 = bf16[64,256]{1,0:T(8,128)(2,1)S(1)} custom-call(bf16[4,64,512]{2,1,0:T(8,128)(2,1)S(1)} %pad_maximum_fusion.3.refs_0_, bf16[4,64,512]{2,1,0:T(8,128)(2,1)S(1)} %collective-permute-done.60.refs_1_, bf16[4,64,512]{2,1,0:T(8,128)(2,1)S(1)} %collective-permute-done.61.refs_2_, bf16[4,64,512]{2,1,0:T(8,128)(2,1)S(1)} %collective-permute-done.62.refs_3_, ...), custom_call_target="tpu_custom_call" | custom-call | tf_op jit(solution)/shard_map/pallas_call | solution.py:379
  158.5 2.1 collective-permute-start.65
  160.9 2.1 collective-permute-start.63
  165.5 2.0 collective-permute-start.68
  169.0 2.4 %collective-permute-done.68.refs_3_ = bf16[4,64,256]{2,1,0:T(8,128)(2,1)S(1)} collective-permute-done((bf16[4,64,256]{2,1,0:T(8,128)(2,1)S(1)}, bf16[4,64,256]{2,1,0:T(8,128)(2,1)S(1)}, u32[]{:S(2)}, u32[]{:S(2)}) %collective-permute-start.68) | collective-permute-done | bytes 131104 | tf_op jit(solution)/shard_map/ppermute | solution.py:212
  174.8 2.1 collective-permute-start.72
  178.7 2.6 %collective-permute-start.69 = (bf16[64,512]{1,0:T(8,128)(2,1)S(1)}, bf16[64,512]{1,0:T(8,128)(2,1)S(1)}, u32[]{:S(2)}, u32[]{:S(2)}) collective-permute-start(bf16[64,512]{1,0:T(8,128)(2,1)S(1)} %shard_map.200.hidden_ref.refs_4_), channel_id=1, source_target_pairs={{0,4},{1,5},{2,6},{3,7},{4,0},{5,1},{6,2},{7,3},{8,12},{9,13},{10,... | collective-permute-start | bytes 196616 | tf_op jit(solution)/shard_map/ppermute | solution.py:212
  186.3 2.8 %collective-permute-start.77 = (bf16[80,256]{1,0:T(8,128)(2,1)S(1)}, bf16[80,256]{1,0:T(8,128)(2,1)S(1)}, u32[]{:S(2)}, u32[]{:S(2)}) collective-permute-start(bf16[80,256]{1,0:T(8,128)(2,1)S(1)} %fusion.8), channel_id=1, source_target_pairs={{0,1},{1,0},{2,3},{3,2},{4,5},{5,4},{6,7},{7,6},{8,9},{9,8},{10,11... | collective-permute-start | bytes 122888 | tf_op jit(solution)/shard_map/ppermute | solution.py:212
  193.9 5.9 %collective-permute-done.78 = bf16[80,256]{1,0:T(8,128)(2,1)S(1)} collective-permute-done((bf16[80,256]{1,0:T(8,128)(2,1)S(1)}, bf16[80,256]{1,0:T(8,128)(2,1)S(1)}, u32[]{:S(2)}, u32[]{:S(2)}) %collective-permute-start.78) | collective-permute-done | bytes 40992 | tf_op jit(solution)/shard_map/ppermute | solution.py:212
  204.8 2.6 %collective-permute-start.80 = (bf16[64,256]{1,0:T(8,128)(2,1)S(1)}, bf16[64,256]{1,0:T(8,128)(2,1)S(1)}, u32[]{:S(2)}, u32[]{:S(2)}) collective-permute-start(bf16[64,256]{1,0:T(8,128)(2,1)S(1)} %shard_map.203), channel_id=1, source_target_pairs={{0,4},{1,5},{2,6},{3,7},{4,0},{5,1},{6,2},{7,3},{8,12},{9,13},{10,... | collective-permute-start | bytes 98312 | tf_op jit(solution)/shard_map/ppermute | solution.py:212
  213.5 2.5 %collective-permute-done.85.refs_3_ = bf16[4,64,256]{2,1,0:T(8,128)(2,1)S(1)} collective-permute-done((bf16[4,64,256]{2,1,0:T(8,128)(2,1)S(1)}, bf16[4,64,256]{2,1,0:T(8,128)(2,1)S(1)}, u32[]{:S(2)}, u32[]{:S(2)}) %collective-permute-start.85) | collective-permute-done | bytes 131104 | tf_op jit(solution)/shard_map/ppermute | solution.py:212
  (249 shorter events, 115.6 us)
Async XLA Ops:
  1.7 14.9 %collective-permute-start.5 = (bf16[80,512]{1,0:T(8,128)(2,1)S(1)}, bf16[80,512]{1,0:T(8,128)(2,1)S(1)}, u32[]{:S(2)}, u32[]{:S(2)}) collective-permute-start(bf16[80,512]{1,0:T(8,128)(2,1)S(1)} %maximum_maximum_fusion), channel_id=1, source_target_pairs={{0,12},{1,13},{2,14},{3,15},{4,8},{5,9},{6,10},{7,11},{8,4},{9,5},... | collective-permute-start | bytes 245768 | tf_op jit(solution)/shard_map/ppermute | solution.py:212
  6.8 10.2 %collective-permute-start.4 = (bf16[80,512]{1,0:T(8,128)(2,1)S(1)}, bf16[80,512]{1,0:T(8,128)(2,1)S(1)}, u32[]{:S(2)}, u32[]{:S(2)}) collective-permute-start(bf16[80,512]{1,0:T(8,128)(2,1)S(1)} %maximum_maximum_fusion), channel_id=1, source_target_pairs={{0,8},{1,9},{2,10},{3,11},{4,12},{5,13},{6,14},{7,15},{8,0},{9,1},... | collective-permute-start | bytes 245768 | tf_op jit(solution)/shard_map/ppermute | solution.py:212
  6.8 10.2 %collective-permute-start.3 = (bf16[80,512]{1,0:T(8,128)(2,1)S(1)}, bf16[80,512]{1,0:T(8,128)(2,1)S(1)}, u32[]{:S(2)}, u32[]{:S(2)}) collective-permute-start(bf16[80,512]{1,0:T(8,128)(2,1)S(1)} %maximum_maximum_fusion), channel_id=1, source_target_pairs={{0,4},{1,5},{2,6},{3,7},{4,0},{5,1},{6,2},{7,3},{8,12},{9,13},{10,... | collective-permute-start | bytes 245768 | tf_op jit(solution)/shard_map/ppermute | solution.py:212
  21.1 11.5 %collective-permute-start.9 = (bf16[512,1024]{1,0:T(8,128)(2,1)}, bf16[512,1024]{1,0:T(8,128)(2,1)S(1)}, u32[]{:S(2)}, u32[]{:S(2)}) collective-permute-start(bf16[512,1024]{1,0:T(8,128)(2,1)} %bitcast.108), channel_id=1, source_target_pairs={{0,16},{16,0},{1,17},{17,1},{2,18},{18,2},{3,19},{19,3},{4,20},{20... | collective-permute-start | bytes 3145736 | tf_op jit(solution)/shard_map/ppermute | solution.py:202
  34.2 10.1 %collective-permute-start.15 = (bf16[8192,256]{1,0:T(8,128)(2,1)}, bf16[8192,256]{1,0:T(8,128)(2,1)}, u32[]{:S(2)}, u32[]{:S(2)}) collective-permute-start(bf16[8192,256]{1,0:T(8,128)(2,1)} %bitcast.15.refs_6_), channel_id=1, source_target_pairs={{0,16},{16,0},{1,17},{17,1},{2,18},{18,2},{3,19},{19,3},{4,20},{20... | collective-permute-start | bytes 12582920 | tf_op jit(solution)/shard_map/ppermute | solution.py:202
  34.9 9.4 %collective-permute-start.14 = (bf16[4,80,512]{2,1,0:T(8,128)(2,1)S(1)}, bf16[4,80,512]{2,1,0:T(8,128)(2,1)S(1)}, u32[]{:S(2)}, u32[]{:S(2)}) collective-permute-start(bf16[4,80,512]{2,1,0:T(8,128)(2,1)S(1)} %pad_maximum_fusion.refs_0_), channel_id=1, source_target_pairs={{0,1},{1,0},{2,3},{3,2},{4,5},{5,4},{6,7},{7,6},{8,9},{9,8},{10,11... | collective-permute-start | bytes 983048 | tf_op jit(solution)/shard_map/ppermute | solution.py:212
  36.5 7.5 %collective-permute-start.13 = (bf16[32,1280]{1,0:T(8,128)(2,1)S(1)}, bf16[32,1280]{1,0:T(8,128)(2,1)S(1)}, u32[]{:S(2)}, u32[]{:S(2)}) collective-permute-start(bf16[32,1280]{1,0:T(8,128)(2,1)S(1)} %fusion.3.p0), channel_id=1, source_target_pairs={{0,3},{1,2},{2,1},{3,0},{4,7},{5,6},{6,5},{7,4},{8,11},{9,10},{10,... | collective-permute-start | bytes 245768 | tf_op jit(solution)/shard_map/ppermute | solution.py:212
  44.3 13.5 %collective-permute-start.20 = (bf16[4096,512]{1,0:T(8,128)(2,1)}, bf16[4096,512]{1,0:T(8,128)(2,1)S(1)}, u32[]{:S(2)}, u32[]{:S(2)}) collective-permute-start(bf16[4096,512]{1,0:T(8,128)(2,1)} %bitcast.97), channel_id=1, source_target_pairs={{0,16},{16,0},{1,17},{17,1},{2,18},{18,2},{3,19},{19,3},{4,20},{20... | collective-permute-start | bytes 12582920 | tf_op jit(solution)/shard_map/ppermute | solution.py:202
  44.7 13.0 %collective-permute-start.19 = (bf16[8,80,512]{2,1,0:T(8,128)(2,1)S(1)}, bf16[8,80,512]{2,1,0:T(8,128)(2,1)S(1)}, u32[]{:S(2)}, u32[]{:S(2)}) collective-permute-start(bf16[8,80,512]{2,1,0:T(8,128)(2,1)S(1)} %constant_dynamic-update-slice_fusion), channel_id=1, source_target_pairs={{0,2},{1,3},{2,0},{3,1},{4,6},{5,7},{6,4},{7,5},{8,10},{9,11},{10,... | collective-permute-start | bytes 1966088 | tf_op jit(solution)/shard_map/ppermute | solution.py:212
  57.8 9.0 %collective-permute-start.25 = (bf16[512,1024]{1,0:T(8,128)(2,1)S(1)}, bf16[512,1024]{1,0:T(8,128)(2,1)S(1)}, u32[]{:S(2)}, u32[]{:S(2)}) collective-permute-start(bf16[512,1024]{1,0:T(8,128)(2,1)S(1)} %bitcast.103), channel_id=1, source_target_pairs={{0,16},{16,0},{1,17},{17,1},{2,18},{18,2},{3,19},{19,3},{4,20},{20... | collective-permute-start | bytes 3145736 | tf_op jit(solution)/shard_map/ppermute | solution.py:202
  58.6 8.2 %collective-permute-start.23 = (bf16[128,256]{1,0:T(8,128)(2,1)S(1)}, bf16[128,256]{1,0:T(8,128)(2,1)S(1)}, u32[]{:S(2)}, u32[]{:S(2)}) collective-permute-start(bf16[128,256]{1,0:T(8,128)(2,1)S(1)} %fusion.7), channel_id=1, source_target_pairs={{0,3},{1,2},{2,1},{3,0},{4,7},{5,6},{6,5},{7,4},{8,11},{9,10},{10,... | collective-permute-start | bytes 196616 | tf_op jit(solution)/shard_map/ppermute | solution.py:212
  69.1 10.8 %collective-permute-start.30 = (bf16[8192,256]{1,0:T(8,128)(2,1)S(1)}, bf16[8192,256]{1,0:T(8,128)(2,1)S(1)}, u32[]{:S(2)}, u32[]{:S(2)}) collective-permute-start(bf16[8192,256]{1,0:T(8,128)(2,1)S(1)} %bitcast.94), channel_id=1, source_target_pairs={{0,16},{16,0},{1,17},{17,1},{2,18},{18,2},{3,19},{19,3},{4,20},{20... | collective-permute-start | bytes 12582920 | tf_op jit(solution)/shard_map/ppermute | solution.py:202
  69.3 10.6 %collective-permute-start.31 = (bf16[2,128,256]{2,1,0:T(8,128)(2,1)S(1)}, bf16[2,128,256]{2,1,0:T(8,128)(2,1)S(1)}, u32[]{:S(2)}, u32[]{:S(2)}) collective-permute-start(bf16[2,128,256]{2,1,0:T(8,128)(2,1)S(1)} %slice.119), channel_id=1, source_target_pairs={{0,8},{1,9},{2,10},{3,11},{4,12},{5,13},{6,14},{7,15},{8,0},{9,1},... | collective-permute-start | bytes 393224 | tf_op jit(solution)/shard_map/ppermute | solution.py:212
  71.7 8.2 %collective-permute-start.28 = (bf16[64,256]{1,0:T(8,128)(2,1)S(1)}, bf16[64,256]{1,0:T(8,128)(2,1)S(1)}, u32[]{:S(2)}, u32[]{:S(2)}) collective-permute-start(bf16[64,256]{1,0:T(8,128)(2,1)S(1)} %shard_map.193), channel_id=1, source_target_pairs={{0,8},{1,9},{2,10},{3,11},{4,12},{5,13},{6,14},{7,15},{8,0},{9,1},... | collective-permute-start | bytes 98312 | tf_op jit(solution)/shard_map/ppermute | solution.py:212
  79.9 9.4 %collective-permute-start.34 = (bf16[4,64,256]{2,1,0:T(8,128)(2,1)S(1)}, bf16[4,64,256]{2,1,0:T(8,128)(2,1)S(1)}, u32[]{:S(2)}, u32[]{:S(2)}) collective-permute-start(bf16[4,64,256]{2,1,0:T(8,128)(2,1)S(1)} %pad_maximum_fusion.5.refs_0_), channel_id=1, source_target_pairs={{0,3},{1,2},{2,1},{3,0},{4,7},{5,6},{6,5},{7,4},{8,11},{9,10},{10,... | collective-permute-start | bytes 393224 | tf_op jit(solution)/shard_map/ppermute | solution.py:212
  81.7 7.6 %collective-permute-start.33 = (bf16[4,64,256]{2,1,0:T(8,128)(2,1)S(1)}, bf16[4,64,256]{2,1,0:T(8,128)(2,1)S(1)}, u32[]{:S(2)}, u32[]{:S(2)}) collective-permute-start(bf16[4,64,256]{2,1,0:T(8,128)(2,1)S(1)} %pad_maximum_fusion.5.refs_0_), channel_id=1, source_target_pairs={{0,2},{1,3},{2,0},{3,1},{4,6},{5,7},{6,4},{7,5},{8,10},{9,11},{10,... | collective-permute-start | bytes 393224 | tf_op jit(solution)/shard_map/ppermute | solution.py:212
  90.2 12.2 %collective-permute-start.41 = (bf16[4096,512]{1,0:T(8,128)(2,1)S(1)}, bf16[4096,512]{1,0:T(8,128)(2,1)S(1)}, u32[]{:S(2)}, u32[]{:S(2)}) collective-permute-start(bf16[4096,512]{1,0:T(8,128)(2,1)S(1)} %bitcast.100), channel_id=1, source_target_pairs={{0,16},{16,0},{1,17},{17,1},{2,18},{18,2},{3,19},{19,3},{4,20},{20... | collective-permute-start | bytes 12582920 | tf_op jit(solution)/shard_map/ppermute | solution.py:202
  90.8 7.5 %collective-permute-start.39 = (bf16[2,80,256]{2,1,0:T(8,128)(2,1)S(1)}, bf16[2,80,256]{2,1,0:T(8,128)(2,1)S(1)}, u32[]{:S(2)}, u32[]{:S(2)}) collective-permute-start(bf16[2,80,256]{2,1,0:T(8,128)(2,1)S(1)} %slice.149), channel_id=1, source_target_pairs={{0,8},{1,9},{2,10},{3,11},{4,12},{5,13},{6,14},{7,15},{8,0},{9,1},... | collective-permute-start | bytes 245768 | tf_op jit(solution)/shard_map/ppermute | solution.py:212
  91.3 7.2 %collective-permute-start.38 = (bf16[64,512]{1,0:T(8,128)(2,1)S(1)}, bf16[64,512]{1,0:T(8,128)(2,1)S(1)}, u32[]{:S(2)}, u32[]{:S(2)}) collective-permute-start(bf16[64,512]{1,0:T(8,128)(2,1)S(1)} %shard_map.194.hidden_ref.refs_4_), channel_id=1, source_target_pairs={{0,12},{1,13},{2,14},{3,15},{4,8},{5,9},{6,10},{7,11},{8,4},{9,5},... | collective-permute-start | bytes 196616 | tf_op jit(solution)/shard_map/ppermute | solution.py:212
  93.2 7.3 %collective-permute-start.37 = (bf16[64,512]{1,0:T(8,128)(2,1)S(1)}, bf16[64,512]{1,0:T(8,128)(2,1)S(1)}, u32[]{:S(2)}, u32[]{:S(2)}) collective-permute-start(bf16[64,512]{1,0:T(8,128)(2,1)S(1)} %shard_map.194.hidden_ref.refs_4_), channel_id=1, source_target_pairs={{0,8},{1,9},{2,10},{3,11},{4,12},{5,13},{6,14},{7,15},{8,0},{9,1},... | collective-permute-start | bytes 196616 | tf_op jit(solution)/shard_map/ppermute | solution.py:212
  103.6 11.0 %collective-permute-start.44 = (bf16[4,64,512]{2,1,0:T(8,128)(2,1)S(1)}, bf16[4,64,512]{2,1,0:T(8,128)(2,1)S(1)}, u32[]{:S(2)}, u32[]{:S(2)}) collective-permute-start(bf16[4,64,512]{2,1,0:T(8,128)(2,1)S(1)} %pad_maximum_fusion.2.refs_0_), channel_id=1, source_target_pairs={{0,3},{1,2},{2,1},{3,0},{4,7},{5,6},{6,5},{7,4},{8,11},{9,10},{10,... | collective-permute-start | bytes 786440 | tf_op jit(solution)/shard_map/ppermute | solution.py:212
  105.1 9.5 %collective-permute-start.43 = (bf16[4,64,512]{2,1,0:T(8,128)(2,1)S(1)}, bf16[4,64,512]{2,1,0:T(8,128)(2,1)S(1)}, u32[]{:S(2)}, u32[]{:S(2)}) collective-permute-start(bf16[4,64,512]{2,1,0:T(8,128)(2,1)S(1)} %pad_maximum_fusion.2.refs_0_), channel_id=1, source_target_pairs={{0,2},{1,3},{2,0},{3,1},{4,6},{5,7},{6,4},{7,5},{8,10},{9,11},{10,... | collective-permute-start | bytes 786440 | tf_op jit(solution)/shard_map/ppermute | solution.py:212
  106.1 8.5 %collective-permute-start.42 = (bf16[4,64,512]{2,1,0:T(8,128)(2,1)S(1)}, bf16[4,64,512]{2,1,0:T(8,128)(2,1)S(1)}, u32[]{:S(2)}, u32[]{:S(2)}) collective-permute-start(bf16[4,64,512]{2,1,0:T(8,128)(2,1)S(1)} %pad_maximum_fusion.2.refs_0_), channel_id=1, source_target_pairs={{0,1},{1,0},{2,3},{3,2},{4,5},{5,4},{6,7},{7,6},{8,9},{9,8},{10,11... | collective-permute-start | bytes 786440 | tf_op jit(solution)/shard_map/ppermute | solution.py:212
  107.2 7.4 %collective-permute-start.46 = (bf16[80,256]{1,0:T(8,128)(2,1)S(1)}, bf16[80,256]{1,0:T(8,128)(2,1)S(1)}, u32[]{:S(2)}, u32[]{:S(2)}) collective-permute-start(bf16[80,256]{1,0:T(8,128)(2,1)S(1)} %add_convert_fusion.7), channel_id=1, source_target_pairs={{0,2},{1,3},{2,0},{3,1},{4,6},{5,7},{6,4},{7,5},{8,10},{9,11},{10,... | collective-permute-start | bytes 122888 | tf_op jit(solution)/shard_map/ppermute | solution.py:212
  125.5 8.5 %collective-permute-start.54 = (bf16[4,64,256]{2,1,0:T(8,128)(2,1)S(1)}, bf16[4,64,256]{2,1,0:T(8,128)(2,1)S(1)}, u32[]{:S(2)}, u32[]{:S(2)}) collective-permute-start(bf16[4,64,256]{2,1,0:T(8,128)(2,1)S(1)} %pad_maximum_fusion.6.refs_0_), channel_id=1, source_target_pairs={{0,3},{1,2},{2,1},{3,0},{4,7},{5,6},{6,5},{7,4},{8,11},{9,10},{10,... | collective-permute-start | bytes 393224 | tf_op jit(solution)/shard_map/ppermute | solution.py:212
  143.4 7.4 %collective-permute-start.62 = (bf16[4,64,512]{2,1,0:T(8,128)(2,1)S(1)}, bf16[4,64,512]{2,1,0:T(8,128)(2,1)S(1)}, u32[]{:S(2)}, u32[]{:S(2)}) collective-permute-start(bf16[4,64,512]{2,1,0:T(8,128)(2,1)S(1)} %pad_maximum_fusion.3.refs_0_), channel_id=1, source_target_pairs={{0,3},{1,2},{2,1},{3,0},{4,7},{5,6},{6,5},{7,4},{8,11},{9,10},{10,... | collective-permute-start | bytes 786440 | tf_op jit(solution)/shard_map/ppermute | solution.py:212
  145.1 8.5 %collective-permute-start.61 = (bf16[4,64,512]{2,1,0:T(8,128)(2,1)S(1)}, bf16[4,64,512]{2,1,0:T(8,128)(2,1)S(1)}, u32[]{:S(2)}, u32[]{:S(2)}) collective-permute-start(bf16[4,64,512]{2,1,0:T(8,128)(2,1)S(1)} %pad_maximum_fusion.3.refs_0_), channel_id=1, source_target_pairs={{0,2},{1,3},{2,0},{3,1},{4,6},{5,7},{6,4},{7,5},{8,10},{9,11},{10,... | collective-permute-start | bytes 786440 | tf_op jit(solution)/shard_map/ppermute | solution.py:212
  146.0 7.5 %collective-permute-start.60 = (bf16[4,64,512]{2,1,0:T(8,128)(2,1)S(1)}, bf16[4,64,512]{2,1,0:T(8,128)(2,1)S(1)}, u32[]{:S(2)}, u32[]{:S(2)}) collective-permute-start(bf16[4,64,512]{2,1,0:T(8,128)(2,1)S(1)} %pad_maximum_fusion.3.refs_0_), channel_id=1, source_target_pairs={{0,1},{1,0},{2,3},{3,2},{4,5},{5,4},{6,7},{7,6},{8,9},{9,8},{10,11... | collective-permute-start | bytes 786440 | tf_op jit(solution)/shard_map/ppermute | solution.py:212
  174.8 7.4 %collective-permute-start.72 = (bf16[2,80,256]{2,1,0:T(8,128)(2,1)S(1)}, bf16[2,80,256]{2,1,0:T(8,128)(2,1)S(1)}, u32[]{:S(2)}, u32[]{:S(2)}) collective-permute-start(bf16[2,80,256]{2,1,0:T(8,128)(2,1)S(1)} %slice.156), channel_id=1, source_target_pairs={{0,8},{1,9},{2,10},{3,11},{4,12},{5,13},{6,14},{7,15},{8,0},{9,1},... | collective-permute-start | bytes 245768 | tf_op jit(solution)/shard_map/ppermute | solution.py:212
  189.2 10.7 %collective-permute-start.76 = (bf16[4,64,512]{2,1,0:T(8,128)(2,1)S(1)}, bf16[4,64,512]{2,1,0:T(8,128)(2,1)S(1)}, u32[]{:S(2)}, u32[]{:S(2)}) collective-permute-start(bf16[4,64,512]{2,1,0:T(8,128)(2,1)S(1)} %pad_maximum_fusion.4.refs_0_), channel_id=1, source_target_pairs={{0,3},{1,2},{2,1},{3,0},{4,7},{5,6},{6,5},{7,4},{8,11},{9,10},{10,... | collective-permute-start | bytes 786440 | tf_op jit(solution)/shard_map/ppermute | solution.py:212
  189.8 10.1 %collective-permute-start.75 = (bf16[4,64,512]{2,1,0:T(8,128)(2,1)S(1)}, bf16[4,64,512]{2,1,0:T(8,128)(2,1)S(1)}, u32[]{:S(2)}, u32[]{:S(2)}) collective-permute-start(bf16[4,64,512]{2,1,0:T(8,128)(2,1)S(1)} %pad_maximum_fusion.4.refs_0_), channel_id=1, source_target_pairs={{0,2},{1,3},{2,0},{3,1},{4,6},{5,7},{6,4},{7,5},{8,10},{9,11},{10,... | collective-permute-start | bytes 786440 | tf_op jit(solution)/shard_map/ppermute | solution.py:212
  190.7 9.1 %collective-permute-start.74 = (bf16[4,64,512]{2,1,0:T(8,128)(2,1)S(1)}, bf16[4,64,512]{2,1,0:T(8,128)(2,1)S(1)}, u32[]{:S(2)}, u32[]{:S(2)}) collective-permute-start(bf16[4,64,512]{2,1,0:T(8,128)(2,1)S(1)} %pad_maximum_fusion.4.refs_0_), channel_id=1, source_target_pairs={{0,1},{1,0},{2,3},{3,2},{4,5},{5,4},{6,7},{7,6},{8,9},{9,8},{10,11... | collective-permute-start | bytes 786440 | tf_op jit(solution)/shard_map/ppermute | solution.py:212
  (69 other events, 545.4 us)

commit v4 on v3

--- a/solution.py
+++ b/solution.py
@@ -218,19 +218,13 @@
     return [sent[k] for k in range(1, GROUP)]
 
 
-def gather_chips(block, beside_first=None, beside_second=None):
-    after = lax.optimization_barrier
+def gather_chips(block, beside=None):
+    extra = beside() if beside is not None else ()
     come = send_group([block] * GROUP, (GROUP, 1))
-    extras = []
-    if beside_first is not None:
-        come, extra = after((come, beside_first()))
-        extras.append(extra)
     first = jnp.stack([block] + come)
     come = send_group([first] * GROUP, (1, GROUP))
-    if beside_second is not None:
-        come, extra = after((come, beside_second(extras[0])))
-        extras.append(extra)
-    return [first] + come, extras
+    come, extra = lax.optimization_barrier((come, extra))
+    return [first] + come, extra
 
 
 def total(parts):
@@ -365,32 +359,11 @@
     out_ref[...] = side_by_side(mixed, rows)
 
 
-def cross_kernel(section, gain_at, tile_rows, *refs):
-    x_refs = refs[:GROUP]
-    gain_refs, weight_refs = refs[GROUP : GROUP + 2], refs[GROUP + 2 : GROUP + 4]
-    near_ref, far_ref, tiles_ref, qk_ref, out_ref, product_ref = refs[GROUP + 4 :]
-    rows = out_ref.shape[0]
-    queries = project(section, gain_at, rows, x_refs, gain_refs, weight_refs, product_ref)
-    cross_attend(tile_rows, queries, near_ref, far_ref, tiles_ref, qk_ref, out_ref)
-
-
-def cross_mix(section, gain_at, tile_rows, rows, pieces, gains, weights, near, far, tiles, qk):
-    columns = weights[0].shape[1]
-    return pl.pallas_call(
-        functools.partial(cross_kernel, section, gain_at, tile_rows),
-        out_shape=jax.ShapeDtypeStruct((rows, columns), jnp.bfloat16),
-        in_specs=[in_vmem()] * (GROUP + 8),
-        out_specs=in_vmem(),
-        scratch_shapes=[pltpu.VMEM((rows, columns), jnp.float32)],
-        compiler_params=params(),
-    )(*pieces, *gains, *weights, near, far, tiles, qk)
-
-
 def attend_kernel(tile_rows, q_ref, near_ref, far_ref, tiles_ref, qk_ref, out_ref):
     cross_attend(tile_rows, q_ref[...], near_ref, far_ref, tiles_ref, qk_ref, out_ref)
 
 
-def cross_mix_from(tile_rows, queries, near, far, tiles, qk):
+def cross_mix(tile_rows, queries, near, far, tiles, qk):
     return pl.pallas_call(
         functools.partial(attend_kernel, tile_rows),
         out_shape=jax.ShapeDtypeStruct(queries.shape, jnp.bfloat16),
@@ -400,15 +373,15 @@
     )(queries, near, far, tiles, qk)
 
 
-def plain_query_kernel(section, gain_at, *refs):
+def plain_query_kernel(section, gain_at, mask_of, *refs):
     x_refs, gain_refs, weight_refs, out_ref = refs[:-5], refs[-5:-3], refs[-3:-1], refs[-1]
     rows = out_ref.shape[0]
-    project(section, gain_at, rows, x_refs, gain_refs, weight_refs, out_ref, text_mask)
-
-
-def plain_query_part(section, gain_at, rows, pieces, gains, weights):
+    project(section, gain_at, rows, x_refs, gain_refs, weight_refs, out_ref, mask_of)
+
+
+def plain_query_part(section, gain_at, rows, pieces, gains, weights, mask_of=gather_mask):
     return pl.pallas_call(
-        functools.partial(plain_query_kernel, section, gain_at),
+        functools.partial(plain_query_kernel, section, gain_at, mask_of),
         out_shape=jax.ShapeDtypeStruct((rows, weights[0].shape[1]), jnp.float32),
         in_specs=[in_vmem()] * (len(pieces) + 4),
         out_specs=in_vmem(),
@@ -547,7 +520,9 @@
     )(*pieces, hidden, small, tiles, own, other)
 
 
-def encoder_kernel(states_hbm, gain_ref, fc1_hbm, fc2_hbm, out_ref, states_ref, fc1_ref, fc2_ref, product, sems):
+def encoder_kernel(states_hbm, gain_ref, fc1_hbm, fc2_hbm, norm_ref, qk_ref, gate_ref, *refs):
+    out_refs, small_ref = refs[:GROUP], refs[GROUP]
+    states_ref, fc1_ref, fc2_ref, product, sems = refs[GROUP + 1 :]
     copies = [
         pltpu.make_async_copy(source, target, sems.at[at])
         for at, (source, target) in enumerate(
@@ -559,11 +534,17 @@
     core = lax.axis_index("section")
     chip = lax.axis_index("tp")
     member = jnp.where(core == 0, chip % GROUP, chip // GROUP)
+    small_ref[0:1, :] = norm_ref[...].astype(jnp.float32)
+    small_ref[1:2, :] = jnp.concatenate(
+        [qk_ref[0:1, :], qk_ref[1:2, :], jnp.zeros((1, norm_ref.shape[1] - 2 * HD), jnp.float32)],
+        axis=1,
+    )
+    small_ref[2:3, :] = jnp.full((1, norm_ref.shape[1]), gate_ref[0], jnp.float32)
     copies[0].wait()
     states = states_ref[...].astype(jnp.float32)
     centred = states - jnp.mean(states, axis=-1, keepdims=True)
     spread = jnp.mean(centred * centred, axis=-1, keepdims=True)
-    normed = (centred * lax.rsqrt(spread + epsilon) * gain_ref[...]).astype(jnp.bfloat16)
+    normed = (centred * lax.rsqrt(spread + epsilon) * gain_ref[...][None]).astype(jnp.bfloat16)
     copies[1].wait()
     inner = dot_rows(normed, fc1_ref[...])
     inner = (0.5 * inner * (1.0 + lax.erf(inner * 2.0 ** (-0.5)))).astype(jnp.bfloat16)
@@ -571,19 +552,21 @@
     product[...] = jnp.dot(inner, fc2_ref[...], preferred_element_type=jnp.float32).astype(
         jnp.bfloat16
     )
-    rows = out_ref.shape[1]
+    rows = out_refs[0].shape[0]
     for k in range(GROUP):
-        out_ref[k] = product[pl.ds(pl.multiple_of((member ^ k) * rows, rows), rows), :]
-
-
-def encoder_part(states, gain, fc1, fc2):
+        out_refs[k][...] = product[pl.ds(pl.multiple_of((member ^ k) * rows, rows), rows), :]
+
+
+def encoder_part(states, gain, fc1, fc2, norm, qk, gate):
     rows, width = states.shape
     in_place = pl.BlockSpec(memory_space=pltpu.HBM)
     return pl.pallas_call(
         encoder_kernel,
-        out_shape=jax.ShapeDtypeStruct((GROUP, rows // GROUP, width), jnp.bfloat16),
-        in_specs=[in_place, in_vmem(), in_place, in_place],
-        out_specs=in_vmem(),
+        out_shape=[jax.ShapeDtypeStruct((rows // GROUP, width), jnp.bfloat16)] * GROUP
+        + [jax.ShapeDtypeStruct((3, norm.shape[1]), jnp.float32)],
+        in_specs=[in_place, in_vmem(), in_place, in_place, in_vmem(), in_vmem()]
+        + [pl.BlockSpec(memory_space=pltpu.SMEM)],
+        out_specs=[in_vmem()] * (GROUP + 1),
         scratch_shapes=[
             pltpu.VMEM(states.shape, jnp.bfloat16),
             pltpu.VMEM(fc1.shape, jnp.bfloat16),
@@ -592,10 +575,10 @@
             pltpu.SemaphoreType.DMA((3,)),
         ],
         compiler_params=params(5 * VMEM_LIMIT),
-    )(states, gain, fc1, fc2)
-
-
-def image_kernel(p0, p1, p2, p3, projector_ref, own_ref, other_ref, out_ref, rows_ref, kv_ref):
+    )(states, gain, fc1, fc2, norm, qk, gate)
+
+
+def image_kernel(p0, p1, p2, p3, projector_ref, own_ref, other_ref, _, out_ref, rows_ref, kv_ref):
     core = lax.axis_index("section")
     chip = lax.axis_index("tp")
     low, high = chip % GROUP, chip // GROUP
@@ -618,19 +601,19 @@
                 ].astype(jnp.bfloat16)
 
 
-def image_part(pieces, projector, own, other):
+def image_part(pieces, projector, own, other, begun):
     rows = GROUP * pieces[0].shape[0]
     return pl.pallas_call(
         image_kernel,
         out_shape=jax.ShapeDtypeStruct((2, GROUP, rows, 2 * HD), jnp.bfloat16),
-        in_specs=[in_vmem()] * 7,
+        in_specs=[in_vmem()] * 8,
         out_specs=in_vmem(),
         scratch_shapes=[
             pltpu.VMEM((rows, projector.shape[0]), jnp.bfloat16),
             pltpu.VMEM((rows, own.shape[1]), jnp.float32),
         ],
         compiler_params=params(),
-    )(*pieces, projector, own, other)
+    )(*pieces, projector, own, other, begun)
 
 
 def rope_tables(positions):
@@ -679,29 +662,22 @@
         [hidden, cross_norm, self_norm, jnp.zeros((14, local_width), jnp.bfloat16)]
     )
     text_come = send_group([entry] * GROUP, (GROUP, GROUP))
-    branch = encoder_part(vision_states, vision_norm_gain[None], vision_fc1.T, vision_fc2)
+    *branch, small = encoder_part(
+        vision_states, vision_norm_gain, vision_fc1.T, vision_fc2, self_norm, cross_qk_gain[0], cross_gate
+    )
     come = send_group(branch, (1, GROUP))
-    come, text_come, own, self_norm, cross_qk_gain, cross_gate = after(
-        (come, text_come, own_cross_kv, self_norm, cross_qk_gain, cross_gate)
-    )
+    come, text_come, own, small = after((come, text_come, own_cross_kv, small))
     near = total([branch[0]] + come).astype(jnp.bfloat16)
     come = send_group([near] * GROUP, (GROUP, 1))
     far_cross_kv = swap_cores(own)
-    small = jnp.concatenate(
-        [
-            self_norm.astype(jnp.float32),
-            jnp.pad(cross_qk_gain.reshape(1, -1), ((0, 0), (0, local_width - 2 * HD))),
-            jnp.broadcast_to(cross_gate[None], (1, local_width)),
-        ]
-    )
     far_small = swap_cores(small)
     text = jnp.stack([entry] + text_come)
-    come, far_cross_kv, far_small, text, own = after(
-        (come, far_cross_kv, far_small, text, own_cross_q)
+    come, far_small, text, own, begun = after(
+        (come, far_small, text, own_cross_q, far_cross_kv[:16, :HD])
     )
     branch_rows = total([near] + come)
     vis_rows = lax.dynamic_index_in_dim(
-        vision_states.reshape(branch.shape), member, 0, keepdims=False
+        vision_states.reshape((GROUP,) + branch[0].shape), member, 0, keepdims=False
     )
     vis_out = (vis_rows.astype(jnp.float32) + jnp.tanh(vision_gate[0]) * branch_rows).astype(
         jnp.bfloat16
@@ -712,7 +688,7 @@
     come, text_come, far_cross_q, own = after((come, text_come, far_cross_q, own_cross_o))
     scalars = [jnp.where(core == 0, small, far_small), jnp.where(core == 0, far_small, small)]
 
-    image_parts = image_part([vis_out] + come, projector, own_cross_kv, far_cross_kv)
+    image_parts = image_part([vis_out] + come, projector, own_cross_kv, far_cross_kv, begun)
     come = send_group(image_parts[0], (GROUP, GROUP))
     text = jnp.concatenate([text, text_come])
     text_come = send_xor(text, (2, 1))
@@ -725,7 +701,7 @@
     far_self_kv = swap_cores(own)
     gains = (gains, far_gains)
     text = [half[at : at + GROUP] for half in (text, text_come) for at in (0, GROUP)]
-    queries = plain_query_part(0, 0, rows, text, gains, (own_cross_q, far_cross_q))
+    queries = plain_query_part(0, 0, rows, text, gains, (own_cross_q, far_cross_q), text_mask)
     come, queries, far_self_kv = after((come, queries, far_self_kv))
     parts = [near] + come
 
@@ -747,54 +723,61 @@
         come = send_group([hidden] * GROUP, (GROUP, 1))
         kv_rows = steps[1](steps[0]())
         extra = steps[2](kv_rows)
+        come, kv_rows, extra = after((come, kv_rows, extra))
         if section == 0:
-            far_self_o = swap_cores(after((own_self_o, hidden))[0])
-            come, kv_rows, extra, far_self_o = after((come, kv_rows, extra, far_self_o))
-        else:
-            come, kv_rows, extra = after((come, kv_rows, extra))
+            far_self_o = swap_cores(own_self_o)
         first = jnp.stack([hidden] + come)
         come = send_group([first] * GROUP, (1, GROUP))
         kv_rows = steps[3](kv_rows, extra)
         kv_rows = steps[5](kv_rows, steps[4](kv_rows))
-        come, kv_rows, extra = after((come, kv_rows, steps[6](kv_rows)))
+        extra = steps[6](kv_rows)
+        if section == 0:
+            come, kv_rows, extra, far_self_o = after((come, kv_rows, extra, far_self_o))
+        else:
+            come, kv_rows, extra = after((come, kv_rows, extra))
         near = steps[7](kv_rows, extra).astype(jnp.bfloat16)
         far = swap_cores(near)
         queries = query_part(
             section, 1, rows, [first] + come, gains, (own_self_q, far_self_q), cosine, sine
         )
         mixed = self_mix(full_width, queries, near, far, cosine, sine)
-        pieces, extras = gather_chips(mixed, *beside_mixed)
+        pieces, extra = gather_chips(mixed, beside_mixed)
         hidden = out_part(
             section, False, pieces, hidden, scalars[section], tiles, own_self_o, far_self_o
         )
-        return hidden, extras
-
-    mixed = cross_mix_from(tile_rows, queries, near, far, tiles, scalars[0])
-    mixed, own, second_kept = after((mixed, own_self_q, image_parts[1]))
-    second = head_steps(second_kept)
-    pieces, ((far_self_q, come), second_come) = gather_chips(
-        mixed,
-        lambda: (swap_cores(own), second[0]()),
-        lambda extra: second[2](second[1](extra[1])),
-    )
-    second_rows = second[3](second[1](come), second_come)
+        return hidden, extra
+
+    mixed = cross_mix(tile_rows, queries, near, far, tiles, scalars[0])
+    mixed, own = after((mixed, own_self_q))
+    pieces, far_self_q = gather_chips(mixed, lambda: swap_cores(own))
     hidden = out_part(0, True, pieces, hidden, scalars[0], tiles, own_cross_o, far_cross_o)
     far_self_o = None
-    hidden, (come, second_come) = self_block(
-        0,
-        hidden,
-        (lambda: second[4](second_rows), lambda extra: second[6](second[5](second_rows, extra))),
-    )
-    second_rows = second[7](second[5](second_rows, come), second_come)
+    hidden, second_kept = after((hidden, image_parts[1]))
+    second = head_steps(second_kept)
+
+    def two_steps():
+        second_rows = second[1](second[0]())
+        return second_rows, second[2](second_rows)
+
+    hidden, (second_rows, come) = self_block(0, hidden, two_steps)
+    second_rows = second[3](second_rows, come)
     results = [hidden]
-    near, far = image_rows(second_rows, 1)
-    pieces, (far,) = gather_chips(hidden, lambda: far)
-    mixed = cross_mix(
-        1, 0, tile_rows, rows, pieces, gains, (own_cross_q, far_cross_q), near, far, tiles, scalars[1]
-    )
+
+    hidden, second_rows = after((hidden, second_rows))
+    come = second[4](second_rows)
+    steps = send_group([hidden] * GROUP, (GROUP, 1))
+    come, steps = after((come, steps))
+    second_rows = second[5](second_rows, come)
+    first = jnp.stack([hidden] + steps)
+    come = second[6](second_rows)
+    pieces = [first] + send_group([first] * GROUP, (1, GROUP))
+    come, pieces = after((come, pieces))
+    near, far = image_rows(second[7](second_rows, come), 1)
+    queries = plain_query_part(1, 0, rows, pieces, gains, (own_cross_q, far_cross_q))
+    mixed = cross_mix(tile_rows, queries, near, far, tiles, scalars[1])
     pieces, _ = gather_chips(mixed)
     hidden = out_part(1, True, pieces, hidden, scalars[1], tiles, own_cross_o, far_cross_o)
-    hidden, _ = self_block(1, hidden, ())
+    hidden, _ = self_block(1, hidden, None)
     results.append(hidden)
     come = swap_cores(jnp.where(core == 0, results[1], results[0]))
     return jnp.where(

time: 221 us -> 207 us (0.937)
  waiting for transfers between devices: 82.7 us -> 73.4 us
  starting transfers between devices: 98.8 us -> 102 us
  local copies, waits for them, and re-layouts: 7.75 us -> 4.67 us
  Pallas kernels: 22.2 us -> 19.4 us
    ppermute x74, waiting for transfers between devices: 79.1 us -> 70.4 us  [send_xor(): return lax.ppermute(block, ('section', 'tp'), route)]
    pallas_call x4 -> x5, Pallas kernels: 13.7 us -> 11 us  [the longest x2 6.27 us: plain_query_part(): pl.pallas_call(functools.partial(plain_query_kernel, section, gain_at, ma...]
  transfers between devices with their start and end apart: 87 -> 87, of which waited for: 40 -> 45; matrix products, arithmetic and copies ran while one was open for 3% -> 2% of each run, Pallas kernels for 6% -> 7%
where the time goes in v4:
time: 207 us
  starting transfers between devices  102 us (49%)
  waiting for transfers between devices  73.4 us (35%)
  Pallas kernels  19.4 us (9%)
  other arithmetic  5.08 us (2%)
  local copies, waits for them, and re-layouts  4.67 us (2%)
  between operations  2.08 us (1%)
    ppermute x74, starting transfers between devices, send_xor(): return lax.ppermute(block, ('section', 'tp'), route)  96.7 us
    ppermute x74, waiting for transfers between devices, send_xor(): return lax.ppermute(block, ('section', 'tp'), route)  70.4 us
    pallas_call x2, Pallas kernels, plain_query_part(): pl.pallas_call(functools.partial(plain_query_kernel, section, gain_at, ma...  6.27 us
    ppermute x13, starting transfers between devices, swap_cores(): return lax.ppermute(block, 'section', [(0, 1), (1, 0)])  5.33 us
    unnamed x29, local copies, waits for them, and re-layouts  4.33 us
  transfers between devices with their start and end apart: 87, of which 45 were waited for; matrix products, arithmetic and copies ran while one was open for 2% of the time, Pallas kernels for 7%

profile of v4, /device:TPU:0, one launch (start us, length us, event | category | flops | bytes accessed | tf_op | source)
XLA Modules:
  0.0 206.6 jit_solution(14954286961440274502)
XLA Ops:
  1.7 5.1 %collective-permute-start.5 = (bf16[80,512]{1,0:T(8,128)(2,1)S(1)}, bf16[80,512]{1,0:T(8,128)(2,1)S(1)}, u32[]{:S(2)}, u32[]{:S(2)}) collective-permute-start(bf16[80,512]{1,0:T(8,128)(2,1)S(1)} %maximum_maximum_fusion), channel_id=1, source_target_pairs={{0,12},{1,13},{2,14},{3,15},{4,8},{5,9},{6,10},{7,11},{8,4},{9,5},... | collective-permute-start | bytes 245768 | tf_op jit(solution)/shard_map/ppermute | solution.py:212
  8.1 3.6 %shard_map.190 = (bf16[32,1280]{1,0:T(8,128)(2,1)}, bf16[32,1280]{1,0:T(8,128)(2,1)}, bf16[32,1280]{1,0:T(8,128)(2,1)}, bf16[32,1280]{1,0:T(8,128)(2,1)}, f32[3,512]{1,0:T(4,128)}) custom-call(bf16[128,1280]{1,0:T(8,128)(2,1)} %states_hbm.1, f32[1280]{0:T(1024)} %gain_ref.1, bf16[320,1280]{1,0:T(8,128)(2,1)} %bitcast.107, bf16[320,1280]{1,0:T(8,128)(2,1)} %fc2_hbm.1, ...), custom_call_target="tpu_custom_call" | custom-call | tf_op jit(solution)/shard_map/pallas_call | solution.py:563
  18.1 2.4 %collective-permute-done.2 = bf16[32,1280]{1,0:T(8,128)(2,1)S(1)} collective-permute-done((bf16[32,1280]{1,0:T(8,128)(2,1)}, bf16[32,1280]{1,0:T(8,128)(2,1)S(1)}, u32[]{:S(2)}, u32[]{:S(2)}) %collective-permute-start.2) | collective-permute-done | bytes 81952 | tf_op jit(solution)/shard_map/ppermute | solution.py:212
  22.3 3.7 %collective-permute-start.8 = (bf16[32,1280]{1,0:T(8,128)(2,1)S(1)}, bf16[32,1280]{1,0:T(8,128)(2,1)S(1)}, u32[]{:S(2)}, u32[]{:S(2)}) collective-permute-start(bf16[32,1280]{1,0:T(8,128)(2,1)S(1)} %add_convert_fusion.3), channel_id=1, source_target_pairs={{0,12},{1,13},{2,14},{3,15},{4,8},{5,9},{6,10},{7,11},{8,4},{9,5},... | collective-permute-start | bytes 245768 | tf_op jit(solution)/shard_map/ppermute | solution.py:212
  28.6 2.7 %collective-permute-done.7 = bf16[32,1280]{1,0:T(8,128)(2,1)S(1)} collective-permute-done((bf16[32,1280]{1,0:T(8,128)(2,1)S(1)}, bf16[32,1280]{1,0:T(8,128)(2,1)S(1)}, u32[]{:S(2)}, u32[]{:S(2)}) %collective-permute-start.7) | collective-permute-done | bytes 81952 | tf_op jit(solution)/shard_map/ppermute | solution.py:212
  37.1 3.0 %collective-permute-done.13.p3 = bf16[32,1280]{1,0:T(8,128)(2,1)S(1)} collective-permute-done((bf16[32,1280]{1,0:T(8,128)(2,1)S(1)}, bf16[32,1280]{1,0:T(8,128)(2,1)S(1)}, u32[]{:S(2)}, u32[]{:S(2)}) %collective-permute-start.13) | collective-permute-done | bytes 81952 | tf_op jit(solution)/shard_map/ppermute | solution.py:212
  45.7 2.1 collective-permute-start.18
  48.0 2.1 %collective-permute-start.16 = (bf16[128,256]{1,0:T(8,128)(2,1)S(1)}, bf16[128,256]{1,0:T(8,128)(2,1)S(1)}, u32[]{:S(2)}, u32[]{:S(2)}) collective-permute-start(bf16[128,256]{1,0:T(8,128)(2,1)S(1)} %get-tuple-element.185), channel_id=1, source_target_pairs={{0,4},{1,5},{2,6},{3,7},{4,0},{5,1},{6,2},{7,3},{8,12},{9,13},{10,... | collective-permute-start | bytes 196616 | tf_op jit(solution)/shard_map/ppermute | solution.py:212
  50.1 1.9 collective-permute-done.18
  52.0 2.4 %collective-permute-done.17 = bf16[128,256]{1,0:T(8,128)(2,1)S(1)} collective-permute-done((bf16[128,256]{1,0:T(8,128)(2,1)S(1)}, bf16[128,256]{1,0:T(8,128)(2,1)S(1)}, u32[]{:S(2)}, u32[]{:S(2)}) %collective-permute-start.17) | collective-permute-done | bytes 65568 | tf_op jit(solution)/shard_map/ppermute | solution.py:212
  58.9 3.2 %shard_map.192.q_ref = f32[64,256]{1,0:T(8,128)S(1)} custom-call(bf16[4,80,512]{2,1,0:T(8,128)(2,1)S(1)} %pad_maximum_fusion.refs_0_, bf16[4,80,512]{2,1,0:T(8,128)(2,1)S(1)} %collective-permute-done.14.refs_1_, bf16[4,80,512]{2,1,0:T(8,128)(2,1)S(1)} %get-tuple-element.182.refs_2_, bf16[4,80,512]{2,1,0:T(8,128)(2,1)S(1)} %get-tuple-element.181.refs_3_, ...), custom_call_target="tpu_custom_call" | custom-call | tf_op jit(solution)/shard_map/pallas_call | solution.py:383
  65.0 2.5 %collective-permute-start.29 = (bf16[64,256]{1,0:T(8,128)(2,1)S(1)}, bf16[64,256]{1,0:T(8,128)(2,1)S(1)}, u32[]{:S(2)}, u32[]{:S(2)}) collective-permute-start(bf16[64,256]{1,0:T(8,128)(2,1)S(1)} %shard_map.193), channel_id=1, source_target_pairs={{0,12},{1,13},{2,14},{3,15},{4,8},{5,9},{6,10},{7,11},{8,4},{9,5},... | collective-permute-start | bytes 98312 | tf_op jit(solution)/shard_map/ppermute | solution.py:212
  67.5 1.9 collective-permute-start.27
  76.1 2.4 %collective-permute-done.32.refs_3_ = bf16[4,64,256]{2,1,0:T(8,128)(2,1)S(1)} collective-permute-done((bf16[4,64,256]{2,1,0:T(8,128)(2,1)S(1)}, bf16[4,64,256]{2,1,0:T(8,128)(2,1)S(1)}, u32[]{:S(2)}, u32[]{:S(2)}) %collective-permute-start.32) | collective-permute-done | bytes 131104 | tf_op jit(solution)/shard_map/ppermute | solution.py:212
  81.5 1.8 collective-permute-start.37
  85.1 2.6 %collective-permute-start.34 = (bf16[64,512]{1,0:T(8,128)(2,1)S(1)}, bf16[64,512]{1,0:T(8,128)(2,1)S(1)}, u32[]{:S(2)}, u32[]{:S(2)}) collective-permute-start(bf16[64,512]{1,0:T(8,128)(2,1)S(1)} %shard_map.194.hidden_ref.refs_4_), channel_id=1, source_target_pairs={{0,4},{1,5},{2,6},{3,7},{4,0},{5,1},{6,2},{7,3},{8,12},{9,13},{10,... | collective-permute-start | bytes 196616 | tf_op jit(solution)/shard_map/ppermute | solution.py:212
  98.7 4.8 %collective-permute-done.43 = bf16[80,256]{1,0:T(8,128)(2,1)S(1)} collective-permute-done((bf16[80,256]{1,0:T(8,128)(2,1)S(1)}, bf16[80,256]{1,0:T(8,128)(2,1)S(1)}, u32[]{:S(2)}, u32[]{:S(2)}) %collective-permute-start.43) | collective-permute-done | bytes 40992 | tf_op jit(solution)/shard_map/ppermute | solution.py:212
  103.5 3.8 %collective-permute-start.45 = (bf16[80,256]{1,0:T(8,128)(2,1)S(1)}, bf16[80,256]{1,0:T(8,128)(2,1)S(1)}, u32[]{:S(2)}, u32[]{:S(2)}) collective-permute-start(bf16[80,256]{1,0:T(8,128)(2,1)S(1)} %add_convert_fusion.7.near_ref), channel_id=1, source_target_pairs={{0,16},{16,0},{1,17},{17,1},{2,18},{18,2},{3,19},{19,3},{4,20},{20... | collective-permute-start | bytes 122888 | tf_op jit(solution)/shard_map/ppermute | solution.py:202
  110.3 2.9 %collective-permute-start.46 = (bf16[64,256]{1,0:T(8,128)(2,1)S(1)}, bf16[64,256]{1,0:T(8,128)(2,1)S(1)}, u32[]{:S(2)}, u32[]{:S(2)}) collective-permute-start(bf16[64,256]{1,0:T(8,128)(2,1)S(1)} %shard_map.197), channel_id=1, source_target_pairs={{0,4},{1,5},{2,6},{3,7},{4,0},{5,1},{6,2},{7,3},{8,12},{9,13},{10,... | collective-permute-start | bytes 98312 | tf_op jit(solution)/shard_map/ppermute | solution.py:212
  120.8 3.7 %collective-permute-done.53 = bf16[128,256]{1,0:T(8,128)(2,1)S(1)} collective-permute-done((bf16[128,256]{1,0:T(8,128)(2,1)S(1)}, bf16[128,256]{1,0:T(8,128)(2,1)S(1)}, u32[]{:S(2)}, u32[]{:S(2)}) %collective-permute-start.53) | collective-permute-done | bytes 65568 | tf_op jit(solution)/shard_map/ppermute | solution.py:212
  128.9 1.8 collective-permute-start.55
  132.4 1.8 collective-permute-done.56
  139.4 5.7 %collective-permute-done.58 = bf16[128,256]{1,0:T(8,128)(2,1)S(1)} collective-permute-done((bf16[128,256]{1,0:T(8,128)(2,1)S(1)}, bf16[128,256]{1,0:T(8,128)(2,1)S(1)}, u32[]{:S(2)}, u32[]{:S(2)}) %collective-permute-start.58) | collective-permute-done | bytes 65568 | tf_op jit(solution)/shard_map/ppermute | solution.py:212
  145.5 3.0 %shard_map.199.q_ref = f32[64,256]{1,0:T(8,128)S(1)} custom-call(bf16[4,64,512]{2,1,0:T(8,128)(2,1)S(1)} %pad_maximum_fusion.3.refs_0_, bf16[4,64,512]{2,1,0:T(8,128)(2,1)S(1)} %collective-permute-done.59.refs_1_, bf16[4,64,512]{2,1,0:T(8,128)(2,1)S(1)} %collective-permute-done.60.refs_2_, bf16[4,64,512]{2,1,0:T(8,128)(2,1)S(1)} %collective-permute-done.61.refs_3_, ...), custom_call_target="tpu_custom_call" | custom-call | tf_op jit(solution)/shard_map/pallas_call | solution.py:383
  149.1 1.9 collective-permute-start.65
  151.8 1.8 collective-permute-start.63
  159.6 2.5 %collective-permute-done.68.refs_3_ = bf16[4,64,256]{2,1,0:T(8,128)(2,1)S(1)} collective-permute-done((bf16[4,64,256]{2,1,0:T(8,128)(2,1)S(1)}, bf16[4,64,256]{2,1,0:T(8,128)(2,1)S(1)}, u32[]{:S(2)}, u32[]{:S(2)}) %collective-permute-start.68) | collective-permute-done | bytes 131104 | tf_op jit(solution)/shard_map/ppermute | solution.py:212
  166.7 2.5 %collective-permute-start.71 = (bf16[64,512]{1,0:T(8,128)(2,1)S(1)}, bf16[64,512]{1,0:T(8,128)(2,1)S(1)}, u32[]{:S(2)}, u32[]{:S(2)}) collective-permute-start(bf16[64,512]{1,0:T(8,128)(2,1)S(1)} %shard_map.201.hidden_ref.refs_4_), channel_id=1, source_target_pairs={{0,12},{1,13},{2,14},{3,15},{4,8},{5,9},{6,10},{7,11},{8,4},{9,5},... | collective-permute-start | bytes 196616 | tf_op jit(solution)/shard_map/ppermute | solution.py:212
  181.0 6.3 %collective-permute-done.78 = bf16[80,256]{1,0:T(8,128)(2,1)S(1)} collective-permute-done((bf16[80,256]{1,0:T(8,128)(2,1)S(1)}, bf16[80,256]{1,0:T(8,128)(2,1)S(1)}, u32[]{:S(2)}, u32[]{:S(2)}) %collective-permute-start.78) | collective-permute-done | bytes 40992 | tf_op jit(solution)/shard_map/ppermute | solution.py:212
  189.2 2.0 collective-permute-start.82
  191.4 2.3 %collective-permute-start.80 = (bf16[64,256]{1,0:T(8,128)(2,1)S(1)}, bf16[64,256]{1,0:T(8,128)(2,1)S(1)}, u32[]{:S(2)}, u32[]{:S(2)}) collective-permute-start(bf16[64,256]{1,0:T(8,128)(2,1)S(1)} %shard_map.204), channel_id=1, source_target_pairs={{0,4},{1,5},{2,6},{3,7},{4,0},{5,1},{6,2},{7,3},{8,12},{9,13},{10,... | collective-permute-start | bytes 98312 | tf_op jit(solution)/shard_map/ppermute | solution.py:212
  199.6 2.5 %collective-permute-done.85.refs_3_ = bf16[4,64,256]{2,1,0:T(8,128)(2,1)S(1)} collective-permute-done((bf16[4,64,256]{2,1,0:T(8,128)(2,1)S(1)}, bf16[4,64,256]{2,1,0:T(8,128)(2,1)S(1)}, u32[]{:S(2)}, u32[]{:S(2)}) %collective-permute-start.85) | collective-permute-done | bytes 131104 | tf_op jit(solution)/shard_map/ppermute | solution.py:212
  (246 shorter events, 111.7 us)
Async XLA Ops:
  1.7 13.3 %collective-permute-start.5 = (bf16[80,512]{1,0:T(8,128)(2,1)S(1)}, bf16[80,512]{1,0:T(8,128)(2,1)S(1)}, u32[]{:S(2)}, u32[]{:S(2)}) collective-permute-start(bf16[80,512]{1,0:T(8,128)(2,1)S(1)} %maximum_maximum_fusion), channel_id=1, source_target_pairs={{0,12},{1,13},{2,14},{3,15},{4,8},{5,9},{6,10},{7,11},{8,4},{9,5},... | collective-permute-start | bytes 245768 | tf_op jit(solution)/shard_map/ppermute | solution.py:212
  6.8 8.5 %collective-permute-start.4 = (bf16[80,512]{1,0:T(8,128)(2,1)S(1)}, bf16[80,512]{1,0:T(8,128)(2,1)S(1)}, u32[]{:S(2)}, u32[]{:S(2)}) collective-permute-start(bf16[80,512]{1,0:T(8,128)(2,1)S(1)} %maximum_maximum_fusion), channel_id=1, source_target_pairs={{0,8},{1,9},{2,10},{3,11},{4,12},{5,13},{6,14},{7,15},{8,0},{9,1},... | collective-permute-start | bytes 245768 | tf_op jit(solution)/shard_map/ppermute | solution.py:212
  6.8 8.5 %collective-permute-start.3 = (bf16[80,512]{1,0:T(8,128)(2,1)S(1)}, bf16[80,512]{1,0:T(8,128)(2,1)S(1)}, u32[]{:S(2)}, u32[]{:S(2)}) collective-permute-start(bf16[80,512]{1,0:T(8,128)(2,1)S(1)} %maximum_maximum_fusion), channel_id=1, source_target_pairs={{0,4},{1,5},{2,6},{3,7},{4,0},{5,1},{6,2},{7,3},{8,12},{9,13},{10,... | collective-permute-start | bytes 245768 | tf_op jit(solution)/shard_map/ppermute | solution.py:212
  22.3 6.3 %collective-permute-start.8 = (bf16[32,1280]{1,0:T(8,128)(2,1)S(1)}, bf16[32,1280]{1,0:T(8,128)(2,1)S(1)}, u32[]{:S(2)}, u32[]{:S(2)}) collective-permute-start(bf16[32,1280]{1,0:T(8,128)(2,1)S(1)} %add_convert_fusion.3), channel_id=1, source_target_pairs={{0,12},{1,13},{2,14},{3,15},{4,8},{5,9},{6,10},{7,11},{8,4},{9,5},... | collective-permute-start | bytes 245768 | tf_op jit(solution)/shard_map/ppermute | solution.py:212
  31.3 9.7 %collective-permute-start.15 = (bf16[8192,256]{1,0:T(8,128)(2,1)}, bf16[8192,256]{1,0:T(8,128)(2,1)}, u32[]{:S(2)}, u32[]{:S(2)}) collective-permute-start(bf16[8192,256]{1,0:T(8,128)(2,1)} %bitcast.81), channel_id=1, source_target_pairs={{0,16},{16,0},{1,17},{17,1},{2,18},{18,2},{3,19},{19,3},{4,20},{20... | collective-permute-start | bytes 12582920 | tf_op jit(solution)/shard_map/ppermute | solution.py:202
  32.0 9.0 %collective-permute-start.14 = (bf16[4,80,512]{2,1,0:T(8,128)(2,1)S(1)}, bf16[4,80,512]{2,1,0:T(8,128)(2,1)S(1)}, u32[]{:S(2)}, u32[]{:S(2)}) collective-permute-start(bf16[4,80,512]{2,1,0:T(8,128)(2,1)S(1)} %pad_maximum_fusion.refs_0_), channel_id=1, source_target_pairs={{0,1},{1,0},{2,3},{3,2},{4,5},{5,4},{6,7},{7,6},{8,9},{9,8},{10,11... | collective-permute-start | bytes 983048 | tf_op jit(solution)/shard_map/ppermute | solution.py:212
  33.5 6.5 %collective-permute-start.13 = (bf16[32,1280]{1,0:T(8,128)(2,1)S(1)}, bf16[32,1280]{1,0:T(8,128)(2,1)S(1)}, u32[]{:S(2)}, u32[]{:S(2)}) collective-permute-start(bf16[32,1280]{1,0:T(8,128)(2,1)S(1)} %fusion.p0), channel_id=1, source_target_pairs={{0,3},{1,2},{2,1},{3,0},{4,7},{5,6},{6,5},{7,4},{8,11},{9,10},{10,... | collective-permute-start | bytes 245768 | tf_op jit(solution)/shard_map/ppermute | solution.py:212
  41.0 13.4 %collective-permute-start.20 = (bf16[4096,512]{1,0:T(8,128)(2,1)}, bf16[4096,512]{1,0:T(8,128)(2,1)S(1)}, u32[]{:S(2)}, u32[]{:S(2)}) collective-permute-start(bf16[4096,512]{1,0:T(8,128)(2,1)} %bitcast.87), channel_id=1, source_target_pairs={{0,16},{16,0},{1,17},{17,1},{2,18},{18,2},{3,19},{19,3},{4,20},{20... | collective-permute-start | bytes 12582920 | tf_op jit(solution)/shard_map/ppermute | solution.py:202
  41.1 13.3 %collective-permute-start.19 = (bf16[8,80,512]{2,1,0:T(8,128)(2,1)S(1)}, bf16[8,80,512]{2,1,0:T(8,128)(2,1)S(1)}, u32[]{:S(2)}, u32[]{:S(2)}) collective-permute-start(bf16[8,80,512]{2,1,0:T(8,128)(2,1)S(1)} %constant_dynamic-update-slice_fusion), channel_id=1, source_target_pairs={{0,2},{1,3},{2,0},{3,1},{4,6},{5,7},{6,4},{7,5},{8,10},{9,11},{10,... | collective-permute-start | bytes 1966088 | tf_op jit(solution)/shard_map/ppermute | solution.py:212
  45.7 6.3 %collective-permute-start.18 = (bf16[128,256]{1,0:T(8,128)(2,1)S(1)}, bf16[128,256]{1,0:T(8,128)(2,1)S(1)}, u32[]{:S(2)}, u32[]{:S(2)}) collective-permute-start(bf16[128,256]{1,0:T(8,128)(2,1)S(1)} %get-tuple-element.183), channel_id=1, source_target_pairs={{0,12},{1,13},{2,14},{3,15},{4,8},{5,9},{6,10},{7,11},{8,4},{9,5},... | collective-permute-start | bytes 196616 | tf_op jit(solution)/shard_map/ppermute | solution.py:212
  47.7 6.7 %collective-permute-start.17 = (bf16[128,256]{1,0:T(8,128)(2,1)S(1)}, bf16[128,256]{1,0:T(8,128)(2,1)S(1)}, u32[]{:S(2)}, u32[]{:S(2)}) collective-permute-start(bf16[128,256]{1,0:T(8,128)(2,1)S(1)} %get-tuple-element.184), channel_id=1, source_target_pairs={{0,8},{1,9},{2,10},{3,11},{4,12},{5,13},{6,14},{7,15},{8,0},{9,1},... | collective-permute-start | bytes 196616 | tf_op jit(solution)/shard_map/ppermute | solution.py:212
  48.0 6.5 %collective-permute-start.16 = (bf16[128,256]{1,0:T(8,128)(2,1)S(1)}, bf16[128,256]{1,0:T(8,128)(2,1)S(1)}, u32[]{:S(2)}, u32[]{:S(2)}) collective-permute-start(bf16[128,256]{1,0:T(8,128)(2,1)S(1)} %get-tuple-element.185), channel_id=1, source_target_pairs={{0,4},{1,5},{2,6},{3,7},{4,0},{5,1},{6,2},{7,3},{8,12},{9,13},{10,... | collective-permute-start | bytes 196616 | tf_op jit(solution)/shard_map/ppermute | solution.py:212
  54.4 7.7 %collective-permute-start.25 = (bf16[512,1024]{1,0:T(8,128)(2,1)S(1)}, bf16[512,1024]{1,0:T(8,128)(2,1)S(1)}, u32[]{:S(2)}, u32[]{:S(2)}) collective-permute-start(bf16[512,1024]{1,0:T(8,128)(2,1)S(1)} %bitcast.93), channel_id=1, source_target_pairs={{0,16},{16,0},{1,17},{17,1},{2,18},{18,2},{3,19},{19,3},{4,20},{20... | collective-permute-start | bytes 3145736 | tf_op jit(solution)/shard_map/ppermute | solution.py:202
  55.2 6.9 %collective-permute-start.23 = (bf16[128,256]{1,0:T(8,128)(2,1)S(1)}, bf16[128,256]{1,0:T(8,128)(2,1)S(1)}, u32[]{:S(2)}, u32[]{:S(2)}) collective-permute-start(bf16[128,256]{1,0:T(8,128)(2,1)S(1)} %fusion.4), channel_id=1, source_target_pairs={{0,3},{1,2},{2,1},{3,0},{4,7},{5,6},{6,5},{7,4},{8,11},{9,10},{10,... | collective-permute-start | bytes 196616 | tf_op jit(solution)/shard_map/ppermute | solution.py:212
  64.4 15.7 %collective-permute-start.33 = (bf16[8192,256]{1,0:T(8,128)(2,1)S(1)}, bf16[8192,256]{1,0:T(8,128)(2,1)S(1)}, u32[]{:S(2)}, u32[]{:S(2)}) collective-permute-start(bf16[8192,256]{1,0:T(8,128)(2,1)S(1)} %bitcast.84), channel_id=1, source_target_pairs={{0,16},{16,0},{1,17},{17,1},{2,18},{18,2},{3,19},{19,3},{4,20},{20... | collective-permute-start | bytes 12582920 | tf_op jit(solution)/shard_map/ppermute | solution.py:202
  64.6 33.1 %collective-permute-start.44 = (bf16[4096,512]{1,0:T(8,128)(2,1)S(1)}, bf16[4096,512]{1,0:T(8,128)(2,1)S(1)}, u32[]{:S(2)}, u32[]{:S(2)}) collective-permute-start(bf16[4096,512]{1,0:T(8,128)(2,1)S(1)} %bitcast.90), channel_id=1, source_target_pairs={{0,16},{16,0},{1,17},{17,1},{2,18},{18,2},{3,19},{19,3},{4,20},{20... | collective-permute-start | bytes 12582920 | tf_op jit(solution)/shard_map/ppermute | solution.py:202
  92.9 10.6 %collective-permute-start.41 = (bf16[4,64,512]{2,1,0:T(8,128)(2,1)S(1)}, bf16[4,64,512]{2,1,0:T(8,128)(2,1)S(1)}, u32[]{:S(2)}, u32[]{:S(2)}) collective-permute-start(bf16[4,64,512]{2,1,0:T(8,128)(2,1)S(1)} %pad_maximum_fusion.2.refs_0_), channel_id=1, source_target_pairs={{0,3},{1,2},{2,1},{3,0},{4,7},{5,6},{6,5},{7,4},{8,11},{9,10},{10,... | collective-permute-start | bytes 786440 | tf_op jit(solution)/shard_map/ppermute | solution.py:212
  94.5 9.0 %collective-permute-start.40 = (bf16[4,64,512]{2,1,0:T(8,128)(2,1)S(1)}, bf16[4,64,512]{2,1,0:T(8,128)(2,1)S(1)}, u32[]{:S(2)}, u32[]{:S(2)}) collective-permute-start(bf16[4,64,512]{2,1,0:T(8,128)(2,1)S(1)} %pad_maximum_fusion.2.refs_0_), channel_id=1, source_target_pairs={{0,2},{1,3},{2,0},{3,1},{4,6},{5,7},{6,4},{7,5},{8,10},{9,11},{10,... | collective-permute-start | bytes 786440 | tf_op jit(solution)/shard_map/ppermute | solution.py:212
  95.5 8.0 %collective-permute-start.39 = (bf16[4,64,512]{2,1,0:T(8,128)(2,1)S(1)}, bf16[4,64,512]{2,1,0:T(8,128)(2,1)S(1)}, u32[]{:S(2)}, u32[]{:S(2)}) collective-permute-start(bf16[4,64,512]{2,1,0:T(8,128)(2,1)S(1)} %pad_maximum_fusion.2.refs_0_), channel_id=1, source_target_pairs={{0,1},{1,0},{2,3},{3,2},{4,5},{5,4},{6,7},{7,6},{8,9},{9,8},{10,11... | collective-permute-start | bytes 786440 | tf_op jit(solution)/shard_map/ppermute | solution.py:212
  96.5 7.0 %collective-permute-start.43 = (bf16[80,256]{1,0:T(8,128)(2,1)S(1)}, bf16[80,256]{1,0:T(8,128)(2,1)S(1)}, u32[]{:S(2)}, u32[]{:S(2)}) collective-permute-start(bf16[80,256]{1,0:T(8,128)(2,1)S(1)} %add_convert_fusion.8), channel_id=1, source_target_pairs={{0,2},{1,3},{2,0},{3,1},{4,6},{5,7},{6,4},{7,5},{8,10},{9,11},{10,... | collective-permute-start | bytes 122888 | tf_op jit(solution)/shard_map/ppermute | solution.py:212
  97.8 15.5 %collective-permute-start.52 = (bf16[2,128,256]{2,1,0:T(8,128)(2,1)S(1)}, bf16[2,128,256]{2,1,0:T(8,128)(2,1)S(1)}, u32[]{:S(2)}, u32[]{:S(2)}) collective-permute-start(bf16[2,128,256]{2,1,0:T(8,128)(2,1)S(1)} %slice.111), channel_id=1, source_target_pairs={{0,8},{1,9},{2,10},{3,11},{4,12},{5,13},{6,14},{7,15},{8,0},{9,1},... | collective-permute-start | bytes 393224 | tf_op jit(solution)/shard_map/ppermute | solution.py:212
  115.7 8.8 %collective-permute-start.51 = (bf16[4,64,256]{2,1,0:T(8,128)(2,1)S(1)}, bf16[4,64,256]{2,1,0:T(8,128)(2,1)S(1)}, u32[]{:S(2)}, u32[]{:S(2)}) collective-permute-start(bf16[4,64,256]{2,1,0:T(8,128)(2,1)S(1)} %pad_maximum_fusion.6.refs_0_), channel_id=1, source_target_pairs={{0,3},{1,2},{2,1},{3,0},{4,7},{5,6},{6,5},{7,4},{8,11},{9,10},{10,... | collective-permute-start | bytes 393224 | tf_op jit(solution)/shard_map/ppermute | solution.py:212
  117.2 7.3 %collective-permute-start.50 = (bf16[4,64,256]{2,1,0:T(8,128)(2,1)S(1)}, bf16[4,64,256]{2,1,0:T(8,128)(2,1)S(1)}, u32[]{:S(2)}, u32[]{:S(2)}) collective-permute-start(bf16[4,64,256]{2,1,0:T(8,128)(2,1)S(1)} %pad_maximum_fusion.6.refs_0_), channel_id=1, source_target_pairs={{0,2},{1,3},{2,0},{3,1},{4,6},{5,7},{6,4},{7,5},{8,10},{9,11},{10,... | collective-permute-start | bytes 393224 | tf_op jit(solution)/shard_map/ppermute | solution.py:212
  134.3 10.9 %collective-permute-start.61 = (bf16[4,64,512]{2,1,0:T(8,128)(2,1)S(1)}, bf16[4,64,512]{2,1,0:T(8,128)(2,1)S(1)}, u32[]{:S(2)}, u32[]{:S(2)}) collective-permute-start(bf16[4,64,512]{2,1,0:T(8,128)(2,1)S(1)} %pad_maximum_fusion.3.refs_0_), channel_id=1, source_target_pairs={{0,3},{1,2},{2,1},{3,0},{4,7},{5,6},{6,5},{7,4},{8,11},{9,10},{10,... | collective-permute-start | bytes 786440 | tf_op jit(solution)/shard_map/ppermute | solution.py:212
  135.6 9.5 %collective-permute-start.60 = (bf16[4,64,512]{2,1,0:T(8,128)(2,1)S(1)}, bf16[4,64,512]{2,1,0:T(8,128)(2,1)S(1)}, u32[]{:S(2)}, u32[]{:S(2)}) collective-permute-start(bf16[4,64,512]{2,1,0:T(8,128)(2,1)S(1)} %pad_maximum_fusion.3.refs_0_), channel_id=1, source_target_pairs={{0,2},{1,3},{2,0},{3,1},{4,6},{5,7},{6,4},{7,5},{8,10},{9,11},{10,... | collective-permute-start | bytes 786440 | tf_op jit(solution)/shard_map/ppermute | solution.py:212
  137.3 7.9 %collective-permute-start.59 = (bf16[4,64,512]{2,1,0:T(8,128)(2,1)S(1)}, bf16[4,64,512]{2,1,0:T(8,128)(2,1)S(1)}, u32[]{:S(2)}, u32[]{:S(2)}) collective-permute-start(bf16[4,64,512]{2,1,0:T(8,128)(2,1)S(1)} %pad_maximum_fusion.3.refs_0_), channel_id=1, source_target_pairs={{0,1},{1,0},{2,3},{3,2},{4,5},{5,4},{6,7},{7,6},{8,9},{9,8},{10,11... | collective-permute-start | bytes 786440 | tf_op jit(solution)/shard_map/ppermute | solution.py:212
  137.9 7.3 %collective-permute-start.58 = (bf16[128,256]{1,0:T(8,128)(2,1)S(1)}, bf16[128,256]{1,0:T(8,128)(2,1)S(1)}, u32[]{:S(2)}, u32[]{:S(2)}) collective-permute-start(bf16[128,256]{1,0:T(8,128)(2,1)S(1)} %add_convert_fusion.4), channel_id=1, source_target_pairs={{0,2},{1,3},{2,0},{3,1},{4,6},{5,7},{6,4},{7,5},{8,10},{9,11},{10,... | collective-permute-start | bytes 196616 | tf_op jit(solution)/shard_map/ppermute | solution.py:212
  166.7 6.5 %collective-permute-start.71 = (bf16[64,512]{1,0:T(8,128)(2,1)S(1)}, bf16[64,512]{1,0:T(8,128)(2,1)S(1)}, u32[]{:S(2)}, u32[]{:S(2)}) collective-permute-start(bf16[64,512]{1,0:T(8,128)(2,1)S(1)} %shard_map.201.hidden_ref.refs_4_), channel_id=1, source_target_pairs={{0,12},{1,13},{2,14},{3,15},{4,8},{5,9},{6,10},{7,11},{8,4},{9,5},... | collective-permute-start | bytes 196616 | tf_op jit(solution)/shard_map/ppermute | solution.py:212
  176.4 10.9 %collective-permute-start.76 = (bf16[4,64,512]{2,1,0:T(8,128)(2,1)S(1)}, bf16[4,64,512]{2,1,0:T(8,128)(2,1)S(1)}, u32[]{:S(2)}, u32[]{:S(2)}) collective-permute-start(bf16[4,64,512]{2,1,0:T(8,128)(2,1)S(1)} %pad_maximum_fusion.4.refs_0_), channel_id=1, source_target_pairs={{0,3},{1,2},{2,1},{3,0},{4,7},{5,6},{6,5},{7,4},{8,11},{9,10},{10,... | collective-permute-start | bytes 786440 | tf_op jit(solution)/shard_map/ppermute | solution.py:212
  177.8 9.5 %collective-permute-start.75 = (bf16[4,64,512]{2,1,0:T(8,128)(2,1)S(1)}, bf16[4,64,512]{2,1,0:T(8,128)(2,1)S(1)}, u32[]{:S(2)}, u32[]{:S(2)}) collective-permute-start(bf16[4,64,512]{2,1,0:T(8,128)(2,1)S(1)} %pad_maximum_fusion.4.refs_0_), channel_id=1, source_target_pairs={{0,2},{1,3},{2,0},{3,1},{4,6},{5,7},{6,4},{7,5},{8,10},{9,11},{10,... | collective-permute-start | bytes 786440 | tf_op jit(solution)/shard_map/ppermute | solution.py:212
  178.9 8.4 %collective-permute-start.74 = (bf16[4,64,512]{2,1,0:T(8,128)(2,1)S(1)}, bf16[4,64,512]{2,1,0:T(8,128)(2,1)S(1)}, u32[]{:S(2)}, u32[]{:S(2)}) collective-permute-start(bf16[4,64,512]{2,1,0:T(8,128)(2,1)S(1)} %pad_maximum_fusion.4.refs_0_), channel_id=1, source_target_pairs={{0,1},{1,0},{2,3},{3,2},{4,5},{5,4},{6,7},{7,6},{8,9},{9,8},{10,11... | collective-permute-start | bytes 786440 | tf_op jit(solution)/shard_map/ppermute | solution.py:212
  180.0 7.3 %collective-permute-start.78 = (bf16[80,256]{1,0:T(8,128)(2,1)S(1)}, bf16[80,256]{1,0:T(8,128)(2,1)S(1)}, u32[]{:S(2)}, u32[]{:S(2)}) collective-permute-start(bf16[80,256]{1,0:T(8,128)(2,1)S(1)} %add_convert_fusion.6), channel_id=1, source_target_pairs={{0,2},{1,3},{2,0},{3,1},{4,6},{5,7},{6,4},{7,5},{8,10},{9,11},{10,... | collective-permute-start | bytes 122888 | tf_op jit(solution)/shard_map/ppermute | solution.py:212
  (69 other events, 524.4 us)
